TPU v7x, 256 devices: a whole 4x4x8 slice. The times are simulated.
256 devices in a mesh: blk: 32 (over z_hi, y, core), op: 8 (over x, z_lo).
Axes of the slice: x: 4, y: 4, z: 8 (z_hi: 4, z_lo: 2; z = z_hi * 2 + z_lo), core: 2. Of those that a mesh axis runs over, the one named last changes fastest.
Arguments:
- initial_state: float32 [8, 6, 96, 32, 128], P('op', None, 'blk'), may hold values from -6 to 6
- target: float32 [8, 6, 96, 32, 128], P('op', None, 'blk'), may hold values from -6 to 6
- features: bfloat16 [8, 16, 96, 32, 128], P('op', None, 'blk'), may hold values from -6 to 6
- coupling: float32 [6, 6], replicated, may hold values from -1 to 1
- in_weight: bfloat16 [16, 256], replicated, may hold values from -1.5 to 1.5
- mid_weight: bfloat16 [256, 256], replicated, may hold values from -0.375 to 0.375
- top_weight: bfloat16 [256, 256], replicated, may hold values from -0.375 to 0.375
- out_weight: bfloat16 [256], replicated, may hold values from -0.375 to 0.375
- biases: float32 [3, 256], replicated, may hold values from -3 to 3
- block_count: int32 [32], P('blk'), may hold values from 1 to 3, as said below
- connectivity: int32 [96, 2], P('blk'), may hold values from 0 to 191, as said below
- orientation: int32 [96, 2], P('blk'), may hold values from 0 to 1
- rotation: int32 [96, 2], P('blk'), may hold values from -1 to 1
Outputs:
- state_final: float32 [8, 6, 96, 32, 128], P('op', None, 'blk')
- grad_in: float32 [16, 256], replicated
- grad_mid: float32 [256, 256], replicated
- grad_top: float32 [256, 256], replicated
- grad_vectors: float32 [4, 256], replicated
Inputs may be any that keep to these rules, and one draw needn't show every extreme that they name: `block_count`: every device has at least one live slot, and some device has all 3 live in every draw. `connectivity`: the ghost rows of a live slot name panels of live slots; those of a slot that is not live name panel 0.
All inputs are finite; a program needn't handle non-finite values.
Results may differ from a plain program's by a relative error of at most 0.00066.
Values sent between devices are 32-bit elements; how exact they have to be, the bound alone decides.
A program may use at most 128 MiB of HBM per device.

v0:
```python
import math

import jax
import jax.numpy as jnp
from jax import lax
from jax.sharding import PartitionSpec as P

tau_step = 0.2
passage_angle = 2.0 * math.pi / 36.0
highest = lax.Precision.HIGHEST


def orient_rotate(rows_in, flipped, cosines, sines):
    turned = jnp.where(flipped[None, :, None] == 1, rows_in[:, :, ::-1], rows_in)
    second = turned[2]
    third = turned[3]
    new_second = cosines[:, None] * second - sines[:, None] * third
    new_third = sines[:, None] * second + cosines[:, None] * third
    return jnp.concatenate([turned[:2], new_second[None], new_third[None], turned[4:]], axis=0)


def sweep_once(state, low, high, beta, coupling):
    extended = jnp.concatenate([low[:, :, None], state, high[:, :, None]], axis=2)
    row_term = extended[:, :, :-2] + extended[:, :, 2:] - 2.0 * state
    left = jnp.concatenate([state[..., :1], state[..., :-1]], axis=-1)
    right = jnp.concatenate([state[..., 1:], state[..., -1:]], axis=-1)
    laplace = row_term + left + right - 2.0 * state
    coupled = jnp.einsum("vw,wsij->vsij", coupling, state, precision=highest)
    return state + tau_step * (laplace - coupled + beta[None] * jnp.tanh(state))


def contract_lead(left_mat, right_mat):
    return lax.dot_general(
        left_mat, right_mat, (((0,), (0,)), ((), ())), preferred_element_type=jnp.float32
    )


def contract_cells(left_mat, right_mat):
    return lax.dot_general(
        left_mat, right_mat, (((1,), (1,)), ((), ())), preferred_element_type=jnp.float32
    )


def per_device(
    initial_state,
    target,
    features,
    coupling,
    in_weight,
    mid_weight,
    top_weight,
    out_weight,
    biases,
    block_count,
    connectivity,
    orientation,
    rotation,
):
    start = initial_state[0]
    nvars, slots_here, rows, cols = start.shape
    owners = lax.axis_size("blk")
    total_cells = lax.axis_size("op") * initial_state.shape[0] * slots_here * owners * rows * cols
    loss_scale = 2.0 / math.sqrt(total_cells)
    live = (jnp.arange(slots_here) < block_count[0]).astype(jnp.float32)
    sources = connectivity.reshape(-1)
    flipped = orientation.reshape(-1)
    angles = rotation.reshape(-1).astype(jnp.float32) * passage_angle
    cosines = jnp.cos(angles)
    sines = jnp.sin(angles)

    def fetch_ghosts(state):
        panels = jnp.stack([state[:, :, 0, :], state[:, :, -1, :]], axis=2).reshape(
            nvars, 2 * slots_here, cols
        )
        every_panel = lax.all_gather(panels, "blk", axis=1, tiled=True)
        picked = jnp.take(every_panel, sources, axis=1)
        ghost = orient_rotate(picked, flipped, cosines, sines)
        return (ghost[:, 0::2], ghost[:, 1::2])

    inputs = features[0].reshape(features.shape[1], -1)
    first = jnp.tanh(contract_lead(in_weight, inputs) + biases[0][:, None]).astype(jnp.bfloat16)
    second = jnp.tanh(contract_lead(mid_weight, first) + biases[1][:, None]).astype(jnp.bfloat16)
    third = jnp.tanh(contract_lead(top_weight, second) + biases[2][:, None]).astype(jnp.bfloat16)
    beta_flat = 1.0 + jnp.dot(out_weight[None, :], third, preferred_element_type=jnp.float32)[0]
    beta = beta_flat.reshape(slots_here, rows, cols)
    low_start, high_start = fetch_ghosts(start)
    middle = sweep_once(start, low_start, high_start, beta, coupling)
    low_middle, high_middle = fetch_ghosts(middle)

    def last_sweep(state, low, high):
        return sweep_once(state, low, high, beta, coupling)

    final, pull = jax.vjp(last_sweep, middle, low_middle, high_middle)
    final_cot = loss_scale * live[None, :, None, None] * (final - target[0])
    middle_cot, low_cot, high_cot = pull(final_cot)
    ghost_cot = jnp.stack([low_cot, high_cot], axis=2).reshape(nvars, 2 * slots_here, cols)
    panel_cot = orient_rotate(ghost_cot, flipped, cosines, -sines)
    onehot = (jnp.arange(2 * slots_here * owners)[:, None] == sources[None, :]).astype(jnp.float32)
    table = jnp.einsum("pg,vgj->vpj", onehot, panel_cot, precision=highest)
    returned = lax.psum_scatter(table, "blk", scatter_dimension=1, tiled=True).reshape(
        nvars, slots_here, 2, cols
    )
    middle_cot = middle_cot.at[:, :, 0].add(returned[:, :, 0]).at[:, :, -1].add(returned[:, :, 1])
    beta_cot = tau_step * (
        jnp.sum(final_cot * jnp.tanh(middle), axis=0)
        + jnp.sum(middle_cot * jnp.tanh(start), axis=0)
    )
    beta_cot = beta_cot.reshape(-1)
    cot_half = beta_cot.astype(jnp.bfloat16)
    grad_out = jnp.dot(third, cot_half, preferred_element_type=jnp.float32)
    third_wide = third.astype(jnp.float32)
    delta_top = (
        out_weight.astype(jnp.float32)[:, None]
        * beta_cot[None, :]
        * (1.0 - third_wide * third_wide)
    ).astype(jnp.bfloat16)
    grad_top = contract_cells(second, delta_top)
    bias_top = jnp.sum(delta_top.astype(jnp.float32), axis=1)
    second_wide = second.astype(jnp.float32)
    delta_mid = (
        jnp.dot(top_weight, delta_top, preferred_element_type=jnp.float32)
        * (1.0 - second_wide * second_wide)
    ).astype(jnp.bfloat16)
    grad_mid = contract_cells(first, delta_mid)
    bias_mid = jnp.sum(delta_mid.astype(jnp.float32), axis=1)
    first_wide = first.astype(jnp.float32)
    delta_first = (
        jnp.dot(mid_weight, delta_mid, preferred_element_type=jnp.float32)
        * (1.0 - first_wide * first_wide)
    ).astype(jnp.bfloat16)
    grad_in = contract_cells(inputs, delta_first)
    bias_first = jnp.sum(delta_first.astype(jnp.float32), axis=1)
    vectors = jnp.stack([grad_out, bias_first, bias_mid, bias_top])
    grad_in, grad_mid, grad_top, vectors = lax.psum(
        (grad_in, grad_mid, grad_top, vectors), ("blk", "op")
    )
    state_final = (live[None, :, None, None] * final)[None]
    return (state_final, grad_in, grad_mid, grad_top, vectors)


def solution(mesh):
    placed = (
        P("op", None, "blk", None, None),
        P("op", None, "blk", None, None),
        P("op", None, "blk", None, None),
        P(),
        P(),
        P(),
        P(),
        P(),
        P(),
        P("blk"),
        P("blk", None),
        P("blk", None),
        P("blk", None),
    )
    return jax.shard_map(
        per_device,
        mesh=mesh,
        in_specs=placed,
        out_specs=(P("op", None, "blk", None, None), P(), P(), P(), P()),
        check_vma=False,
    )
```

profile of v0, /device:TPU:1, one launch (start us, length us, event | category | flops | bytes accessed | tf_op | source)
XLA Modules:
  0.0 699.4 jit_solution(13023234716193653685)
XLA Ops:
  7.2 0.8 copy.50
  8.0 0.1 reshape.258
  8.1 1.2 copy.82
  9.3 0.2 fusion.55
  9.5 0.2 fusion.56
  9.7 0.7 broadcast_compare_fusion
  10.4 0.1 copy.49
  10.5 0.1 eq.27
  10.6 0.7 reshape.285
  11.2 0.7 fusion.49
  12.0 0.1 copy.51
  12.1 0.1 cos.11
  12.1 0.1 copy.52
  12.2 0.1 sin.14
  12.3 0.8 fusion.61
  13.1 1.2 reshape_squeeze.3
  14.3 54.5 %all_gather.6 = f32[6,192,128]{2,0,1:T(8,128)} all-gather(f32[6,6,128]{2,0,1:T(8,128)S(1)} %bitcast.152), channel_id=1, replica_groups=mesh['blk'=32,'op'=8] {'blk'}, dimensions={1}, use_global_device_ids=true | all-gather | bytes 608256 | tf_op jit(solution)/shard_map/all_gather | solution.py:75
  68.8 1.7 gather_fusion
  70.5 0.1 select_bitcast_fusion.1
  70.6 0.1 rev.9
  70.7 0.1 broadcast_select_fusion.2
  70.8 0.1 multiply_subtract_fusion.2
  70.9 2.5 fusion.1
  73.4 2.5 fusion.8
  76.0 1.9 fusion.9
  78.0 0.6 copy-done.11
  78.6 2.7 copy-done.1
  81.2 0.9 fusion.62
  82.2 0.7 fusion.14
  83.0 41.9 %all_gather.7 = f32[6,192,128]{2,0,1:T(8,128)S(1)} all-gather(f32[6,6,128]{2,0,1:T(8,128)S(1)} %bitcast.153), channel_id=1, replica_groups=mesh['blk'=32,'op'=8] {'blk'}, dimensions={1}, use_global_device_ids=true | all-gather | bytes 608256 | tf_op jit(solution)/shard_map/all_gather | solution.py:75
  124.9 0.6 gather_fusion.1
  125.5 0.1 select_bitcast_fusion
  125.6 0.1 rev.10
  125.6 0.1 broadcast_select_fusion.1
  125.7 0.1 multiply_subtract_fusion.1
  125.8 0.2 fusion.52
  126.0 0.2 fusion.53
  126.9 0.7 fusion.17
  127.6 0.4 broadcast_multiply_fusion
  128.0 0.1 rev.11
  128.1 0.1 broadcast_select_fusion
  128.2 0.1 multiply_subtract_fusion
  128.3 1.3 convolution_bitcast_fusion.1
  129.7 0.2 all-reduce.13.cloned.1.call-start
  129.9 0.2 split.25
  130.1 0.8 copy.62
  130.9 0.6 dynamic-slice.14
  132.1 0.2 fusion.51
  132.3 0.9 fusion.24
  133.2 265.9 %all-reduce.11.cloned.1.call-done = f32[6,192,128]{2,1,0:T(8,128)} async-done(((f32[6,192,128]{2,1,0:T(8,128)}), f32[6,192,128]{2,1,0:T(8,128)}) %all-reduce.11.cloned.1.call-update) | async-done | bytes 589840
  399.1 0.8 constant_dynamic-slice_fusion
  400.0 0.3 multiply_reduce_fusion
  400.3 5.6 convert_reduce_fusion.1
  406.0 8.5 %fusion.50 = f32[256,256]{1,0:T(8,128)} fusion(bf16[12288,256]{1,0:T(8,128)(2,1)} %copy-done.11, bf16[256,12288]{1,0:T(8,128)(2,1)} %copy-done.1, f32[12288]{0:T(1024)S(1)} %bitcast.148, f32[256]{0:T(256)S(1)} %convert_element_type.78), kind=kOutput, calls=%fused_computation.116 | convolution fusion | flops 1629487104 | bytes 12895232 | tf_op jit(solution)/shard_map/dot_general | solution.py:39
  414.5 7.6 %convert_reduce_fusion = (f32[256]{0:T(256)S(1)}, bf16[12288,256]{1,0:T(8,128)(2,1)S(1)}) fusion(bf16[12288,256]{1,0:T(8,128)(2,1)} %copy-done.11, bf16[256,256]{1,0:T(8,128)(2,1)S(1)} %copy-done, bf16[256,12288]{1,0:T(8,128)(2,1)S(1)} %bitcast.136, f32[12288]{0:T(1024)S(1)} %bitcast.149, f32[256]{0:T(256)S(1)} %convert_element_type.78), kind=kOutput, calls=%fused_computation.17 | convolution fusion | flops 1651506944 | bytes 19056640 | tf_op jit(solution)/shard_map/dot_general | solution.py:121
  422.0 2.6 copy-done.10
  424.6 2.5 fusion.63
  427.1 8.3 %convert_reduce_fusion.2 = (f32[256]{0:T(256)S(1)}, bf16[256,12288]{1,0:T(8,128)(2,1)S(1)}) fusion(bf16[256,12288]{1,0:T(8,128)(2,1)} %copy-done.2, bf16[12288,256]{1,0:T(8,128)(2,1)} %copy-done.10, bf16[256,256]{1,0:T(8,128)(2,1)S(1)} %copy-done.7), kind=kOutput, calls=%fused_computation.19 | convolution fusion | flops 1632632576 | bytes 19006464 | tf_op jit(solution)/shard_map/dot_general | solution.py:128
  435.5 1.7 convolution_bitcast_fusion.4
  437.2 4.5 fusion.64
  441.8 78.6 %all-reduce.6 = (f32[16,256]{1,0:T(8,128)}, f32[4,256]{1,0:T(4,128)}) all-reduce(f32[16,256]{1,0:T(8,128)S(1)} %convolution_bitcast_fusion.4, f32[4,256]{1,0:T(4,128)S(1)} %pad_maximum_fusion.10), channel_id=1, replica_groups=mesh['blk'=32,'op'=8] {'blk','op'}, use_global_device_ids=true, to_apply=%region_3.5 | all-reduce | flops 5120 | bytes 40960 | tf_op jit(solution)/shard_map/psum | solution.py:134
  520.3 168.9 %all-reduce.13.cloned.1.call-done = (f32[256,256]{1,0:T(8,128)}, f32[256,256]{1,0:T(8,128)}) async-done(((f32[256,256]{1,0:T(8,128)}, f32[256,256]{1,0:T(8,128)}), (f32[256,256]{1,0:T(8,128)}, f32[256,256]{1,0:T(8,128)})) %all-reduce.13.cloned.1.call-update) | async-done | bytes 524304 | tf_op jit(solution)/shard_map/psum | solution.py:134
  689.2 1.7 copy.89
  690.9 1.7 copy.90
  (64 shorter events, 0.5 us)
Async XLA Ops:
  7.2 68.9 %copy-start = (bf16[256,256]{1,0:T(8,128)(2,1)S(1)}, bf16[256,256]{1,0:T(8,128)(2,1)}, u32[]{:S(2)}) copy-start(bf16[256,256]{1,0:T(8,128)(2,1)} %param.25) | copy-start | bytes 393220
  7.2 391.9 %all-reduce.11.cloned.1.call-start = ((), (), s32[]{:S(2)}) async-start(), calls=%async_computation | async-start | bytes 1179648
  8.1 65.3 %copy-start.7 = (bf16[256,256]{1,0:T(8,128)(2,1)S(1)}, bf16[256,256]{1,0:T(8,128)(2,1)}, u32[]{:S(2)}) copy-start(bf16[256,256]{1,0:T(8,128)(2,1)} %param.24) | copy-start | bytes 393220
  73.4 2.6 copy-start.2
  76.0 2.6 copy-start.11
  78.6 2.7 copy-start.1
  81.2 0.9 copy-start.5
  82.2 45.5 %copy-start.3 = (f32[1,6,3,32,128]{4,3,2,1,0:T(8,128)S(1)}, f32[1,6,3,32,128]{4,3,2,1,0:T(8,128)}, u32[]{:S(2)}) copy-start(f32[1,6,3,32,128]{4,3,2,1,0:T(8,128)} %param.20) | copy-start | bytes 884740
  82.2 47.7 %copy-start.8 = (bf16[256]{0:T(256)(128)(2,1)S(1)}, bf16[256]{0:T(256)(128)(2,1)}, u32[]{:S(2)}) copy-start(bf16[256]{0:T(256)(128)(2,1)} %param.26) | copy-start | bytes 1540
  82.9 47.9 %copy-start.9 = (u32[256]{0:T(256)S(1)}, u32[256]{0:T(256)}, u32[]{:S(2)}) copy-start(u32[256]{0:T(256)} %constant.104) | copy-start | bytes 3076
  125.8 6.5 copy-start.6
  126.9 273.0 %copy-start.4 = (f32[1,6,3,32,128]{4,3,2,1,0:T(8,128)S(1)}, f32[1,6,3,32,128]{4,3,2,1,0:T(8,128)}, u32[]{:S(2)}) copy-start(f32[1,6,3,32,128]{4,3,2,1,0:T(8,128)} %param.19) | copy-start | bytes 884740
  129.7 559.5 %all-reduce.13.cloned.1.call-start = ((), (), s32[]{:S(2)}) async-start(), calls=%async_computation.1 | async-start | bytes 1048576 | tf_op jit(solution)/shard_map/psum | solution.py:134
  400.3 14.1 %slice-start = ((s8[6291456]{0:T(1024)(128)(4,1)}), s8[4194304]{0:T(1024)(128)(4,1)S(1)}, s32[]{:S(2)}) async-start(s8[6291456]{0:T(1024)(128)(4,1)} %bitcast.135), calls=%async_computation.2 | async-start | bytes 8388608
  405.9 8.5 %slice-start.1 = ((s8[6291456]{0:T(1024)(128)(4,1)}), s8[2097152]{0:T(1024)(128)(4,1)S(1)}, s32[]{:S(2)}) async-start(s8[6291456]{0:T(1024)(128)(4,1)} %bitcast.135), calls=%async_computation.3 | async-start | bytes 4194304
  406.0 18.6 %slice-start.2 = ((s8[6291456]{0:T(1024)(128)(4,1)}), s8[4194304]{0:T(1024)(128)(4,1)S(1)}, s32[]{:S(2)}) async-start(s8[6291456]{0:T(1024)(128)(4,1)} %bitcast.141), calls=%async_computation.4 | async-start | bytes 8388608
  414.5 10.2 %slice-start.3 = ((s8[6291456]{0:T(1024)(128)(4,1)}), s8[2097152]{0:T(1024)(128)(4,1)S(1)}, s32[]{:S(2)}) async-start(s8[6291456]{0:T(1024)(128)(4,1)} %bitcast.141), calls=%async_computation.5 | async-start | bytes 4194304
  422.0 2.6 copy-start.10
Sparse Core Ops, SparseCore 0:
  129.8 269.3 all-reduce.10
  437.4 251.7 all-reduce.12
where the time goes:
time: 701 us; the launch traced here: 699 us
  waiting for transfers between devices  435 us (62%)
  blocking collectives  175 us (25%)
  matrix products  44.6 us (6%)
  local copies, waits for them, and re-layouts  20.3 us (3%)
  between operations  15.8 us (2%)
  other arithmetic  8.51 us (1%)
    unnamed x3, waiting for transfers between devices  266 us
    psum x1, waiting for transfers between devices, per_device(): lax.psum((grad_in, grad_mid, grad_top, vectors), ('blk', 'op'))  169 us
    all_gather x2, blocking collectives, fetch_ghosts(): every_panel = lax.all_gather(panels, 'blk', axis=1, tiled=True)  96.4 us
    psum x1, blocking collectives, per_device(): lax.psum((grad_in, grad_mid, grad_top, vectors), ('blk', 'op'))  78.6 us
    unnamed x40, local copies, waits for them, and re-layouts  14.1 us
  transfers between devices with their start and end apart: 2, of which 2 were waited for; matrix products, arithmetic and copies ran while one was open for 1% of the time, Pallas kernels for 0%

commit v1 on v0

v1 whole, which is shorter than its diff:
```python
import functools
import math

import jax
import jax.numpy as jnp
from jax import lax
from jax.experimental import pallas as pl
from jax.experimental.pallas import tpu as pltpu
from jax.sharding import PartitionSpec as P

MESH = pl.DeviceIdType.MESH
tau = 0.2
passage_angle = 2.0 * math.pi / 36.0
cos_step = math.cos(passage_angle)
sin_step = math.sin(passage_angle)
highest = lax.Precision.HIGHEST
f32 = jnp.float32
bf16 = jnp.bfloat16

NV, NS, BI, BJ, HID, NF = 6, 3, 32, 128, 256, 16
PL = 8
ZN = 4
ON = 8
NCH = 12
CW = 1024
ROW = NV * BJ


def nt(a, b):
    return lax.dot_general(a, b, (((1,), (1,)), ((), ())), preferred_element_type=f32)


def mm(a, b):
    return jnp.dot(a, b, preferred_element_type=f32)


def lanes_sum(u, lane):
    left = jnp.where(lane == 0, u, pltpu.roll(u, 1, 1))
    right = jnp.where(lane == BJ - 1, u, pltpu.roll(u, BJ - 1, 1))
    return left + right


def kernel(
    loss_scale,
    state, target, feat, coup, in_w, mid_w, top_w, out_w, biases, count, conn, orient, rot,
    out_state, out_in, out_mid, out_top, out_vec,
    x_r, first_r, second_r, third_r,
    win_t, wmid_t, wtop_t, bias_c, ow_c,
    mid_r, ts_r, tm_r, fc_r, beta_r, bc_r,
    plane, zout, zin, inner, tile_r, meta, sel_r, selt_r, ghost_r,
    cz, tbl, ret,
    gtop, gmid, gin, gvec, gout,
    rs1, a1, rs2, rs3, full, sm1, sm2, sm3,
    pl_s, pl_r, me_s, me_r, zz_s, zz_r, cz_s, cz_r, rt_s, rt_r,
    g1_s, g1_r, g2_s, g2_r, g3_s, g3_r, g4_s, g4_r, g5_s, g5_r,
    s1_s, s1_r, s2_s, s2_r, s3_s, s3_r,
):
    b = lax.axis_index("blk")
    o = lax.axis_index("op")
    z = lax.div(b, PL)
    p = lax.rem(b, PL)

    plane_peers = [lax.rem(p + d, PL) for d in range(1, PL)]
    z_peers = [lax.rem(z + d, ZN) for d in range(1, ZN)]
    o_peers = [lax.rem(o + d, ON) for d in range(1, ON)]

    def at_plane(q):
        return {"blk": z * PL + q}

    def at_z(w):
        return {"blk": w * PL + p}

    def at_o(w):
        return {"op": w}

    sent = []

    def send(src, dst, s_sem, r_sem, device):
        copy = pltpu.make_async_remote_copy(
            src_ref=src, dst_ref=dst, send_sem=s_sem, recv_sem=r_sem, device_id=device, device_id_type=MESH
        )
        copy.start()

    def got(dst, s_sem, r_sem, device):
        pltpu.make_async_remote_copy(
            src_ref=dst, dst_ref=dst, send_sem=s_sem, recv_sem=r_sem, device_id=device, device_id_type=MESH
        ).wait_recv()

    def gone(src, s_sem, r_sem, device):
        pltpu.make_async_remote_copy(
            src_ref=src, dst_ref=src, send_sem=s_sem, recv_sem=r_sem, device_id=device, device_id_type=MESH
        ).wait_send()

    barrier = pltpu.get_barrier_semaphore()
    for q in plane_peers:
        pl.semaphore_signal(barrier, inc=1, device_id=at_plane(q), device_id_type=MESH)
    for w in z_peers:
        pl.semaphore_signal(barrier, inc=1, device_id=at_z(w), device_id_type=MESH)
    for w in o_peers:
        pl.semaphore_signal(barrier, inc=1, device_id=at_o(w), device_id_type=MESH)

    rowi = lax.broadcasted_iota(jnp.int32, (8, BJ), 0)
    lane8 = lax.broadcasted_iota(jnp.int32, (8, BJ), 1)
    meta_t = jnp.full((8, BJ), -1.0, f32)
    flip_t = jnp.zeros((8, BJ), f32)
    cos_t = jnp.ones((8, BJ), f32)
    sin_t = jnp.zeros((8, BJ), f32)
    live_t = jnp.zeros((8, BJ), f32)
    live = []
    for s in range(NS):
        live.append(jnp.where(s < count[0], 1.0, 0.0).astype(f32))
        for e in range(2):
            here = rowi == 2 * s + e
            idx = conn[s, e]
            idx = idx + 2 * ((idx * 10923) >> 16)
            meta_t = jnp.where(here, idx.astype(f32), meta_t)
            flip_t = jnp.where(here, orient[s, e].astype(f32), flip_t)
            turn = rot[s, e]
            cos_t = jnp.where(here, jnp.where(turn == 0, 1.0, cos_step).astype(f32), cos_t)
            sin_t = jnp.where(here, turn.astype(f32) * sin_step, sin_t)
            live_t = jnp.where(here, live[s], live_t)
    meta[z] = meta_t
    tile_r[0] = flip_t
    tile_r[1] = cos_t
    tile_r[2] = sin_t
    tile_r[3] = live_t

    def pack(dst, field, rows):
        dst[...] = jnp.zeros((8, ROW), f32)
        for v in range(NV):
            for s in range(NS):
                for e in range(2):
                    dst[2 * s + e:2 * s + e + 1, v * BJ:(v + 1) * BJ] = field[v, s, rows[e]:rows[e] + 1, :]

    def cut(ref):
        return [ref[:, v * BJ:(v + 1) * BJ] for v in range(NV)]

    mine = plane.at[0, p]
    pack(mine, state, (0, BI - 1))

    pl.semaphore_wait(barrier, PL - 1 + ZN - 1 + ON - 1)

    def send_plane(k):
        for q in plane_peers:
            send(plane.at[k, p], plane.at[k, p], pl_s.at[k, q], pl_r.at[k, p], at_plane(q))

    for w in z_peers:
        send(meta.at[z], meta.at[z], me_s.at[w], me_r.at[z], at_z(w))
    send_plane(0)

    def pick(k):
        for q in plane_peers:
            got(plane.at[k, q], pl_s.at[k, q], pl_r.at[k, q], at_plane(q))
        every = plane[k].reshape(PL * 8, ROW)
        chosen = jnp.dot(sel_r[:, :PL * 8], every, preferred_element_type=f32, precision=highest)
        for w in range(ZN):
            zout[k, w] = chosen[8 * w:8 * w + 8]
        zin[k, z] = zout[k, z]
        for w in z_peers:
            send(zout.at[k, w], zin.at[k, z], zz_s.at[k, w], zz_r.at[k, z], at_z(w))

    def make_sel():
        for w in z_peers:
            got(meta.at[w], me_s.at[w], me_r.at[w], at_z(w))
        lane = lax.broadcasted_iota(jnp.int32, (ZN * 8, BJ), 1)
        named = meta[...].reshape(ZN * 8, BJ)
        local = named - (z * (PL * 8)).astype(f32)
        sel = jnp.where((local == lane.astype(f32)) & (lane < PL * 8), 1.0, 0.0).astype(f32)
        sel_r[...] = sel
        selt_r[...] = jnp.concatenate([sel, jnp.zeros((BJ - ZN * 8, BJ), f32)], axis=0).T

    def turned(parts, sign):
        flip, cos, sin = tile_r[0], tile_r[1], tile_r[2] * sign
        whole = jnp.concatenate(parts, axis=0)
        r = lax.broadcasted_iota(jnp.int32, (BJ, BJ), 0)
        c = lax.broadcasted_iota(jnp.int32, (BJ, BJ), 1)
        anti = jnp.where(r + c == BJ - 1, 1.0, 0.0).astype(f32)
        back = jnp.dot(whole, anti, preferred_element_type=f32, precision=highest)
        out = [jnp.where(flip > 0.5, back[8 * v:8 * v + 8], parts[v]) for v in range(NV)]
        c2 = cos * out[2] - sin * out[3]
        c3 = sin * out[2] + cos * out[3]
        return [out[0], out[1], c2, c3, out[4], out[5]]

    def ghosts(k):
        for w in z_peers:
            got(zin.at[k, w], zz_s.at[k, w], zz_r.at[k, w], at_z(w))
        total = (zin[k, 0] + zin[k, 1]) + (zin[k, 2] + zin[k, 3])
        parts = turned([total[:, v * BJ:(v + 1) * BJ] for v in range(NV)], 1.0)
        for v in range(NV):
            ghost_r[k, :, v * BJ:(v + 1) * BJ] = parts[v]

    def edge_beta():
        t = jnp.zeros((8, BJ), f32)
        for s in range(NS):
            for e in range(2):
                row = s * BI + e * (BI - 1)
                t = jnp.where(rowi == 2 * s + e, beta_r[row:row + 1, :], t)
        return t

    def edge_sweep(e, n, gh, beta_e):
        res = []
        for v in range(NV):
            lap = gh[v] + n[v] + lanes_sum(e[v], lane8) - 4.0 * e[v]
            coupled = coup[v, 0] * e[0]
            for w in range(1, NV):
                coupled = coupled + coup[v, w] * e[w]
            res.append(e[v] + tau * (lap - coupled + beta_e * jnp.tanh(e[v])))
        return res

    pad = jnp.zeros((BJ - NF, HID), f32)
    win_t[...] = jnp.concatenate([in_w[...].astype(f32), pad], axis=0).T[:, :NF].astype(bf16)
    wmid_t[...] = mid_w[...].astype(f32).T.astype(bf16)
    wtop_t[...] = top_w[...].astype(f32).T.astype(bf16)
    for k in range(3):
        bias_c[k] = jnp.broadcast_to(biases[k:k + 1, :], (BJ, HID)).T
    ow_c[...] = jnp.broadcast_to(out_w[...].astype(f32), (BJ, HID)).T
    ow_rows = jnp.broadcast_to(out_w[...].astype(f32), (16, HID)).astype(bf16)

    for s in range(NS):
        for h in range(2):
            block = feat[:, s, 16 * h:16 * h + 16, :].astype(f32).reshape(NF * 16, BJ)
            x_t = block.reshape(NF, 16, BJ)
            for r in range(16):
                chunk = 4 * s + 2 * h + r // 8
                x_r[chunk, :, (r % 8) * BJ:(r % 8 + 1) * BJ] = x_t[:, r, :].astype(bf16)

    def chunk_of(k):
        side = lax.rem(k, 2)
        slot = lax.rem(lax.div(k, 2), NS)
        inside = lax.div(k, 6)
        return 4 * slot + 3 * side + inside * (1 - 2 * side)

    SUB = 256

    def forward(k, carry):
        c = chunk_of(k)
        tile = jnp.zeros((8, BJ), f32)
        for j in range(CW // SUB):
            cols = slice(j * SUB, (j + 1) * SUB)
            b0 = jnp.concatenate([bias_c[0]] * (SUB // BJ), axis=1)
            b1 = jnp.concatenate([bias_c[1]] * (SUB // BJ), axis=1)
            b2 = jnp.concatenate([bias_c[2]] * (SUB // BJ), axis=1)
            f1 = jnp.tanh(mm(win_t[...], x_r[c, :, cols]) + b0).astype(bf16)
            first_r[c, :, cols] = f1
            f2 = jnp.tanh(mm(wmid_t[...], f1) + b1).astype(bf16)
            second_r[c, :, cols] = f2
            f3 = jnp.tanh(mm(wtop_t[...], f2) + b2).astype(bf16)
            third_r[c, :, cols] = f3
            bt = mm(ow_rows, f3)[:8] + 1.0
            for i in range(SUB // BJ):
                tile = jnp.where(rowi == j * (SUB // BJ) + i, bt[:, i * BJ:(i + 1) * BJ], tile)
        beta_r[pl.ds(pl.multiple_of(c * 8, 8), 8), :] = tile

        @pl.when(k == 2)
        def _():
            make_sel()
            pick(0)

        @pl.when(k == 5)
        def _():
            ghosts(0)
            pack(inner, state, (1, BI - 2))
            res = edge_sweep(cut(plane.at[0, p]), cut(inner), cut(ghost_r.at[0]), edge_beta())
            for v in range(NV):
                plane[1, p, :, v * BJ:(v + 1) * BJ] = res[v]
            send_plane(1)

        @pl.when(k == 9)
        def _():
            pick(1)

        return carry

    lax.fori_loop(0, NCH, forward, 0)

    rows32 = lax.broadcasted_iota(jnp.int32, (BI, BJ), 0)
    lane32 = lax.broadcasted_iota(jnp.int32, (BI, BJ), 1)

    def stencil(u, low, high):
        up = jnp.where(rows32 == 0, low, pltpu.roll(u, 1, 0))
        down = jnp.where(rows32 == BI - 1, high, pltpu.roll(u, BI - 1, 0))
        return up + down + lanes_sum(u, lane32) - 4.0 * u

    def low_high(k, s, v):
        cols = slice(v * BJ, (v + 1) * BJ)
        return ghost_r[k, 2 * s:2 * s + 1, cols], ghost_r[k, 2 * s + 1:2 * s + 2, cols]

    for s in range(NS):
        us = [state[v, s] for v in range(NV)]
        beta = beta_r[s * BI:(s + 1) * BI, :]
        for v in range(NV):
            t = jnp.tanh(us[v])
            ts_r[v, s] = t
            low, high = low_high(0, s, v)
            coupled = coup[v, 0] * us[0]
            for w in range(1, NV):
                coupled = coupled + coup[v, w] * us[w]
            mid_r[v, s] = us[v] + tau * (stencil(us[v], low, high) - coupled + beta * t)

    ghosts(1)
    pack(inner, mid_r, (1, BI - 2))
    final_e = edge_sweep(cut(plane.at[1, p]), cut(inner), cut(ghost_r.at[1]), edge_beta())
    pack(inner, target, (0, BI - 1))
    goal_e = cut(inner)
    cot_e = [tau * (loss_scale * tile_r[3] * (final_e[v] - goal_e[v])) for v in range(NV)]
    cot_e = turned(cot_e, -1.0)
    for v in range(NV):
        cz[z, :, v * BJ:(v + 1) * BJ] = cot_e[v]
    for w in z_peers:
        send(cz.at[z], cz.at[z], cz_s.at[w], cz_r.at[z], at_z(w))

    for s in range(NS):
        us = [mid_r[v, s] for v in range(NV)]
        beta = beta_r[s * BI:(s + 1) * BI, :]
        for v in range(NV):
            t = jnp.tanh(us[v])
            tm_r[v, s] = t
            low, high = low_high(1, s, v)
            coupled = coup[v, 0] * us[0]
            for w in range(1, NV):
                coupled = coupled + coup[v, w] * us[w]
            final = us[v] + tau * (stencil(us[v], low, high) - coupled + beta * t)
            out_state[v, s] = live[s] * final
            fc_r[v, s] = loss_scale * live[s] * (final - target[v, s])

    for s in range(NS):
        gs = [fc_r[v, s] for v in range(NV)]
        beta = beta_r[s * BI:(s + 1) * BI, :]
        acc = jnp.zeros((BI, BJ), f32)
        for v in range(NV):
            t = tm_r[v, s]
            coupled = coup[0, v] * gs[0]
            for w in range(1, NV):
                coupled = coupled + coup[w, v] * gs[w]
            mc = gs[v] + tau * (stencil(gs[v], 0.0, 0.0) - coupled + beta * (1.0 - t * t) * gs[v])
            acc = acc + (gs[v] * t + mc * ts_r[v, s])
        bc_r[s * BI:(s + 1) * BI, :] = tau * acc

    def table():
        for w in z_peers:
            got(cz.at[w], cz_s.at[w], cz_r.at[w], at_z(w))
        cots = cz[...].reshape(ZN * 8, ROW)
        sums = jnp.dot(selt_r[:PL * 8, :ZN * 8], cots, preferred_element_type=f32, precision=highest)
        for q in range(PL):
            tbl[q] = sums[8 * q:8 * q + 8]
        ret[p] = tbl[p]
        for q in plane_peers:
            send(tbl.at[q], ret.at[p], rt_s.at[q], rt_r.at[p], at_plane(q))

    def returned():
        for q in plane_peers:
            got(ret.at[q], rt_s.at[q], rt_r.at[q], at_plane(q))
        total = ret[0]
        for q in range(1, PL):
            total = total + ret[q]
        start = plane[0, p]
        extra = jnp.zeros((8, BJ), f32)
        for v in range(NV):
            cols = slice(v * BJ, (v + 1) * BJ)
            extra = extra + total[:, cols] * jnp.tanh(start[:, cols])
        for s in range(NS):
            for e in range(2):
                row = s * BI + e * (BI - 1)
                bc_r[row:row + 1, :] = bc_r[row:row + 1, :] + tau * extra[2 * s + e:2 * s + e + 1]

    ones = jnp.ones((16, CW), bf16)
    gout[...] = jnp.zeros((HID, BJ), f32)
    gtop[...] = jnp.zeros((HID + 16, HID), f32)
    gmid[...] = jnp.zeros((HID + 16, HID), f32)
    gin[...] = jnp.zeros((NF + 16, HID), f32)

    def back_top(k, carry):
        c = chunk_of(lax.rem(k + 6, NCH))

        @pl.when(k == 3)
        def _():
            table()

        @pl.when(k == 6)
        def _():
            returned()

        bc = bc_r[pl.ds(pl.multiple_of(c * 8, 8), 8), :]
        ch = bc.astype(bf16).astype(f32)
        RB = 64
        for i in range(HID // RB):
            rows = slice(i * RB, (i + 1) * RB)
            ow = ow_c[rows]
            acc = gout[rows]
            for j in range(CW // BJ):
                cols = slice(j * BJ, (j + 1) * BJ)
                t = third_r[c, rows, cols].astype(f32)
                acc = acc + t * ch[j:j + 1]
                third_r[c, rows, cols] = (ow * bc[j:j + 1] * (1.0 - t * t)).astype(bf16)
            gout[rows] = acc
        gtop[...] += nt(jnp.concatenate([second_r[c], ones], axis=0), third_r[c])
        return carry

    lax.fori_loop(0, NCH, back_top, 0)

    def rs_1(i, g):
        for q in plane_peers:
            part = pl.ds(pl.multiple_of(q * 32, 32), 32)
            send(g.at[part], rs1.at[i, p], g1_s.at[i, q], g1_r.at[i, p], at_plane(q))

    def rs_2(i, g):
        total = g[pl.ds(pl.multiple_of(p * 32, 32), 32), :]
        for q in plane_peers:
            got(rs1.at[i, q], g1_s.at[i, q], g1_r.at[i, q], at_plane(q))
            total = total + rs1[i, q]
        a1[i] = total
        for w in z_peers:
            part = pl.ds(pl.multiple_of(w * 8, 8), 8)
            send(a1.at[i, part], rs2.at[i, z], g2_s.at[i, w], g2_r.at[i, z], at_z(w))

    def rs_3(i):
        total = a1[i, pl.ds(pl.multiple_of(z * 8, 8), 8), :]
        for w in z_peers:
            got(rs2.at[i, w], g2_s.at[i, w], g2_r.at[i, w], at_z(w))
            total = total + rs2[i, w]
        rs3[i, o] = total
        for w in o_peers:
            send(rs3.at[i, o], rs3.at[i, o], g3_s.at[i, w], g3_r.at[i, o], at_o(w))

    def ag_2(i):
        for w in o_peers:
            got(rs3.at[i, w], g3_s.at[i, w], g3_r.at[i, w], at_o(w))
        total = rs3[i, 0]
        for w in range(1, ON):
            total = total + rs3[i, w]
        own = pl.ds(pl.multiple_of(p * 32 + z * 8, 8), 8)
        full[i, own, :] = total
        for w in z_peers:
            send(full.at[i, own], full.at[i, own], g4_s.at[i, w], g4_r.at[i, z], at_z(w))

    def ag_1(i):
        for w in z_peers:
            part = pl.ds(pl.multiple_of(p * 32 + w * 8, 8), 8)
            got(full.at[i, part], g4_s.at[i, w], g4_r.at[i, w], at_z(w))
        own = pl.ds(pl.multiple_of(p * 32, 32), 32)
        for q in plane_peers:
            send(full.at[i, own], full.at[i, own], g5_s.at[i, q], g5_r.at[i, p], at_plane(q))

    def ag_end(i, out):
        for q in plane_peers:
            part = pl.ds(pl.multiple_of(q * 32, 32), 32)
            got(full.at[i, part], g5_s.at[i, q], g5_r.at[i, q], at_plane(q))
        out[...] = full[i]

    def small_1():
        sm1[p, 0:NF] = gin[0:NF]
        sm1[p, NF:NF + 8] = gvec[...]
        for q in plane_peers:
            send(sm1.at[p], sm1.at[p], s1_s.at[q], s1_r.at[p], at_plane(q))

    def small_2():
        for q in plane_peers:
            got(sm1.at[q], s1_s.at[q], s1_r.at[q], at_plane(q))
        total = sm1[0]
        for q in range(1, PL):
            total = total + sm1[q]
        sm2[z] = total
        for w in z_peers:
            send(sm2.at[z], sm2.at[z], s2_s.at[w], s2_r.at[z], at_z(w))

    def small_3():
        for w in z_peers:
            got(sm2.at[w], s2_s.at[w], s2_r.at[w], at_z(w))
        total = (sm2[0] + sm2[1]) + (sm2[2] + sm2[3])
        sm3[o] = total
        for w in o_peers:
            send(sm3.at[o], sm3.at[o], s3_s.at[w], s3_r.at[o], at_o(w))

    def small_end():
        for w in o_peers:
            got(sm3.at[w], s3_s.at[w], s3_r.at[w], at_o(w))
        total = sm3[0]
        for w in range(1, ON):
            total = total + sm3[w]
        out_in[...] = total[0:NF]
        out_vec[...] = total[NF:NF + 4]

    rs_1(0, gtop)

    def back_mid(k, carry):
        for j in range(CW // SUB):
            cols = slice(j * SUB, (j + 1) * SUB)
            s2 = second_r[k, :, cols].astype(f32)
            d = mm(top_w[...], third_r[k, :, cols]) * (1.0 - s2 * s2)
            second_r[k, :, cols] = d.astype(bf16)
        gmid[...] += nt(jnp.concatenate([first_r[k], ones], axis=0), second_r[k])

        @pl.when(k == 6)
        def _():
            rs_2(0, gtop)

        @pl.when(k == 11)
        def _():
            rs_3(0)

        return carry

    lax.fori_loop(0, NCH, back_mid, 0)
    rs_1(1, gmid)

    def back_first(k, carry):
        for j in range(CW // SUB):
            cols = slice(j * SUB, (j + 1) * SUB)
            s1 = first_r[k, :, cols].astype(f32)
            d = mm(mid_w[...], second_r[k, :, cols]) * (1.0 - s1 * s1)
            first_r[k, :, cols] = d.astype(bf16)
        gin[...] += nt(jnp.concatenate([x_r[k], ones], axis=0), first_r[k])

        @pl.when(k == 4)
        def _():
            ag_2(0)

        @pl.when(k == 6)
        def _():
            rs_2(1, gmid)

        @pl.when(k == 9)
        def _():
            ag_1(0)

        @pl.when(k == 11)
        def _():
            rs_3(1)

        return carry

    lax.fori_loop(0, NCH, back_first, 0)

    gvec[...] = jnp.zeros((8, HID), f32)
    gvec[0:1] = jnp.sum(gout[...].T, axis=0, keepdims=True)
    gvec[1:2] = gin[NF:NF + 1]
    gvec[2:3] = gmid[HID:HID + 1]
    gvec[3:4] = gtop[HID:HID + 1]
    small_1()
    ag_2(1)
    small_2()
    ag_1(1)
    small_3()
    ag_end(0, out_top)
    ag_end(1, out_mid)
    small_end()

    for k in range(2):
        for q in plane_peers:
            gone(plane.at[k, p], pl_s.at[k, q], pl_r.at[k, p], at_plane(q))
        for w in z_peers:
            gone(zout.at[k, w], zz_s.at[k, w], zz_r.at[k, z], at_z(w))
    for w in z_peers:
        gone(meta.at[z], me_s.at[w], me_r.at[z], at_z(w))
        gone(cz.at[z], cz_s.at[w], cz_r.at[z], at_z(w))
        gone(sm2.at[z], s2_s.at[w], s2_r.at[z], at_z(w))
    for q in plane_peers:
        gone(tbl.at[q], rt_s.at[q], rt_r.at[p], at_plane(q))
        gone(sm1.at[p], s1_s.at[q], s1_r.at[p], at_plane(q))
    for w in o_peers:
        gone(sm3.at[o], s3_s.at[w], s3_r.at[o], at_o(w))
    for i, g in enumerate((gtop, gmid)):
        for q in plane_peers:
            gone(g.at[pl.ds(pl.multiple_of(q * 32, 32), 32)], g1_s.at[i, q], g1_r.at[i, p], at_plane(q))
            own = pl.ds(pl.multiple_of(p * 32, 32), 32)
            gone(full.at[i, own], g5_s.at[i, q], g5_r.at[i, p], at_plane(q))
        for w in z_peers:
            gone(a1.at[i, pl.ds(pl.multiple_of(w * 8, 8), 8)], g2_s.at[i, w], g2_r.at[i, z], at_z(w))
            own = pl.ds(pl.multiple_of(p * 32 + z * 8, 8), 8)
            gone(full.at[i, own], g4_s.at[i, w], g4_r.at[i, z], at_z(w))
        for w in o_peers:
            gone(rs3.at[i, o], g3_s.at[i, w], g3_r.at[i, o], at_o(w))


def per_device(
    initial_state, target, features, coupling, in_weight, mid_weight, top_weight, out_weight, biases,
    block_count, connectivity, orientation, rotation,
):
    cells = lax.axis_size("op") * lax.axis_size("blk") * NS * BI * BJ
    loss_scale = 2.0 / math.sqrt(cells)
    vmem = pl.BlockSpec(memory_space=pltpu.VMEM)
    smem = pl.BlockSpec(memory_space=pltpu.SMEM)
    dma = pltpu.SemaphoreType.DMA
    field = pltpu.VMEM((NV, NS, BI, BJ), f32)
    outs = pl.pallas_call(
        functools.partial(kernel, loss_scale),
        out_shape=(
            jax.ShapeDtypeStruct((NV, NS, BI, BJ), f32),
            jax.ShapeDtypeStruct((NF, HID), f32),
            jax.ShapeDtypeStruct((HID, HID), f32),
            jax.ShapeDtypeStruct((HID, HID), f32),
            jax.ShapeDtypeStruct((4, HID), f32),
        ),
        in_specs=[vmem, vmem, vmem, smem, vmem, vmem, vmem, vmem, vmem, smem, smem, smem, smem],
        out_specs=(vmem,) * 5,
        scratch_shapes=[
            pltpu.VMEM((NCH, NF, CW), bf16),
            pltpu.VMEM((NCH, HID, CW), bf16),
            pltpu.VMEM((NCH, HID, CW), bf16),
            pltpu.VMEM((NCH, HID, CW), bf16),
            pltpu.VMEM((HID, NF), bf16),
            pltpu.VMEM((HID, HID), bf16),
            pltpu.VMEM((HID, HID), bf16),
            pltpu.VMEM((3, HID, BJ), f32),
            pltpu.VMEM((HID, BJ), f32),
            field, field, field, field,
            pltpu.VMEM((NS * BI, BJ), f32),
            pltpu.VMEM((NS * BI, BJ), f32),
            pltpu.VMEM((2, PL, 8, ROW), f32),
            pltpu.VMEM((2, ZN, 8, ROW), f32),
            pltpu.VMEM((2, ZN, 8, ROW), f32),
            pltpu.VMEM((8, ROW), f32),
            pltpu.VMEM((4, 8, BJ), f32),
            pltpu.VMEM((ZN, 8, BJ), f32),
            pltpu.VMEM((ZN * 8, BJ), f32),
            pltpu.VMEM((BJ, BJ), f32),
            pltpu.VMEM((2, 8, ROW), f32),
            pltpu.VMEM((ZN, 8, ROW), f32),
            pltpu.VMEM((PL, 8, ROW), f32),
            pltpu.VMEM((PL, 8, ROW), f32),
            pltpu.VMEM((HID + 16, HID), f32),
            pltpu.VMEM((HID + 16, HID), f32),
            pltpu.VMEM((NF + 16, HID), f32),
            pltpu.VMEM((8, HID), f32),
            pltpu.VMEM((HID, BJ), f32),
            pltpu.VMEM((2, PL, 32, HID), f32),
            pltpu.VMEM((2, 32, HID), f32),
            pltpu.VMEM((2, ZN, 8, HID), f32),
            pltpu.VMEM((2, ON, 8, HID), f32),
            pltpu.VMEM((2, HID, HID), f32),
            pltpu.VMEM((PL, 24, HID), f32),
            pltpu.VMEM((ZN, 24, HID), f32),
            pltpu.VMEM((ON, 24, HID), f32),
            dma((2, PL)), dma((2, PL)), dma((ZN,)), dma((ZN,)), dma((2, ZN)), dma((2, ZN)),
            dma((ZN,)), dma((ZN,)), dma((PL,)), dma((PL,)),
            dma((2, PL)), dma((2, PL)), dma((2, ZN)), dma((2, ZN)), dma((2, ON)), dma((2, ON)),
            dma((2, ZN)), dma((2, ZN)), dma((2, PL)), dma((2, PL)),
            dma((PL,)), dma((PL,)), dma((ZN,)), dma((ZN,)), dma((ON,)), dma((ON,)),
        ],
        compiler_params=pltpu.CompilerParams(
            collective_id=0, has_side_effects=True, vmem_limit_bytes=56 * 2**20
        ),
    )(
        initial_state[0], target[0], features[0], coupling, in_weight, mid_weight, top_weight,
        out_weight.reshape(1, HID), biases, block_count, connectivity, orientation, rotation,
    )
    return (outs[0][None],) + tuple(outs[1:])


def solution(mesh):
    wide = P("op", None, "blk", None, None)
    return jax.shard_map(
        per_device,
        mesh=mesh,
        in_specs=(wide, wide, wide) + (P(),) * 6 + (P("blk"),) + (P("blk", None),) * 3,
        out_specs=(wide, P(), P(), P(), P()),
        check_vma=False,
    )
```

time: 701 us -> 103 us (0.15)
  waiting for transfers between devices: 435 us -> 0 us
  blocking collectives: 175 us -> 0 us
  Pallas kernels: 0 us -> 93.8 us
  matrix products: 44.6 us -> 0 us
  between operations: 15.8 us -> 1.32 us
  local copies, waits for them, and re-layouts: 20.3 us -> 8.04 us
  other arithmetic: 8.51 us -> 0 us
    unnamed x3 -> x0, waiting for transfers between devices: 266 us -> none
    psum x1 -> x0, waiting for transfers between devices: 169 us -> none  [per_device(): lax.psum((grad_in, grad_mid, grad_top, vectors), ('blk', 'op'))]
    all_gather x2 -> x0, blocking collectives: 96.4 us -> none  [fetch_ghosts(): every_panel = lax.all_gather(panels, 'blk', axis=1, tiled=True)]
    pallas_call x0 -> x1, Pallas kernels: none -> 93.8 us  [per_device(): pl.pallas_call(functools.partial(kernel, loss_scale), out_shape=(jax.Shap...]
    psum x1 -> x0, blocking collectives: 78.6 us -> none  [per_device(): lax.psum((grad_in, grad_mid, grad_top, vectors), ('blk', 'op'))]
    dot_general x14 -> x0, matrix products: 44.6 us -> none  [the longest x3 12.7 us: contract_cells(): lax.dot_general(left_mat, right_mat, (((1,), (1,)), ((), ())), preferred_...]
    unnamed x40 -> x24, local copies, waits for them, and re-layouts: 14.1 us -> 7.47 us
  transfers between devices with their start and end apart: 2 -> 0, of which waited for: 2 -> 0; matrix products, arithmetic and copies ran while one was open for 1% -> 0% of each run, Pallas kernels for 0% -> 0%
where the time goes in v1:
time: 103 us
  Pallas kernels  93.8 us (91%)
  local copies, waits for them, and re-layouts  8.04 us (8%)
  between operations  1.32 us (1%)
    pallas_call x1, Pallas kernels, per_device(): pl.pallas_call(functools.partial(kernel, loss_scale), out_shape=(jax.Shap...  93.8 us
    unnamed x24, local copies, waits for them, and re-layouts  7.47 us

profile of v1, /device:TPU:1, one launch (start us, length us, event | category | flops | bytes accessed | tf_op | source)
XLA Modules:
  0.0 103.1 jit_solution(4977530382827437249)
XLA Ops:
  1.3 0.0 copy-start.7
  1.3 0.6 copy-done.7
  1.9 0.0 copy-start.4
  1.9 0.6 reshape.13.out_w
  2.5 0.1 copy-done.4
  2.6 0.0 copy-start.5
  2.6 0.7 copy.18.conn
  3.3 0.0 copy-done.5
  3.3 0.0 copy-start.6
  3.3 0.7 copy.19.orient
  4.0 0.0 copy-done.6
  4.0 0.7 copy.20.rot
  4.6 93.8 %shard_map.164 = (f32[6,3,32,128]{3,2,1,0:T(8,128)}, f32[16,256]{1,0:T(8,128)}, f32[256,256]{1,0:T(8,128)}, f32[256,256]{1,0:T(8,128)}, f32[4,256]{1,0:T(4,128)}) custom-call(f32[6,3,32,128]{3,2,1,0:T(8,128)} %bitcast.6, f32[6,3,32,128]{3,2,1,0:T(8,128)} %bitcast.7, bf16[16,3,32,128]{3,2,1,0:T(8,128)(2,1)} %bitcast.4, f32[6,6]{1,0:T(8,128)} %coup.1, ...), custom_call_target="tpu_custom_call" | custom-call | tf_op jit(solution)/shard_map/pallas_call | solution.py:585
  98.4 0.0 copy-start.2
  98.4 0.0 copy-start.1
  98.4 1.7 %copy.27 = f32[1,6,3,32,128]{4,3,2,1,0:T(8,128)} copy(f32[1,6,3,32,128]{4,3,2,1,0:T(8,128)} %bitcast.5) | data formatting | bytes 589824
  100.2 0.0 copy-done.2
  100.2 0.6 copy.28
  100.8 0.0 copy-done.1
  100.8 0.0 copy-start
  100.8 0.7 copy.29
  101.5 0.3 copy-done
  101.8 0.0 copy-start.3
  101.8 0.7 copy.30
  102.5 0.0 copy-done.3
  102.5 0.6 copy.31
Async XLA Ops:
  1.3 0.7 copy-start.7
  1.9 0.7 copy-start.4
  2.6 0.7 copy-start.5
  3.3 0.7 copy-start.6
  98.4 1.8 %copy-start.2 = (f32[16,256]{1,0:T(8,128)S(1)}, f32[16,256]{1,0:T(8,128)}, u32[]{:S(2)}) copy-start(f32[16,256]{1,0:T(8,128)} %get-tuple-element.21) | copy-start | bytes 49156
  98.4 2.4 %copy-start.1 = (f32[256,256]{1,0:T(8,128)S(1)}, f32[256,256]{1,0:T(8,128)}, u32[]{:S(2)}) copy-start(f32[256,256]{1,0:T(8,128)} %get-tuple-element.22) | copy-start | bytes 786436
  100.8 1.0 %copy-start = (f32[256,256]{1,0:T(8,128)S(1)}, f32[256,256]{1,0:T(8,128)}, u32[]{:S(2)}) copy-start(f32[256,256]{1,0:T(8,128)} %get-tuple-element.23) | copy-start | bytes 786436
  101.8 0.7 copy-start.3

commit v2 on v1

v2 whole, which is shorter than its diff:
```python
import functools
import math

import jax
import jax.numpy as jnp
from jax import lax
from jax.experimental import pallas as pl
from jax.experimental.pallas import tpu as pltpu
from jax.sharding import PartitionSpec as P

MESH = pl.DeviceIdType.MESH
tau = 0.2
passage_angle = 2.0 * math.pi / 36.0
cos_step = math.cos(passage_angle)
sin_step = math.sin(passage_angle)
highest = lax.Precision.HIGHEST
f32 = jnp.float32
bf16 = jnp.bfloat16

NV, NS, BI, BJ, HID, NF = 6, 3, 32, 128, 256, 16
PL = 8
ZN = 4
OWN = PL * ZN
NCH = 12
CW = 1024
EDGE = NCH - 1
AN = 32
BN = 8


def row_of(s, i):
    if i == 0 or i == BI - 1:
        return 8 * EDGE + 2 * s + (i != 0)
    inner = (BI - 2) * s + i - 1
    return inner if inner < 8 * EDGE else inner + 2 * NS


def runs(s):
    whole = (BI - 2) * s
    first = min(BI - 2, 8 * EDGE - whole)
    res = [(1, whole, first)]
    if first < BI - 2:
        res.append((1 + first, row_of(s, 1 + first), BI - 2 - first))
    return res


def nt(a, b):
    return lax.dot_general(a, b, (((1,), (1,)), ((), ())), preferred_element_type=f32)


def mm(a, b):
    return jnp.dot(a, b, preferred_element_type=f32)


def lanes_sum(u, lane):
    left = jnp.where(lane == 0, u, pltpu.roll(u, 1, 1))
    right = jnp.where(lane == BJ - 1, u, pltpu.roll(u, BJ - 1, 1))
    return left + right


def kernel(
    loss_scale,
    state, target, feat, coup, in_w, mid_w, top_w, out_w, biases, count, conn, orient, rot,
    out_state, out_in, out_mid, out_top, out_vec,
    x_r, first_r, second_r, third_r,
    xs, win_t, wmid_t, wtop_t, bias_c, ow_c,
    mid_r, ts_r, tm_r, fc_r, beta_r, betan_r, bc_r, bcn_r,
    edge, gath, picked, arr, inner, tile_r, meta, sel_r, selt_r, anti, ghost_r,
    cote, cz, tbl, ret,
    gtop, gmid, gin, gout,
    ra, rb, full, sg, sa, sb, sf,
    pl_s, pl_r, me_s, me_r, zz_s, zz_r, cz_s, cz_r, rt_s, rt_r,
    a1_s, a1_r, a2_s, a2_r, a3_s, a3_r, s1_s, s1_r, s2_s, s2_r, s3_s, s3_r,
):
    b = lax.axis_index("blk")
    o = lax.axis_index("op")
    z = lax.div(b, PL)
    p = lax.rem(b, PL)
    x_at = lax.div(o, 2)
    z_lo = lax.rem(o, 2)
    a = x_at * PL + p
    zz = z * 2 + z_lo

    def at_own(q):
        return {"blk": q}

    def at_a(q):
        return {"blk": z * PL + lax.rem(q, PL), "op": lax.div(q, PL) * 2 + z_lo}

    def at_b(w):
        return {"blk": lax.div(w, 2) * PL + p, "op": x_at * 2 + lax.rem(w, 2)}

    def send(src, dst, s_sem, r_sem, device):
        copy = pltpu.make_async_remote_copy(
            src_ref=src, dst_ref=dst, send_sem=s_sem, recv_sem=r_sem, device_id=device, device_id_type=MESH
        )
        copy.start()

    def got(dst, s_sem, r_sem, device):
        pltpu.make_async_remote_copy(
            src_ref=dst, dst_ref=dst, send_sem=s_sem, recv_sem=r_sem, device_id=device, device_id_type=MESH
        ).wait_recv()

    def gone(src, s_sem, r_sem, device):
        pltpu.make_async_remote_copy(
            src_ref=src, dst_ref=src, send_sem=s_sem, recv_sem=r_sem, device_id=device, device_id_type=MESH
        ).wait_send()

    barrier = pltpu.get_barrier_semaphore()
    def every(first, last, body):
        def step(d, carry):
            body(d)
            return carry

        lax.fori_loop(first, last, step, 0)

    def greet(device):
        pl.semaphore_signal(barrier, inc=1, device_id=device, device_id_type=MESH)

    every(1, OWN, lambda d: greet(at_own(lax.rem(b + d, OWN))))
    every(PL, AN, lambda d: greet(at_a(lax.rem(x_at * PL + d, AN))))
    every(0, ZN, lambda d: greet(at_b(2 * d + 1 - z_lo)))

    rowi = lax.broadcasted_iota(jnp.int32, (8, BJ), 0)
    lane8 = lax.broadcasted_iota(jnp.int32, (8, BJ), 1)
    row1 = lax.broadcasted_iota(jnp.int32, (1, BJ), 1) - lax.rem(b, 16) * 8
    meta_t = jnp.where((row1 >= 6) & (row1 < 8), -1000.0, 0.0).astype(f32)
    flip_t = jnp.zeros((8, BJ), f32)
    cos_t = jnp.ones((8, BJ), f32)
    sin_t = jnp.zeros((8, BJ), f32)
    live_t = jnp.zeros((8, BJ), f32)
    live = []
    for s in range(NS):
        live.append(jnp.where(s < count[0], 1.0, 0.0).astype(f32))
        for e in range(2):
            here = rowi == 2 * s + e
            idx = conn[e, s]
            idx = idx + 2 * ((idx * 10923) >> 16)
            meta_t = jnp.where(row1 == 2 * s + e, idx.astype(f32), meta_t)
            flip_t = jnp.where(here, orient[e, s].astype(f32), flip_t)
            turn = rot[e, s]
            cos_t = jnp.where(here, jnp.where(turn == 0, 1.0, cos_step).astype(f32), cos_t)
            sin_t = jnp.where(here, turn.astype(f32) * sin_step, sin_t)
            live_t = jnp.where(here, live[s], live_t)
    meta[b] = meta_t
    tile_r[0] = flip_t
    tile_r[1] = cos_t
    tile_r[2] = sin_t
    tile_r[3] = live_t

    def pack(dst, field, rows):
        dst[...] = jnp.zeros((NV, 8, BJ), f32)
        for v in range(NV):
            for s in range(NS):
                for e in range(2):
                    dst[v, 2 * s + e:2 * s + e + 1, :] = field[v, s, rows[e]:rows[e] + 1, :]

    def cut(ref):
        return [ref[v] for v in range(NV)]

    def thirds(u):
        u1 = u.astype(bf16)
        u2 = (u - u1.astype(f32)).astype(bf16)
        u3 = (u - u1.astype(f32) - u2.astype(f32)).astype(bf16)
        return u1, u2, u3

    def by_rows(mask, u):
        r = mm(mask, jnp.concatenate(thirds(u), axis=1))
        return r[:, :BJ] + r[:, BJ:2 * BJ] + r[:, 2 * BJ:]

    pack(edge.at[0], state, (0, BI - 1))
    anti_r = lax.broadcasted_iota(jnp.int32, (BJ, BJ), 0)
    anti_c = lax.broadcasted_iota(jnp.int32, (BJ, BJ), 1)
    anti[...] = jnp.where(anti_r + anti_c == BJ - 1, 1.0, 0.0).astype(bf16)

    pad = jnp.zeros((BJ - NF, HID), f32)
    win_t[...] = jnp.concatenate([in_w[...].astype(f32), pad], axis=0).T[:, :NF].astype(bf16)
    wmid_t[...] = mid_w[...].astype(f32).T.astype(bf16)
    wtop_t[...] = top_w[...].astype(f32).T.astype(bf16)
    for k in range(3):
        bias_c[k] = jnp.broadcast_to(biases[k:k + 1, :], (BJ, HID)).T
    ow_c[...] = jnp.broadcast_to(out_w[...].astype(f32).reshape(1, HID), (BJ, HID)).T

    for s in range(NS):
        for h in range(2):
            xs[s, h] = feat[:, s, 16 * h:16 * h + 16, :].astype(f32).reshape(NF * 16, BJ)
    for s in range(NS):
        for h in range(2):
            for r in range(16):
                row = row_of(s, 16 * h + r)
                x_r[row // 8, :, (row % 8) * BJ:(row % 8 + 1) * BJ] = xs[s, h, pl.ds(r, NF, stride=16), :].astype(bf16)

    pl.semaphore_wait(barrier, OWN - 1 + AN - PL + ZN)

    def send_plane(k):
        for v in range(NV):
            @pl.when(p != v)
            def _():
                send(edge.at[k, v], gath.at[k, p], pl_s.at[k], pl_r.at[k], at_own(z * PL + v))

        @pl.when(p < NV)
        def _():
            gath[k, p] = edge[k, p]

    send_plane(0)
    every(1, OWN, lambda d: send(meta.at[b], meta.at[b], me_s, me_r, at_own(lax.rem(b + d, OWN))))

    def make_sel():
        got(meta.at[pl.ds(0, OWN - 1)], me_s, me_r, at_own(b))
        panel = lax.broadcasted_iota(jnp.int32, (BJ, BJ), 0)
        for h in range(2):
            named = jnp.sum(meta[16 * h:16 * h + 16], axis=0) - (z * (PL * 8)).astype(f32)
            sel = jnp.where((named == panel.astype(f32)) & (panel < PL * 8), 1.0, 0.0).astype(f32)
            selt_r[:, h * BJ:(h + 1) * BJ] = sel[:PL * 8].astype(bf16)
            sel_r[h * BJ:(h + 1) * BJ, :] = sel.T[:, :PL * 8].astype(bf16)

    def pick(k):
        @pl.when(p < NV)
        def _():
            got(gath.at[k, pl.ds(0, PL - 1)], pl_s.at[k], pl_r.at[k], at_own(b))
            chosen = by_rows(sel_r[...], gath[k].reshape(PL * 8, BJ))
            picked[k] = chosen.reshape(OWN, 8, BJ)
            arr[k, z * NV + p] = picked[k, b]

            def part(d):
                q = lax.rem(b + d, OWN)
                send(picked.at[k, q], arr.at[k, z * NV + p], zz_s.at[k], zz_r.at[k], at_own(q))

            every(1, OWN, part)

    def turned(parts, sign):
        flip, cos, sin = tile_r[0], tile_r[1], tile_r[2] * sign
        r = mm(jnp.concatenate(thirds(jnp.concatenate(parts, axis=0)), axis=0), anti[...])
        n = 8 * NV
        back = r[:n] + r[n:2 * n] + r[2 * n:]
        out = [jnp.where(flip > 0.5, back[8 * v:8 * v + 8], parts[v]) for v in range(NV)]
        c2 = cos * out[2] - sin * out[3]
        c3 = sin * out[2] + cos * out[3]
        return [out[0], out[1], c2, c3, out[4], out[5]]

    def got_some(ref, few, s_sem, r_sem):
        @pl.when(p < NV)
        def _():
            got(ref.at[pl.ds(0, few)], s_sem, r_sem, at_own(b))

        @pl.when(p >= NV)
        def _():
            got(ref.at[pl.ds(0, few + 1)], s_sem, r_sem, at_own(b))

    def gone_some(ref, few, s_sem, r_sem):
        @pl.when(p < NV)
        def _():
            gone(ref.at[pl.ds(0, few)], s_sem, r_sem, at_own(b))

        @pl.when(p >= NV)
        def _():
            gone(ref.at[pl.ds(0, few + 1)], s_sem, r_sem, at_own(b))

    def ghosts(k):
        got_some(arr.at[k], ZN * NV - 1, zz_s.at[k], zz_r.at[k])
        parts = [
            (arr[k, v] + arr[k, NV + v]) + (arr[k, 2 * NV + v] + arr[k, 3 * NV + v]) for v in range(NV)
        ]
        parts = turned(parts, 1.0)
        for v in range(NV):
            ghost_r[k, v] = parts[v]

    def edge_sweep(e, n, gh):
        res = []
        beta_e = jnp.where(rowi < 2 * NS, beta_r[8 * EDGE:8 * EDGE + 8, :], 0.0)
        for v in range(NV):
            lap = gh[v] + n[v] + lanes_sum(e[v], lane8) - 4.0 * e[v]
            coupled = coup[v, 0] * e[0]
            for w in range(1, NV):
                coupled = coupled + coup[v, w] * e[w]
            res.append(e[v] + tau * (lap - coupled + beta_e * jnp.tanh(e[v])))
        return res

    SUB = 256

    weights = (win_t, wmid_t, wtop_t)
    acts = (x_r, first_r, second_r, third_r)
    SUBS = 2 * CW // SUB

    def forward(k, carry):
        pair = (lax.rem(2 * k + EDGE, NCH), 2 * k)

        def place(j):
            return pair[j // (CW // SUB)], slice((j % (CW // SUB)) * SUB, (j % (CW // SUB) + 1) * SUB)

        def product(layer, j):
            c, cols = place(j)
            return mm(weights[layer][...], acts[layer][c, :, cols])

        tiles = [jnp.zeros((8, BJ), f32), jnp.zeros((8, BJ), f32)]

        def activate(layer, j, d):
            c, cols = place(j)
            bias = bias_c[layer]
            for i in range(SUB // BJ):
                t = jnp.tanh(d[:, i * BJ:(i + 1) * BJ] + bias).astype(bf16)
                acts[layer + 1][c, :, cols.start + i * BJ:cols.start + (i + 1) * BJ] = t
                if layer == 2:
                    bt = jnp.sum(ow_c[...] * t.astype(f32), axis=0, keepdims=True) + 1.0
                    row = (j % (CW // SUB)) * (SUB // BJ) + i
                    half = j // (CW // SUB)
                    tiles[half] = jnp.where(rowi == row, bt, tiles[half])

        tasks = [(layer, j) for layer in range(3) for j in range(SUBS)]
        held = None
        for task in tasks:
            d = product(*task)
            if held is not None:
                activate(*held)
            held = task + (d,)
        activate(*held)
        for half in range(2):
            beta_r[pl.ds(pl.multiple_of(pair[half] * 8, 8), 8), :] = tiles[half]

        @pl.when(k == 0)
        def _():
            make_sel()
            pick(0)

        @pl.when(k == 2)
        def _():
            ghosts(0)
            pack(inner, state, (1, BI - 2))
            res = edge_sweep(cut(edge.at[0]), cut(inner), cut(ghost_r.at[0]))
            for v in range(NV):
                edge[1, v] = res[v]
            send_plane(1)

        @pl.when(k == 3)
        def _():
            pick(1)

        return carry

    lax.fori_loop(0, NCH // 2, forward, 0)

    for s in range(NS):
        for e in range(2):
            g = 8 * EDGE + 2 * s + e
            row = s * BI + e * (BI - 1)
            betan_r[row:row + 1, :] = beta_r[g:g + 1, :]
        for first, place, length in runs(s):
            betan_r[s * BI + first:s * BI + first + length, :] = beta_r[place:place + length, :]

    rows32 = lax.broadcasted_iota(jnp.int32, (BI, BJ), 0)
    lane32 = lax.broadcasted_iota(jnp.int32, (BI, BJ), 1)

    def stencil(u, low, high):
        up = jnp.where(rows32 == 0, low, pltpu.roll(u, 1, 0))
        down = jnp.where(rows32 == BI - 1, high, pltpu.roll(u, BI - 1, 0))
        return up + down + lanes_sum(u, lane32) - 4.0 * u

    def low_high(k, s, v):
        return ghost_r[k, v, 2 * s:2 * s + 1, :], ghost_r[k, v, 2 * s + 1:2 * s + 2, :]

    for s in range(NS):
        us = [state[v, s] for v in range(NV)]
        beta = betan_r[s * BI:(s + 1) * BI, :]
        for v in range(NV):
            t = jnp.tanh(us[v])
            ts_r[v, s] = t
            low, high = low_high(0, s, v)
            coupled = coup[v, 0] * us[0]
            for w in range(1, NV):
                coupled = coupled + coup[v, w] * us[w]
            mid_r[v, s] = us[v] + tau * (stencil(us[v], low, high) - coupled + beta * t)

    ghosts(1)
    pack(inner, mid_r, (1, BI - 2))
    final_e = edge_sweep(cut(edge.at[1]), cut(inner), cut(ghost_r.at[1]))
    pack(inner, target, (0, BI - 1))
    goal_e = cut(inner)
    cot_e = [tau * (loss_scale * tile_r[3] * (final_e[v] - goal_e[v])) for v in range(NV)]
    cot_e = turned(cot_e, -1.0)
    for v in range(NV):
        cote[v] = cot_e[v]
    for w in range(ZN):
        for v in range(NV):
            there = w * PL + v

            @pl.when(b != there)
            def _():
                send(cote.at[v], cz.at[b], cz_s, cz_r, at_own(there))

    @pl.when(p < NV)
    def _():
        cz[b] = cote[p]

    for s in range(NS):
        us = [mid_r[v, s] for v in range(NV)]
        beta = betan_r[s * BI:(s + 1) * BI, :]
        for v in range(NV):
            t = jnp.tanh(us[v])
            tm_r[v, s] = t
            low, high = low_high(1, s, v)
            coupled = coup[v, 0] * us[0]
            for w in range(1, NV):
                coupled = coupled + coup[v, w] * us[w]
            final = us[v] + tau * (stencil(us[v], low, high) - coupled + beta * t)
            out_state[v, s] = live[s] * final
            fc_r[v, s] = loss_scale * live[s] * (final - target[v, s])

    for s in range(NS):
        gs = [fc_r[v, s] for v in range(NV)]
        beta = betan_r[s * BI:(s + 1) * BI, :]
        acc = jnp.zeros((BI, BJ), f32)
        for v in range(NV):
            t = tm_r[v, s]
            coupled = coup[0, v] * gs[0]
            for w in range(1, NV):
                coupled = coupled + coup[w, v] * gs[w]
            mc = gs[v] + tau * (stencil(gs[v], 0.0, 0.0) - coupled + beta * (1.0 - t * t) * gs[v])
            acc = acc + (gs[v] * t + mc * ts_r[v, s])
        bcn_r[s * BI:(s + 1) * BI, :] = tau * acc
        for first, place, length in runs(s):
            bc_r[place:place + length, :] = bcn_r[s * BI + first:s * BI + first + length, :]

    def table():
        @pl.when(p < NV)
        def _():
            got(cz.at[pl.ds(0, OWN - 1)], cz_s, cz_r, at_own(b))
            sums = by_rows(selt_r[...], cz[...].reshape(OWN * 8, BJ))
            tbl[...] = sums.reshape(PL, 8, BJ)
            ret[p] = tbl[p]

            def part(d):
                q = lax.rem(p + d, PL)
                send(tbl.at[q], ret.at[p], rt_s, rt_r, at_own(z * PL + q))

            every(1, PL, part)

    def returned():
        got_some(ret, NV - 1, rt_s, rt_r)
        extra = jnp.zeros((8, BJ), f32)
        for v in range(NV):
            extra = extra + ret[v] * jnp.tanh(edge[0, v])
        for s in range(NS):
            for e in range(2):
                g = 2 * s + e
                row = s * BI + e * (BI - 1)
                bc_r[8 * EDGE + g:8 * EDGE + g + 1, :] = bcn_r[row:row + 1, :] + tau * extra[g:g + 1]

    ones = jnp.ones((16, CW), bf16)
    gout[...] = jnp.zeros((HID, BJ), f32)
    gtop[...] = jnp.zeros((HID + 16, HID), f32)
    gmid[...] = jnp.zeros((HID + 16, HID), f32)
    gin[...] = jnp.zeros((NF + 16, HID), f32)

    def weigh(c, acc, left, right, fresh=None):
        part = nt(jnp.concatenate([left[c], ones], axis=0), right[c])
        if fresh is not None:
            part = jnp.where(fresh, part, 0.0)
        acc[...] = acc[...] + part

    def before(k, half):
        return lax.rem(2 * k + half + NCH - 2, NCH)

    RB = 64

    def top_delta(c):
        bc = bc_r[pl.ds(pl.multiple_of(c * 8, 8), 8), :]
        ch = bc.astype(bf16).astype(f32)
        for i in range(HID // RB):
            rows = slice(i * RB, (i + 1) * RB)
            ow = ow_c[rows]
            acc = gout[rows]
            for j in range(CW // BJ):
                cols = slice(j * BJ, (j + 1) * BJ)
                t = third_r[c, rows, cols].astype(f32)
                acc = acc + t * ch[j:j + 1]
                third_r[c, rows, cols] = (ow * bc[j:j + 1] * (1.0 - t * t)).astype(bf16)
            gout[rows] = acc

    def back_top(k, carry):
        for half in range(2):
            weigh(before(k, half), gtop, second_r, third_r, k > 0)
            top_delta(2 * k + half)
        return carry

    def layer_back(k, weight, source, act, acc, left, fresh=None):
        held = None

        def put(c, cols, d):
            for i in range(SUB // BJ):
                here = slice(cols.start + i * BJ, cols.start + (i + 1) * BJ)
                t = act[c, :, here].astype(f32)
                act[c, :, here] = (d[:, i * BJ:(i + 1) * BJ] * (1.0 - t * t)).astype(bf16)

        for half in range(2):
            c = 2 * k + half
            for j in range(CW // SUB):
                cols = slice(j * SUB, (j + 1) * SUB)
                d = mm(weight[...], source[c, :, cols])
                if held is not None:
                    put(*held)
                held = (c, cols, d)
            if half == 0:
                weigh(before(k, 0), acc, left, act, fresh)
        put(*held)
        weigh(before(k, 1), acc, left, act, fresh)

    def back_mid(k, carry):
        layer_back(k, top_w, third_r, second_r, gmid, first_r, k > 0)
        return carry

    def ar_1(i, g):
        def part(d):
            q = lax.rem(a + d, AN)
            send(g.at[pl.ds(pl.multiple_of(q * 8, 8), 8)], ra.at[i, a], a1_s.at[i], a1_r.at[i], at_a(q))

        every(1, AN, part)
        ra[i, a] = g[pl.ds(pl.multiple_of(a * 8, 8), 8), :]

    def ar_2(i):
        got(ra.at[i, pl.ds(0, AN - 1)], a1_s.at[i], a1_r.at[i], at_a(a))
        total = ra[i, 0]
        for q in range(1, AN):
            total = total + ra[i, q]
        rb[i, zz] = total
        for d in range(1, BN):
            w = lax.rem(zz + d, BN)
            send(rb.at[i, zz], rb.at[i, zz], a2_s.at[i], a2_r.at[i], at_b(w))

    def ar_3(i):
        got(rb.at[i, pl.ds(0, BN - 1)], a2_s.at[i], a2_r.at[i], at_b(zz))
        total = rb[i, 0]
        for w in range(1, BN):
            total = total + rb[i, w]
        full[i, a] = total
        every(1, AN, lambda d: send(full.at[i, a], full.at[i, a], a3_s.at[i], a3_r.at[i], at_a(lax.rem(a + d, AN))))

    def ar_4(i, out):
        got(full.at[i, pl.ds(0, AN - 1)], a3_s.at[i], a3_r.at[i], at_a(a))
        out[...] = full[i].reshape(HID, HID)

    def small_1():
        for r in range(NF):
            sg[r] = gin[r:r + 1]
        sg[NF] = jnp.sum(gout[...].T, axis=0, keepdims=True)
        sg[NF + 1] = gin[NF:NF + 1]
        sg[NF + 2] = gmid[HID:HID + 1]
        sg[NF + 3] = gtop[HID:HID + 1]
        sg[NF + 4:] = jnp.zeros((AN - NF - 4, 1, HID), f32)
        def part(d):
            q = lax.rem(a + d, AN)
            send(sg.at[q], sa.at[a], s1_s, s1_r, at_a(q))

        every(1, AN, part)
        sa[a] = sg[a]

    def small_2():
        got(sa.at[pl.ds(0, AN - 1)], s1_s, s1_r, at_a(a))
        sb[zz] = jnp.sum(sa[...], axis=0)
        for d in range(1, BN):
            w = lax.rem(zz + d, BN)
            send(sb.at[zz], sb.at[zz], s2_s, s2_r, at_b(w))

    def small_3():
        got(sb.at[pl.ds(0, BN - 1)], s2_s, s2_r, at_b(zz))
        sf[a] = jnp.sum(sb[...], axis=0)
        every(1, AN, lambda d: send(sf.at[a], sf.at[a], s3_s, s3_r, at_a(lax.rem(a + d, AN))))

    def small_4():
        got(sf.at[pl.ds(0, AN - 1)], s3_s, s3_r, at_a(a))
        for r in range(NF):
            out_in[r:r + 1] = sf[r]
        for r in range(4):
            out_vec[r:r + 1] = sf[NF + r]

    LAST = NCH // 2 - 1
    lax.fori_loop(0, LAST, back_top, 0)
    weigh(EDGE - 3, gtop, second_r, third_r)
    weigh(EDGE - 2, gtop, second_r, third_r)
    table()
    lax.fori_loop(0, LAST, back_mid, 0)
    top_delta(EDGE - 1)
    weigh(EDGE - 1, gtop, second_r, third_r)
    returned()
    top_delta(EDGE)
    weigh(EDGE, gtop, second_r, third_r)
    ar_1(0, gtop)
    layer_back(LAST, top_w, third_r, second_r, gmid, first_r)
    weigh(EDGE - 1, gmid, first_r, second_r)
    weigh(EDGE, gmid, first_r, second_r)
    ar_1(1, gmid)

    def back_first(k, carry):
        layer_back(k, mid_w, second_r, first_r, gin, x_r, k > 0)

        @pl.when(k == 3)
        def _():
            ar_2(0)

        @pl.when(k == 5)
        def _():
            ar_2(1)

        return carry

    lax.fori_loop(0, LAST + 1, back_first, 0)
    weigh(EDGE - 1, gin, x_r, first_r)
    weigh(EDGE, gin, x_r, first_r)

    small_1()
    ar_3(0)
    ar_3(1)
    small_2()
    ar_4(0, out_top)
    small_3()
    ar_4(1, out_mid)
    small_4()

    gone(meta.at[pl.ds(0, OWN - 1)], me_s, me_r, at_own(b))
    for k in range(2):
        gone_some(edge.at[k], NV - 1, pl_s.at[k], pl_r.at[k])

        @pl.when(p < NV)
        def _():
            gone(picked.at[k, pl.ds(0, OWN - 1)], zz_s.at[k], zz_r.at[k], at_own(b))
    gone_some(cz, ZN * NV - 1, cz_s, cz_r)

    @pl.when(p < NV)
    def _():
        gone(tbl.at[pl.ds(0, PL - 1)], rt_s, rt_r, at_own(b))
    for i in range(2):
        gone(ra.at[i, pl.ds(0, AN - 1)], a1_s.at[i], a1_r.at[i], at_a(a))
        gone(rb.at[i, pl.ds(0, BN - 1)], a2_s.at[i], a2_r.at[i], at_b(zz))
        gone(full.at[i, pl.ds(0, AN - 1)], a3_s.at[i], a3_r.at[i], at_a(a))
    gone(sa.at[pl.ds(0, AN - 1)], s1_s, s1_r, at_a(a))
    gone(sb.at[pl.ds(0, BN - 1)], s2_s, s2_r, at_b(zz))
    gone(sf.at[pl.ds(0, AN - 1)], s3_s, s3_r, at_a(a))


def copy_kernel(*refs):
    ins, outs, sem = refs[:5], refs[5:10], refs[10]
    copies = [pltpu.make_async_copy(ins[i], outs[i], sem.at[i]) for i in range(5)]
    for copy in copies:
        copy.start()
    for copy in copies:
        copy.wait()


def per_device(
    initial_state, target, features, coupling, in_weight, mid_weight, top_weight, out_weight, biases,
    block_count, connectivity, orientation, rotation,
):
    cells = lax.axis_size("op") * lax.axis_size("blk") * NS * BI * BJ
    loss_scale = 2.0 / math.sqrt(cells)
    vmem = pl.BlockSpec(memory_space=pltpu.VMEM)
    smem = pl.BlockSpec(memory_space=pltpu.SMEM)
    dma = pltpu.SemaphoreType.DMA
    field = pltpu.VMEM((NV, NS, BI, BJ), f32)
    outs = pl.pallas_call(
        functools.partial(kernel, loss_scale),
        out_shape=(
            jax.ShapeDtypeStruct((NV, NS, BI, BJ), f32),
            jax.ShapeDtypeStruct((NF, HID), f32),
            jax.ShapeDtypeStruct((HID, HID), f32),
            jax.ShapeDtypeStruct((HID, HID), f32),
            jax.ShapeDtypeStruct((4, HID), f32),
        ),
        in_specs=[vmem, vmem, vmem, smem, vmem, vmem, vmem, vmem, vmem, smem, smem, smem, smem],
        out_specs=(vmem,) * 5,
        scratch_shapes=[
            pltpu.VMEM((NCH, NF, CW), bf16),
            pltpu.VMEM((NCH, HID, CW), bf16),
            pltpu.VMEM((NCH, HID, CW), bf16),
            pltpu.VMEM((NCH, HID, CW), bf16),
            pltpu.VMEM((NS, 2, NF * 16, BJ), f32),
            pltpu.VMEM((HID, NF), bf16),
            pltpu.VMEM((HID, HID), bf16),
            pltpu.VMEM((HID, HID), bf16),
            pltpu.VMEM((3, HID, BJ), f32),
            pltpu.VMEM((HID, BJ), f32),
            field, field, field, field,
            pltpu.VMEM((NS * BI, BJ), f32),
            pltpu.VMEM((NS * BI, BJ), f32),
            pltpu.VMEM((NS * BI, BJ), f32),
            pltpu.VMEM((NS * BI, BJ), f32),
            pltpu.VMEM((2, NV, 8, BJ), f32),
            pltpu.VMEM((2, PL, 8, BJ), f32),
            pltpu.VMEM((2, OWN, 8, BJ), f32),
            pltpu.VMEM((2, ZN * NV, 8, BJ), f32),
            pltpu.VMEM((NV, 8, BJ), f32),
            pltpu.VMEM((4, 8, BJ), f32),
            pltpu.VMEM((OWN, 1, BJ), f32),
            pltpu.VMEM((OWN * 8, PL * 8), bf16),
            pltpu.VMEM((PL * 8, OWN * 8), bf16),
            pltpu.VMEM((BJ, BJ), bf16),
            pltpu.VMEM((2, NV, 8, BJ), f32),
            pltpu.VMEM((NV, 8, BJ), f32),
            pltpu.VMEM((OWN, 8, BJ), f32),
            pltpu.VMEM((PL, 8, BJ), f32),
            pltpu.VMEM((NV, 8, BJ), f32),
            pltpu.VMEM((HID + 16, HID), f32),
            pltpu.VMEM((HID + 16, HID), f32),
            pltpu.VMEM((NF + 16, HID), f32),
            pltpu.VMEM((HID, BJ), f32),
            pltpu.VMEM((2, AN, 8, HID), f32),
            pltpu.VMEM((2, BN, 8, HID), f32),
            pltpu.VMEM((2, AN, 8, HID), f32),
            pltpu.VMEM((AN, 1, HID), f32),
            pltpu.VMEM((AN, 1, HID), f32),
            pltpu.VMEM((BN, 1, HID), f32),
            pltpu.VMEM((AN, 1, HID), f32),
            dma((2,)), dma((2,)), dma, dma, dma((2,)), dma((2,)), dma, dma, dma, dma,
            dma((2,)), dma((2,)), dma((2,)), dma((2,)), dma((2,)), dma((2,)),
            dma, dma, dma, dma, dma, dma,
        ],
        compiler_params=pltpu.CompilerParams(
            collective_id=0, has_side_effects=True, vmem_limit_bytes=56 * 2**20
        ),
    )(
        initial_state[0], target[0], features[0], coupling, in_weight, mid_weight, top_weight,
        out_weight, biases, block_count, connectivity.T, orientation.T, rotation.T,
    )
    outs = pl.pallas_call(
        copy_kernel,
        out_shape=tuple(jax.ShapeDtypeStruct(x.shape, x.dtype) for x in outs),
        in_specs=[vmem] * 5,
        out_specs=(pl.BlockSpec(memory_space=pl.ANY),) * 5,
        scratch_shapes=[dma((5,))],
    )(*outs)
    return (outs[0][None],) + tuple(outs[1:])


def solution(mesh):
    wide = P("op", None, "blk", None, None)
    return jax.shard_map(
        per_device,
        mesh=mesh,
        in_specs=(wide, wide, wide) + (P(),) * 6 + (P("blk"),) + (P("blk", None),) * 3,
        out_specs=(wide, P(), P(), P(), P()),
        check_vma=False,
    )
```

time: 103 us -> 80.2 us (0.78)
  Pallas kernels: 93.8 us -> 78.8 us
  local copies, waits for them, and re-layouts: 8.04 us -> 0 us
    pallas_call x1, Pallas kernels: 93.8 us -> 76.7 us  [per_device(): pl.pallas_call(functools.partial(kernel, loss_scale), out_shape=(jax.Shap...]
    unnamed x24 -> x0, local copies, waits for them, and re-layouts: 7.47 us -> none
    pallas_call x0 -> x1, Pallas kernels: none -> 2.07 us  [per_device(): pl.pallas_call(copy_kernel, out_shape=tuple((jax.ShapeDtypeStruct(x.shape...]
where the time goes in v2:
time: 80.2 us; the launch traced here: 80 us
  Pallas kernels  78.8 us (98%)
  between operations  1.29 us (2%)
    pallas_call x1, Pallas kernels, per_device(): pl.pallas_call(functools.partial(kernel, loss_scale), out_shape=(jax.Shap...  76.7 us
    pallas_call x1, Pallas kernels, per_device(): pl.pallas_call(copy_kernel, out_shape=tuple((jax.ShapeDtypeStruct(x.shape...  2.07 us

profile of v2, /device:TPU:1, one launch (start us, length us, event | category | flops | bytes accessed | tf_op | source)
XLA Modules:
  0.0 80.0 jit_solution(1839473817790940688)
XLA Ops:
  1.3 76.7 %shard_map.164 = (f32[6,3,32,128]{3,2,1,0:T(8,128)}, f32[16,256]{1,0:T(8,128)}, f32[256,256]{1,0:T(8,128)}, f32[256,256]{1,0:T(8,128)}, f32[4,256]{1,0:T(4,128)}) custom-call(f32[6,3,32,128]{3,2,1,0:T(8,128)} %bitcast.8, f32[6,3,32,128]{3,2,1,0:T(8,128)} %bitcast.9, bf16[16,3,32,128]{3,2,1,0:T(8,128)(2,1)} %bitcast.7, f32[6,6]{1,0:T(8,128)} %coup.1, ...), custom_call_target="tpu_custom_call" | custom-call | tf_op jit(solution)/shard_map/pallas_call | solution.py:658
  78.0 2.1 %shard_map.165 = (f32[6,3,32,128]{3,2,1,0:T(8,128)}, f32[16,256]{1,0:T(8,128)}, f32[256,256]{1,0:T(8,128)}, f32[256,256]{1,0:T(8,128)}, f32[4,256]{1,0:T(4,128)}) custom-call(f32[6,3,32,128]{3,2,1,0:T(8,128)} %get-tuple-element.15.refs_0_, f32[16,256]{1,0:T(8,128)} %get-tuple-element.16.refs_1_, f32[256,256]{1,0:T(8,128)} %get-tuple-element.17.refs_2_, ...), custom_call_target="tpu_custom_call" | custom-call | tf_op jit(solution)/shard_map/pallas_call | solution.py:722

commit v3 on v2

--- a/solution.py
+++ b/solution.py
@@ -20,12 +20,12 @@
 NV, NS, BI, BJ, HID, NF = 6, 3, 32, 128, 256, 16
 PL = 8
 ZN = 4
-OWN = PL * ZN
 NCH = 12
 CW = 1024
 EDGE = NCH - 1
-AN = 32
+AN = 16
 BN = 8
+ROW = NV * BJ
 
 
 def row_of(s, i):
@@ -65,27 +65,37 @@
     x_r, first_r, second_r, third_r,
     xs, win_t, wmid_t, wtop_t, bias_c, ow_c,
     mid_r, ts_r, tm_r, fc_r, beta_r, betan_r, bc_r, bcn_r,
-    edge, gath, picked, arr, inner, tile_r, meta, sel_r, selt_r, anti, ghost_r,
-    cote, cz, tbl, ret,
+    plane, zout, zin, inner, tile_r, meta, sel_r, selt_r, ghost_r,
+    cz, tbl, ret,
     gtop, gmid, gin, gout,
-    ra, rb, full, sg, sa, sb, sf,
+    cg, gsum, ra, rb, full, other, sg, sc, sa, sb, sf, st,
     pl_s, pl_r, me_s, me_r, zz_s, zz_r, cz_s, cz_r, rt_s, rt_r,
-    a1_s, a1_r, a2_s, a2_r, a3_s, a3_r, s1_s, s1_r, s2_s, s2_r, s3_s, s3_r,
+    c_s, c_r, a1_s, a1_r, a2_s, a2_r, a3_s, a3_r, f_s, f_r, s0_s, s0_r, s1_s, s1_r, s2_s, s2_r, s3_s, s3_r,
 ):
     b = lax.axis_index("blk")
     o = lax.axis_index("op")
     z = lax.div(b, PL)
     p = lax.rem(b, PL)
+
+    plane_peers = [lax.rem(p + d, PL) for d in range(1, PL)]
+    z_peers = [lax.rem(z + d, ZN) for d in range(1, ZN)]
     x_at = lax.div(o, 2)
     z_lo = lax.rem(o, 2)
-    a = x_at * PL + p
+    core = lax.rem(b, 2)
+    a = x_at * ZN + lax.div(p, 2)
     zz = z * 2 + z_lo
 
-    def at_own(q):
-        return {"blk": q}
+    def at_plane(q):
+        return {"blk": z * PL + q}
+
+    def at_z(w):
+        return {"blk": w * PL + p}
 
     def at_a(q):
-        return {"blk": z * PL + lax.rem(q, PL), "op": lax.div(q, PL) * 2 + z_lo}
+        return {"blk": z * PL + lax.rem(q, 4) * 2 + core, "op": lax.div(q, 4) * 2 + z_lo}
+
+    def partner():
+        return {"blk": b + 1 - 2 * core}
 
     def at_b(w):
         return {"blk": lax.div(w, 2) * PL + p, "op": x_at * 2 + lax.rem(w, 2)}
@@ -107,24 +117,19 @@
         ).wait_send()
 
     barrier = pltpu.get_barrier_semaphore()
-    def every(first, last, body):
-        def step(d, carry):
-            body(d)
-            return carry
-
-        lax.fori_loop(first, last, step, 0)
-
     def greet(device):
         pl.semaphore_signal(barrier, inc=1, device_id=device, device_id_type=MESH)
 
-    every(1, OWN, lambda d: greet(at_own(lax.rem(b + d, OWN))))
-    every(PL, AN, lambda d: greet(at_a(lax.rem(x_at * PL + d, AN))))
-    every(0, ZN, lambda d: greet(at_b(2 * d + 1 - z_lo)))
+    for q in plane_peers:
+        greet(at_plane(q))
+    for d in range(4, AN):
+        greet(at_a(lax.rem(x_at * 4 + d, AN)))
+    for d in range(1, BN):
+        greet(at_b(lax.rem(zz + d, BN)))
 
     rowi = lax.broadcasted_iota(jnp.int32, (8, BJ), 0)
     lane8 = lax.broadcasted_iota(jnp.int32, (8, BJ), 1)
-    row1 = lax.broadcasted_iota(jnp.int32, (1, BJ), 1) - lax.rem(b, 16) * 8
-    meta_t = jnp.where((row1 >= 6) & (row1 < 8), -1000.0, 0.0).astype(f32)
+    meta_t = jnp.full((8, BJ), -1.0, f32)
     flip_t = jnp.zeros((8, BJ), f32)
     cos_t = jnp.ones((8, BJ), f32)
     sin_t = jnp.zeros((8, BJ), f32)
@@ -136,42 +141,30 @@
             here = rowi == 2 * s + e
             idx = conn[e, s]
             idx = idx + 2 * ((idx * 10923) >> 16)
-            meta_t = jnp.where(row1 == 2 * s + e, idx.astype(f32), meta_t)
+            meta_t = jnp.where(here, idx.astype(f32), meta_t)
             flip_t = jnp.where(here, orient[e, s].astype(f32), flip_t)
             turn = rot[e, s]
             cos_t = jnp.where(here, jnp.where(turn == 0, 1.0, cos_step).astype(f32), cos_t)
             sin_t = jnp.where(here, turn.astype(f32) * sin_step, sin_t)
             live_t = jnp.where(here, live[s], live_t)
-    meta[b] = meta_t
+    meta[z] = meta_t
     tile_r[0] = flip_t
     tile_r[1] = cos_t
     tile_r[2] = sin_t
     tile_r[3] = live_t
 
     def pack(dst, field, rows):
-        dst[...] = jnp.zeros((NV, 8, BJ), f32)
+        dst[...] = jnp.zeros((8, ROW), f32)
         for v in range(NV):
             for s in range(NS):
                 for e in range(2):
-                    dst[v, 2 * s + e:2 * s + e + 1, :] = field[v, s, rows[e]:rows[e] + 1, :]
+                    dst[2 * s + e:2 * s + e + 1, v * BJ:(v + 1) * BJ] = field[v, s, rows[e]:rows[e] + 1, :]
 
     def cut(ref):
-        return [ref[v] for v in range(NV)]
-
-    def thirds(u):
-        u1 = u.astype(bf16)
-        u2 = (u - u1.astype(f32)).astype(bf16)
-        u3 = (u - u1.astype(f32) - u2.astype(f32)).astype(bf16)
-        return u1, u2, u3
-
-    def by_rows(mask, u):
-        r = mm(mask, jnp.concatenate(thirds(u), axis=1))
-        return r[:, :BJ] + r[:, BJ:2 * BJ] + r[:, 2 * BJ:]
-
-    pack(edge.at[0], state, (0, BI - 1))
-    anti_r = lax.broadcasted_iota(jnp.int32, (BJ, BJ), 0)
-    anti_c = lax.broadcasted_iota(jnp.int32, (BJ, BJ), 1)
-    anti[...] = jnp.where(anti_r + anti_c == BJ - 1, 1.0, 0.0).astype(bf16)
+        return [ref[:, v * BJ:(v + 1) * BJ] for v in range(NV)]
+
+    mine = plane.at[0, p]
+    pack(mine, state, (0, BI - 1))
 
     pad = jnp.zeros((BJ - NF, HID), f32)
     win_t[...] = jnp.concatenate([in_w[...].astype(f32), pad], axis=0).T[:, :NF].astype(bf16)
@@ -190,80 +183,56 @@
                 row = row_of(s, 16 * h + r)
                 x_r[row // 8, :, (row % 8) * BJ:(row % 8 + 1) * BJ] = xs[s, h, pl.ds(r, NF, stride=16), :].astype(bf16)
 
-    pl.semaphore_wait(barrier, OWN - 1 + AN - PL + ZN)
+    pl.semaphore_wait(barrier, PL - 1 + AN - 4 + BN - 1)
 
     def send_plane(k):
-        for v in range(NV):
-            @pl.when(p != v)
-            def _():
-                send(edge.at[k, v], gath.at[k, p], pl_s.at[k], pl_r.at[k], at_own(z * PL + v))
-
-        @pl.when(p < NV)
-        def _():
-            gath[k, p] = edge[k, p]
-
+        for q in plane_peers:
+            send(plane.at[k, p], plane.at[k, p], pl_s.at[k, q], pl_r.at[k, p], at_plane(q))
+
+    for w in z_peers:
+        send(meta.at[z], meta.at[z], me_s.at[w], me_r.at[z], at_z(w))
     send_plane(0)
-    every(1, OWN, lambda d: send(meta.at[b], meta.at[b], me_s, me_r, at_own(lax.rem(b + d, OWN))))
+
+    def pick(k):
+        for q in plane_peers:
+            got(plane.at[k, q], pl_s.at[k, q], pl_r.at[k, q], at_plane(q))
+        every = plane[k].reshape(PL * 8, ROW)
+        chosen = jnp.dot(sel_r[:, :PL * 8], every, preferred_element_type=f32, precision=highest)
+        for w in range(ZN):
+            zout[k, w] = chosen[8 * w:8 * w + 8]
+        zin[k, z] = zout[k, z]
+        for w in z_peers:
+            send(zout.at[k, w], zin.at[k, z], zz_s.at[k, w], zz_r.at[k, z], at_z(w))
 
     def make_sel():
-        got(meta.at[pl.ds(0, OWN - 1)], me_s, me_r, at_own(b))
-        panel = lax.broadcasted_iota(jnp.int32, (BJ, BJ), 0)
-        for h in range(2):
-            named = jnp.sum(meta[16 * h:16 * h + 16], axis=0) - (z * (PL * 8)).astype(f32)
-            sel = jnp.where((named == panel.astype(f32)) & (panel < PL * 8), 1.0, 0.0).astype(f32)
-            selt_r[:, h * BJ:(h + 1) * BJ] = sel[:PL * 8].astype(bf16)
-            sel_r[h * BJ:(h + 1) * BJ, :] = sel.T[:, :PL * 8].astype(bf16)
-
-    def pick(k):
-        @pl.when(p < NV)
-        def _():
-            got(gath.at[k, pl.ds(0, PL - 1)], pl_s.at[k], pl_r.at[k], at_own(b))
-            chosen = by_rows(sel_r[...], gath[k].reshape(PL * 8, BJ))
-            picked[k] = chosen.reshape(OWN, 8, BJ)
-            arr[k, z * NV + p] = picked[k, b]
-
-            def part(d):
-                q = lax.rem(b + d, OWN)
-                send(picked.at[k, q], arr.at[k, z * NV + p], zz_s.at[k], zz_r.at[k], at_own(q))
-
-            every(1, OWN, part)
+        for w in z_peers:
+            got(meta.at[w], me_s.at[w], me_r.at[w], at_z(w))
+        lane = lax.broadcasted_iota(jnp.int32, (ZN * 8, BJ), 1)
+        named = meta[...].reshape(ZN * 8, BJ)
+        local = named - (z * (PL * 8)).astype(f32)
+        sel = jnp.where((local == lane.astype(f32)) & (lane < PL * 8), 1.0, 0.0).astype(f32)
+        sel_r[...] = sel
+        selt_r[...] = jnp.concatenate([sel, jnp.zeros((BJ - ZN * 8, BJ), f32)], axis=0).T
 
     def turned(parts, sign):
         flip, cos, sin = tile_r[0], tile_r[1], tile_r[2] * sign
-        r = mm(jnp.concatenate(thirds(jnp.concatenate(parts, axis=0)), axis=0), anti[...])
-        n = 8 * NV
-        back = r[:n] + r[n:2 * n] + r[2 * n:]
+        whole = jnp.concatenate(parts, axis=0)
+        r = lax.broadcasted_iota(jnp.int32, (BJ, BJ), 0)
+        c = lax.broadcasted_iota(jnp.int32, (BJ, BJ), 1)
+        anti = jnp.where(r + c == BJ - 1, 1.0, 0.0).astype(f32)
+        back = jnp.dot(whole, anti, preferred_element_type=f32, precision=highest)
         out = [jnp.where(flip > 0.5, back[8 * v:8 * v + 8], parts[v]) for v in range(NV)]
         c2 = cos * out[2] - sin * out[3]
         c3 = sin * out[2] + cos * out[3]
         return [out[0], out[1], c2, c3, out[4], out[5]]
 
-    def got_some(ref, few, s_sem, r_sem):
-        @pl.when(p < NV)
-        def _():
-            got(ref.at[pl.ds(0, few)], s_sem, r_sem, at_own(b))
-
-        @pl.when(p >= NV)
-        def _():
-            got(ref.at[pl.ds(0, few + 1)], s_sem, r_sem, at_own(b))
-
-    def gone_some(ref, few, s_sem, r_sem):
-        @pl.when(p < NV)
-        def _():
-            gone(ref.at[pl.ds(0, few)], s_sem, r_sem, at_own(b))
-
-        @pl.when(p >= NV)
-        def _():
-            gone(ref.at[pl.ds(0, few + 1)], s_sem, r_sem, at_own(b))
-
     def ghosts(k):
-        got_some(arr.at[k], ZN * NV - 1, zz_s.at[k], zz_r.at[k])
-        parts = [
-            (arr[k, v] + arr[k, NV + v]) + (arr[k, 2 * NV + v] + arr[k, 3 * NV + v]) for v in range(NV)
-        ]
-        parts = turned(parts, 1.0)
+        for w in z_peers:
+            got(zin.at[k, w], zz_s.at[k, w], zz_r.at[k, w], at_z(w))
+        total = (zin[k, 0] + zin[k, 1]) + (zin[k, 2] + zin[k, 3])
+        parts = turned([total[:, v * BJ:(v + 1) * BJ] for v in range(NV)], 1.0)
         for v in range(NV):
-            ghost_r[k, v] = parts[v]
+            ghost_r[k, :, v * BJ:(v + 1) * BJ] = parts[v]
 
     def edge_sweep(e, n, gh):
         res = []
@@ -326,12 +295,12 @@
         def _():
             ghosts(0)
             pack(inner, state, (1, BI - 2))
-            res = edge_sweep(cut(edge.at[0]), cut(inner), cut(ghost_r.at[0]))
+            res = edge_sweep(cut(plane.at[0, p]), cut(inner), cut(ghost_r.at[0]))
             for v in range(NV):
-                edge[1, v] = res[v]
+                plane[1, p, :, v * BJ:(v + 1) * BJ] = res[v]
             send_plane(1)
 
-        @pl.when(k == 3)
+        @pl.when(k == 4)
         def _():
             pick(1)
 
@@ -356,7 +325,8 @@
         return up + down + lanes_sum(u, lane32) - 4.0 * u
 
     def low_high(k, s, v):
-        return ghost_r[k, v, 2 * s:2 * s + 1, :], ghost_r[k, v, 2 * s + 1:2 * s + 2, :]
+        cols = slice(v * BJ, (v + 1) * BJ)
+        return ghost_r[k, 2 * s:2 * s + 1, cols], ghost_r[k, 2 * s + 1:2 * s + 2, cols]
 
     for s in range(NS):
         us = [state[v, s] for v in range(NV)]
@@ -372,24 +342,15 @@
 
     ghosts(1)
     pack(inner, mid_r, (1, BI - 2))
-    final_e = edge_sweep(cut(edge.at[1]), cut(inner), cut(ghost_r.at[1]))
+    final_e = edge_sweep(cut(plane.at[1, p]), cut(inner), cut(ghost_r.at[1]))
     pack(inner, target, (0, BI - 1))
     goal_e = cut(inner)
     cot_e = [tau * (loss_scale * tile_r[3] * (final_e[v] - goal_e[v])) for v in range(NV)]
     cot_e = turned(cot_e, -1.0)
     for v in range(NV):
-        cote[v] = cot_e[v]
-    for w in range(ZN):
-        for v in range(NV):
-            there = w * PL + v
-
-            @pl.when(b != there)
-            def _():
-                send(cote.at[v], cz.at[b], cz_s, cz_r, at_own(there))
-
-    @pl.when(p < NV)
-    def _():
-        cz[b] = cote[p]
+        cz[z, :, v * BJ:(v + 1) * BJ] = cot_e[v]
+    for w in z_peers:
+        send(cz.at[z], cz.at[z], cz_s.at[w], cz_r.at[z], at_z(w))
 
     for s in range(NS):
         us = [mid_r[v, s] for v in range(NV)]
@@ -421,24 +382,27 @@
             bc_r[place:place + length, :] = bcn_r[s * BI + first:s * BI + first + length, :]
 
     def table():
-        @pl.when(p < NV)
-        def _():
-            got(cz.at[pl.ds(0, OWN - 1)], cz_s, cz_r, at_own(b))
-            sums = by_rows(selt_r[...], cz[...].reshape(OWN * 8, BJ))
-            tbl[...] = sums.reshape(PL, 8, BJ)
-            ret[p] = tbl[p]
-
-            def part(d):
-                q = lax.rem(p + d, PL)
-                send(tbl.at[q], ret.at[p], rt_s, rt_r, at_own(z * PL + q))
-
-            every(1, PL, part)
+        for w in z_peers:
+            got(cz.at[w], cz_s.at[w], cz_r.at[w], at_z(w))
+        cots = cz[...].reshape(ZN * 8, ROW)
+        sums = jnp.dot(selt_r[:PL * 8, :ZN * 8], cots, preferred_element_type=f32, precision=highest)
+        for q in range(PL):
+            tbl[q] = sums[8 * q:8 * q + 8]
+        ret[p] = tbl[p]
+        for q in plane_peers:
+            send(tbl.at[q], ret.at[p], rt_s.at[q], rt_r.at[p], at_plane(q))
 
     def returned():
-        got_some(ret, NV - 1, rt_s, rt_r)
+        for q in plane_peers:
+            got(ret.at[q], rt_s.at[q], rt_r.at[q], at_plane(q))
+        total = ret[0]
+        for q in range(1, PL):
+            total = total + ret[q]
+        start = plane[0, p]
         extra = jnp.zeros((8, BJ), f32)
         for v in range(NV):
-            extra = extra + ret[v] * jnp.tanh(edge[0, v])
+            cols = slice(v * BJ, (v + 1) * BJ)
+            extra = extra + total[:, cols] * jnp.tanh(start[:, cols])
         for s in range(NS):
             for e in range(2):
                 g = 2 * s + e
@@ -508,69 +472,83 @@
         layer_back(k, top_w, third_r, second_r, gmid, first_r, k > 0)
         return carry
 
-    def ar_1(i, g):
-        def part(d):
+    grads = (gtop, gmid)
+    R = HID // AN
+
+    def hand(i):
+        @pl.when(core != i)
+        def _():
+            send(grads[i].at[pl.ds(0, HID)], cg, c_s, c_r, partner())
+
+    def ar_1(i):
+        got(cg, c_s, c_r, partner())
+        gsum[...] = (grads[i][0:HID] + cg[...]).reshape(AN, R, HID)
+        for d in range(1, AN):
             q = lax.rem(a + d, AN)
-            send(g.at[pl.ds(pl.multiple_of(q * 8, 8), 8)], ra.at[i, a], a1_s.at[i], a1_r.at[i], at_a(q))
-
-        every(1, AN, part)
-        ra[i, a] = g[pl.ds(pl.multiple_of(a * 8, 8), 8), :]
-
-    def ar_2(i):
-        got(ra.at[i, pl.ds(0, AN - 1)], a1_s.at[i], a1_r.at[i], at_a(a))
-        total = ra[i, 0]
+            send(gsum.at[q], ra.at[a], a1_s, a1_r, at_a(q))
+        ra[a] = gsum[a]
+
+    def ar_2():
+        got(ra.at[pl.ds(0, AN - 1)], a1_s, a1_r, at_a(a))
+        total = ra[0]
         for q in range(1, AN):
-            total = total + ra[i, q]
-        rb[i, zz] = total
+            total = total + ra[q]
+        rb[zz] = total
         for d in range(1, BN):
-            w = lax.rem(zz + d, BN)
-            send(rb.at[i, zz], rb.at[i, zz], a2_s.at[i], a2_r.at[i], at_b(w))
-
-    def ar_3(i):
-        got(rb.at[i, pl.ds(0, BN - 1)], a2_s.at[i], a2_r.at[i], at_b(zz))
-        total = rb[i, 0]
+            send(rb.at[zz], rb.at[zz], a2_s, a2_r, at_b(lax.rem(zz + d, BN)))
+
+    def ar_3():
+        got(rb.at[pl.ds(0, BN - 1)], a2_s, a2_r, at_b(zz))
+        total = rb[0]
         for w in range(1, BN):
-            total = total + rb[i, w]
-        full[i, a] = total
-        every(1, AN, lambda d: send(full.at[i, a], full.at[i, a], a3_s.at[i], a3_r.at[i], at_a(lax.rem(a + d, AN))))
-
-    def ar_4(i, out):
-        got(full.at[i, pl.ds(0, AN - 1)], a3_s.at[i], a3_r.at[i], at_a(a))
-        out[...] = full[i].reshape(HID, HID)
+            total = total + rb[w]
+        full[a] = total
+        for d in range(1, AN):
+            send(full.at[a], full.at[a], a3_s, a3_r, at_a(lax.rem(a + d, AN)))
+
+    def ar_4(out):
+        got(full.at[pl.ds(0, AN - 1)], a3_s, a3_r, at_a(a))
+        send(full, other, f_s, f_r, partner())
+        out[...] = full[...].reshape(HID, HID)
+
+    def ar_5(out):
+        got(other, f_s, f_r, partner())
+        out[...] = other[...].reshape(HID, HID)
+
+    def small_0():
+        sg[0:NF] = gin[0:NF]
+        sg[NF:NF + 1] = jnp.sum(gout[...].T, axis=0, keepdims=True)
+        sg[NF + 1:NF + 2] = gin[NF:NF + 1]
+        sg[NF + 2:NF + 3] = gmid[HID:HID + 1]
+        sg[NF + 3:NF + 4] = gtop[HID:HID + 1]
+        sg[NF + 4:NF + 8] = jnp.zeros((4, HID), f32)
+
+        @pl.when(core == 1)
+        def _():
+            send(sg, sc, s0_s, s0_r, partner())
 
     def small_1():
-        for r in range(NF):
-            sg[r] = gin[r:r + 1]
-        sg[NF] = jnp.sum(gout[...].T, axis=0, keepdims=True)
-        sg[NF + 1] = gin[NF:NF + 1]
-        sg[NF + 2] = gmid[HID:HID + 1]
-        sg[NF + 3] = gtop[HID:HID + 1]
-        sg[NF + 4:] = jnp.zeros((AN - NF - 4, 1, HID), f32)
-        def part(d):
-            q = lax.rem(a + d, AN)
-            send(sg.at[q], sa.at[a], s1_s, s1_r, at_a(q))
-
-        every(1, AN, part)
-        sa[a] = sg[a]
+        got(sc, s0_s, s0_r, partner())
+        sa[a] = sg[...] + sc[...]
+        for d in range(1, AN):
+            send(sa.at[a], sa.at[a], s1_s, s1_r, at_a(lax.rem(a + d, AN)))
 
     def small_2():
         got(sa.at[pl.ds(0, AN - 1)], s1_s, s1_r, at_a(a))
-        sb[zz] = jnp.sum(sa[...], axis=0)
+        total = sa[0]
+        for q in range(1, AN):
+            total = total + sa[q]
+        sb[zz] = total
         for d in range(1, BN):
-            w = lax.rem(zz + d, BN)
-            send(sb.at[zz], sb.at[zz], s2_s, s2_r, at_b(w))
+            send(sb.at[zz], sb.at[zz], s2_s, s2_r, at_b(lax.rem(zz + d, BN)))
 
     def small_3():
         got(sb.at[pl.ds(0, BN - 1)], s2_s, s2_r, at_b(zz))
-        sf[a] = jnp.sum(sb[...], axis=0)
-        every(1, AN, lambda d: send(sf.at[a], sf.at[a], s3_s, s3_r, at_a(lax.rem(a + d, AN))))
-
-    def small_4():
-        got(sf.at[pl.ds(0, AN - 1)], s3_s, s3_r, at_a(a))
-        for r in range(NF):
-            out_in[r:r + 1] = sf[r]
-        for r in range(4):
-            out_vec[r:r + 1] = sf[NF + r]
+        total = sb[0]
+        for w in range(1, BN):
+            total = total + sb[w]
+        sf[...] = total
+        send(sf, st, s3_s, s3_r, partner())
 
     LAST = NCH // 2 - 1
     lax.fori_loop(0, LAST, back_top, 0)
@@ -583,22 +561,26 @@
     returned()
     top_delta(EDGE)
     weigh(EDGE, gtop, second_r, third_r)
-    ar_1(0, gtop)
+    hand(0)
     layer_back(LAST, top_w, third_r, second_r, gmid, first_r)
     weigh(EDGE - 1, gmid, first_r, second_r)
     weigh(EDGE, gmid, first_r, second_r)
-    ar_1(1, gmid)
+    hand(1)
+
+    @pl.when(core == 0)
+    def _():
+        ar_1(0)
 
     def back_first(k, carry):
         layer_back(k, mid_w, second_r, first_r, gin, x_r, k > 0)
 
-        @pl.when(k == 3)
+        @pl.when((k == 1) & (core == 1))
         def _():
-            ar_2(0)
-
-        @pl.when(k == 5)
+            ar_1(1)
+
+        @pl.when((k == 4) & (core == 0))
         def _():
-            ar_2(1)
+            ar_2()
 
         return carry
 
@@ -606,34 +588,54 @@
     weigh(EDGE - 1, gin, x_r, first_r)
     weigh(EDGE, gin, x_r, first_r)
 
-    small_1()
-    ar_3(0)
-    ar_3(1)
-    small_2()
-    ar_4(0, out_top)
-    small_3()
-    ar_4(1, out_mid)
-    small_4()
-
-    gone(meta.at[pl.ds(0, OWN - 1)], me_s, me_r, at_own(b))
+    small_0()
+
+    @pl.when(core == 0)
+    def _():
+        small_1()
+        ar_3()
+        small_2()
+        ar_4(out_top)
+        small_3()
+        out_in[...] = sf[0:NF]
+        out_vec[...] = sf[NF:NF + 4]
+        ar_5(out_mid)
+
+    @pl.when(core == 1)
+    def _():
+        ar_2()
+        ar_3()
+        ar_4(out_mid)
+        ar_5(out_top)
+        got(st, s3_s, s3_r, partner())
+        out_in[...] = st[0:NF]
+        out_vec[...] = st[NF:NF + 4]
+
     for k in range(2):
-        gone_some(edge.at[k], NV - 1, pl_s.at[k], pl_r.at[k])
-
-        @pl.when(p < NV)
-        def _():
-            gone(picked.at[k, pl.ds(0, OWN - 1)], zz_s.at[k], zz_r.at[k], at_own(b))
-    gone_some(cz, ZN * NV - 1, cz_s, cz_r)
-
-    @pl.when(p < NV)
+        for q in plane_peers:
+            gone(plane.at[k, p], pl_s.at[k, q], pl_r.at[k, p], at_plane(q))
+        for w in z_peers:
+            gone(zout.at[k, w], zz_s.at[k, w], zz_r.at[k, z], at_z(w))
+    for w in z_peers:
+        gone(meta.at[z], me_s.at[w], me_r.at[z], at_z(w))
+        gone(cz.at[z], cz_s.at[w], cz_r.at[z], at_z(w))
+    for q in plane_peers:
+        gone(tbl.at[q], rt_s.at[q], rt_r.at[p], at_plane(q))
+    gone(cg, c_s, c_r, partner())
+    gone(ra.at[pl.ds(0, AN - 1)], a1_s, a1_r, at_a(a))
+    gone(rb.at[pl.ds(0, BN - 1)], a2_s, a2_r, at_b(zz))
+    gone(full.at[pl.ds(0, AN - 1)], a3_s, a3_r, at_a(a))
+    gone(full, f_s, f_r, partner())
+
+    @pl.when(core == 0)
     def _():
-        gone(tbl.at[pl.ds(0, PL - 1)], rt_s, rt_r, at_own(b))
-    for i in range(2):
-        gone(ra.at[i, pl.ds(0, AN - 1)], a1_s.at[i], a1_r.at[i], at_a(a))
-        gone(rb.at[i, pl.ds(0, BN - 1)], a2_s.at[i], a2_r.at[i], at_b(zz))
-        gone(full.at[i, pl.ds(0, AN - 1)], a3_s.at[i], a3_r.at[i], at_a(a))
-    gone(sa.at[pl.ds(0, AN - 1)], s1_s, s1_r, at_a(a))
-    gone(sb.at[pl.ds(0, BN - 1)], s2_s, s2_r, at_b(zz))
-    gone(sf.at[pl.ds(0, AN - 1)], s3_s, s3_r, at_a(a))
+        gone(sa.at[pl.ds(0, AN - 1)], s1_s, s1_r, at_a(a))
+        gone(sb.at[pl.ds(0, BN - 1)], s2_s, s2_r, at_b(zz))
+        gone(sf, s3_s, s3_r, partner())
+
+    @pl.when(core == 1)
+    def _():
+        gone(sg, s0_s, s0_r, partner())
 
 
 def copy_kernel(*refs):
@@ -682,35 +684,37 @@
             pltpu.VMEM((NS * BI, BJ), f32),
             pltpu.VMEM((NS * BI, BJ), f32),
             pltpu.VMEM((NS * BI, BJ), f32),
-            pltpu.VMEM((2, NV, 8, BJ), f32),
-            pltpu.VMEM((2, PL, 8, BJ), f32),
-            pltpu.VMEM((2, OWN, 8, BJ), f32),
-            pltpu.VMEM((2, ZN * NV, 8, BJ), f32),
-            pltpu.VMEM((NV, 8, BJ), f32),
+            pltpu.VMEM((2, PL, 8, ROW), f32),
+            pltpu.VMEM((2, ZN, 8, ROW), f32),
+            pltpu.VMEM((2, ZN, 8, ROW), f32),
+            pltpu.VMEM((8, ROW), f32),
             pltpu.VMEM((4, 8, BJ), f32),
-            pltpu.VMEM((OWN, 1, BJ), f32),
-            pltpu.VMEM((OWN * 8, PL * 8), bf16),
-            pltpu.VMEM((PL * 8, OWN * 8), bf16),
-            pltpu.VMEM((BJ, BJ), bf16),
-            pltpu.VMEM((2, NV, 8, BJ), f32),
-            pltpu.VMEM((NV, 8, BJ), f32),
-            pltpu.VMEM((OWN, 8, BJ), f32),
-            pltpu.VMEM((PL, 8, BJ), f32),
-            pltpu.VMEM((NV, 8, BJ), f32),
+            pltpu.VMEM((ZN, 8, BJ), f32),
+            pltpu.VMEM((ZN * 8, BJ), f32),
+            pltpu.VMEM((BJ, BJ), f32),
+            pltpu.VMEM((2, 8, ROW), f32),
+            pltpu.VMEM((ZN, 8, ROW), f32),
+            pltpu.VMEM((PL, 8, ROW), f32),
+            pltpu.VMEM((PL, 8, ROW), f32),
             pltpu.VMEM((HID + 16, HID), f32),
             pltpu.VMEM((HID + 16, HID), f32),
             pltpu.VMEM((NF + 16, HID), f32),
             pltpu.VMEM((HID, BJ), f32),
-            pltpu.VMEM((2, AN, 8, HID), f32),
-            pltpu.VMEM((2, BN, 8, HID), f32),
-            pltpu.VMEM((2, AN, 8, HID), f32),
-            pltpu.VMEM((AN, 1, HID), f32),
-            pltpu.VMEM((AN, 1, HID), f32),
-            pltpu.VMEM((BN, 1, HID), f32),
-            pltpu.VMEM((AN, 1, HID), f32),
-            dma((2,)), dma((2,)), dma, dma, dma((2,)), dma((2,)), dma, dma, dma, dma,
-            dma((2,)), dma((2,)), dma((2,)), dma((2,)), dma((2,)), dma((2,)),
-            dma, dma, dma, dma, dma, dma,
+            pltpu.VMEM((HID, HID), f32),
+            pltpu.VMEM((AN, HID // AN, HID), f32),
+            pltpu.VMEM((AN, HID // AN, HID), f32),
+            pltpu.VMEM((BN, HID // AN, HID), f32),
+            pltpu.VMEM((AN, HID // AN, HID), f32),
+            pltpu.VMEM((AN, HID // AN, HID), f32),
+            pltpu.VMEM((24, HID), f32),
+            pltpu.VMEM((24, HID), f32),
+            pltpu.VMEM((AN, 24, HID), f32),
+            pltpu.VMEM((BN, 24, HID), f32),
+            pltpu.VMEM((24, HID), f32),
+            pltpu.VMEM((24, HID), f32),
+            dma((2, PL)), dma((2, PL)), dma((ZN,)), dma((ZN,)), dma((2, ZN)), dma((2, ZN)),
+            dma((ZN,)), dma((ZN,)), dma((PL,)), dma((PL,)),
+            dma, dma, dma, dma, dma, dma, dma, dma, dma, dma, dma, dma, dma, dma, dma, dma, dma, dma,
         ],
         compiler_params=pltpu.CompilerParams(
             collective_id=0, has_side_effects=True, vmem_limit_bytes=56 * 2**20

time: 80.2 us -> 74.9 us (0.934)
  Pallas kernels: 78.8 us -> 73.5 us
    pallas_call x1, Pallas kernels: 76.7 us -> 71.4 us  [per_device(): pl.pallas_call(functools.partial(kernel, loss_scale), out_shape=(jax.Shap...]
where the time goes in v3:
time: 74.9 us; the launch traced here: 74.8 us
  Pallas kernels  73.5 us (98%)
  between operations  1.29 us (2%)
    pallas_call x1, Pallas kernels, per_device(): pl.pallas_call(functools.partial(kernel, loss_scale), out_shape=(jax.Shap...  71.4 us
    pallas_call x1, Pallas kernels, per_device(): pl.pallas_call(copy_kernel, out_shape=tuple((jax.ShapeDtypeStruct(x.shape...  2.07 us

profile of v3, /device:TPU:1, one launch (start us, length us, event | category | flops | bytes accessed | tf_op | source)
XLA Modules:
  0.0 74.8 jit_solution(9856855090683630354)
XLA Ops:
  1.3 71.4 %shard_map.164 = (f32[6,3,32,128]{3,2,1,0:T(8,128)}, f32[16,256]{1,0:T(8,128)}, f32[256,256]{1,0:T(8,128)}, f32[256,256]{1,0:T(8,128)}, f32[4,256]{1,0:T(4,128)}) custom-call(f32[6,3,32,128]{3,2,1,0:T(8,128)} %bitcast.8, f32[6,3,32,128]{3,2,1,0:T(8,128)} %bitcast.9, bf16[16,3,32,128]{3,2,1,0:T(8,128)(2,1)} %bitcast.7, f32[6,6]{1,0:T(8,128)} %coup.1, ...), custom_call_target="tpu_custom_call" | custom-call | tf_op jit(solution)/shard_map/pallas_call | solution.py:660
  72.7 2.1 %shard_map.165 = (f32[6,3,32,128]{3,2,1,0:T(8,128)}, f32[16,256]{1,0:T(8,128)}, f32[256,256]{1,0:T(8,128)}, f32[256,256]{1,0:T(8,128)}, f32[4,256]{1,0:T(4,128)}) custom-call(f32[6,3,32,128]{3,2,1,0:T(8,128)} %get-tuple-element.15.refs_0_, f32[16,256]{1,0:T(8,128)} %get-tuple-element.16.refs_1_, f32[256,256]{1,0:T(8,128)} %get-tuple-element.17.refs_2_, ...), custom_call_target="tpu_custom_call" | custom-call | tf_op jit(solution)/shard_map/pallas_call | solution.py:726

commit v4 on v3

--- a/solution.py
+++ b/solution.py
@@ -60,9 +60,9 @@
 
 def kernel(
     loss_scale,
-    state, target, feat, coup, in_w, mid_w, top_w, out_w, biases, count, conn, orient, rot,
+    state_h, target_h, feat_h, coup, in_w, mid_w, top_w, out_w, biases, count, conn, orient, rot,
     out_state, out_in, out_mid, out_top, out_vec,
-    x_r, first_r, second_r, third_r,
+    state, target, feat, x0, x1, first0, first1, second0, second1, third0, third1,
     xs, win_t, wmid_t, wtop_t, bias_c, ow_c,
     mid_r, ts_r, tm_r, fc_r, beta_r, betan_r, bc_r, bcn_r,
     plane, zout, zin, inner, tile_r, meta, sel_r, selt_r, ghost_r,
@@ -70,8 +70,9 @@
     gtop, gmid, gin, gout,
     cg, gsum, ra, rb, full, other, sg, sc, sa, sb, sf, st,
     pl_s, pl_r, me_s, me_r, zz_s, zz_r, cz_s, cz_r, rt_s, rt_r,
-    c_s, c_r, a1_s, a1_r, a2_s, a2_r, a3_s, a3_r, f_s, f_r, s0_s, s0_r, s1_s, s1_r, s2_s, s2_r, s3_s, s3_r,
+    in_s, c_s, c_r, a1_s, a1_r, a2_s, a2_r, a3_s, a3_r, f_s, f_r, s0_s, s0_r, s1_s, s1_r, s2_s, s2_r, s3_s, s3_r,
 ):
+    x_r, first_r, second_r, third_r = (x0, x1), (first0, first1), (second0, second1), (third0, third1)
     b = lax.axis_index("blk")
     o = lax.axis_index("op")
     z = lax.div(b, PL)
@@ -126,6 +127,10 @@
         greet(at_a(lax.rem(x_at * 4 + d, AN)))
     for d in range(1, BN):
         greet(at_b(lax.rem(zz + d, BN)))
+
+    loads = [pltpu.make_async_copy(h, v, in_s.at[i]) for i, (h, v) in enumerate(((state_h, state), (feat_h, feat), (target_h, target)))]
+    for load in loads:
+        load.start()
 
     rowi = lax.broadcasted_iota(jnp.int32, (8, BJ), 0)
     lane8 = lax.broadcasted_iota(jnp.int32, (8, BJ), 1)
@@ -163,25 +168,9 @@
     def cut(ref):
         return [ref[:, v * BJ:(v + 1) * BJ] for v in range(NV)]
 
+    loads[0].wait()
     mine = plane.at[0, p]
     pack(mine, state, (0, BI - 1))
-
-    pad = jnp.zeros((BJ - NF, HID), f32)
-    win_t[...] = jnp.concatenate([in_w[...].astype(f32), pad], axis=0).T[:, :NF].astype(bf16)
-    wmid_t[...] = mid_w[...].astype(f32).T.astype(bf16)
-    wtop_t[...] = top_w[...].astype(f32).T.astype(bf16)
-    for k in range(3):
-        bias_c[k] = jnp.broadcast_to(biases[k:k + 1, :], (BJ, HID)).T
-    ow_c[...] = jnp.broadcast_to(out_w[...].astype(f32).reshape(1, HID), (BJ, HID)).T
-
-    for s in range(NS):
-        for h in range(2):
-            xs[s, h] = feat[:, s, 16 * h:16 * h + 16, :].astype(f32).reshape(NF * 16, BJ)
-    for s in range(NS):
-        for h in range(2):
-            for r in range(16):
-                row = row_of(s, 16 * h + r)
-                x_r[row // 8, :, (row % 8) * BJ:(row % 8 + 1) * BJ] = xs[s, h, pl.ds(r, NF, stride=16), :].astype(bf16)
 
     pl.semaphore_wait(barrier, PL - 1 + AN - 4 + BN - 1)
 
@@ -245,6 +234,24 @@
             res.append(e[v] + tau * (lap - coupled + beta_e * jnp.tanh(e[v])))
         return res
 
+    pad = jnp.zeros((BJ - NF, HID), f32)
+    win_t[...] = jnp.concatenate([in_w[...].astype(f32), pad], axis=0).T[:, :NF].astype(bf16)
+    wmid_t[...] = mid_w[...].astype(f32).T.astype(bf16)
+    wtop_t[...] = top_w[...].astype(f32).T.astype(bf16)
+    for k in range(3):
+        bias_c[k] = jnp.broadcast_to(biases[k:k + 1, :], (BJ, HID)).T
+    ow_c[...] = jnp.broadcast_to(out_w[...].astype(f32).reshape(1, HID), (BJ, HID)).T
+
+    loads[1].wait()
+    for s in range(NS):
+        for h in range(2):
+            xs[s, h] = feat[:, s, 16 * h:16 * h + 16, :].astype(f32).reshape(NF * 16, BJ)
+    for s in range(NS):
+        for h in range(2):
+            for r in range(16):
+                row = row_of(s, 16 * h + r)
+                x_r[row // 8 % 2][row // 16, :, (row % 8) * BJ:(row % 8 + 1) * BJ] = xs[s, h, pl.ds(r, NF, stride=16), :].astype(bf16)
+
     SUB = 256
 
     weights = (win_t, wmid_t, wtop_t)
@@ -252,23 +259,24 @@
     SUBS = 2 * CW // SUB
 
     def forward(k, carry):
-        pair = (lax.rem(2 * k + EDGE, NCH), 2 * k)
+        pair = (lax.rem(k + EDGE // 2, NCH // 2), k)
 
         def place(j):
-            return pair[j // (CW // SUB)], slice((j % (CW // SUB)) * SUB, (j % (CW // SUB) + 1) * SUB)
+            half = j // (CW // SUB)
+            return 1 - half, pair[half], slice((j % (CW // SUB)) * SUB, (j % (CW // SUB) + 1) * SUB)
 
         def product(layer, j):
-            c, cols = place(j)
-            return mm(weights[layer][...], acts[layer][c, :, cols])
+            par, c, cols = place(j)
+            return mm(weights[layer][...], acts[layer][par][c, :, cols])
 
         tiles = [jnp.zeros((8, BJ), f32), jnp.zeros((8, BJ), f32)]
 
         def activate(layer, j, d):
-            c, cols = place(j)
+            par, c, cols = place(j)
             bias = bias_c[layer]
             for i in range(SUB // BJ):
                 t = jnp.tanh(d[:, i * BJ:(i + 1) * BJ] + bias).astype(bf16)
-                acts[layer + 1][c, :, cols.start + i * BJ:cols.start + (i + 1) * BJ] = t
+                acts[layer + 1][par][c, :, cols.start + i * BJ:cols.start + (i + 1) * BJ] = t
                 if layer == 2:
                     bt = jnp.sum(ow_c[...] * t.astype(f32), axis=0, keepdims=True) + 1.0
                     row = (j % (CW // SUB)) * (SUB // BJ) + i
@@ -284,7 +292,7 @@
             held = task + (d,)
         activate(*held)
         for half in range(2):
-            beta_r[pl.ds(pl.multiple_of(pair[half] * 8, 8), 8), :] = tiles[half]
+            beta_r[pl.ds(pl.multiple_of((2 * pair[half] + 1 - half) * 8, 8), 8), :] = tiles[half]
 
         @pl.when(k == 0)
         def _():
@@ -343,6 +351,7 @@
     ghosts(1)
     pack(inner, mid_r, (1, BI - 2))
     final_e = edge_sweep(cut(plane.at[1, p]), cut(inner), cut(ghost_r.at[1]))
+    loads[2].wait()
     pack(inner, target, (0, BI - 1))
     goal_e = cut(inner)
     cot_e = [tau * (loss_scale * tile_r[3] * (final_e[v] - goal_e[v])) for v in range(NV)]
@@ -415,19 +424,20 @@
     gmid[...] = jnp.zeros((HID + 16, HID), f32)
     gin[...] = jnp.zeros((NF + 16, HID), f32)
 
-    def weigh(c, acc, left, right, fresh=None):
-        part = nt(jnp.concatenate([left[c], ones], axis=0), right[c])
+    def weigh(par, k, acc, left, right, fresh=None):
+        part = nt(jnp.concatenate([left[par][k], ones], axis=0), right[par][k])
         if fresh is not None:
             part = jnp.where(fresh, part, 0.0)
         acc[...] = acc[...] + part
 
-    def before(k, half):
-        return lax.rem(2 * k + half + NCH - 2, NCH)
+    def before(k):
+        return lax.rem(k + NCH // 2 - 1, NCH // 2)
 
     RB = 64
 
-    def top_delta(c):
-        bc = bc_r[pl.ds(pl.multiple_of(c * 8, 8), 8), :]
+    def top_delta(par, k):
+        third = third_r[par]
+        bc = bc_r[pl.ds(pl.multiple_of((2 * k + par) * 8, 8), 8), :]
         ch = bc.astype(bf16).astype(f32)
         for i in range(HID // RB):
             rows = slice(i * RB, (i + 1) * RB)
@@ -435,38 +445,42 @@
             acc = gout[rows]
             for j in range(CW // BJ):
                 cols = slice(j * BJ, (j + 1) * BJ)
-                t = third_r[c, rows, cols].astype(f32)
+                t = third[k, rows, cols].astype(f32)
                 acc = acc + t * ch[j:j + 1]
-                third_r[c, rows, cols] = (ow * bc[j:j + 1] * (1.0 - t * t)).astype(bf16)
+                third[k, rows, cols] = (ow * bc[j:j + 1] * (1.0 - t * t)).astype(bf16)
             gout[rows] = acc
 
     def back_top(k, carry):
-        for half in range(2):
-            weigh(before(k, half), gtop, second_r, third_r, k > 0)
-            top_delta(2 * k + half)
+        weigh(1, before(k), gtop, second_r, third_r, k > 0)
+        top_delta(0, k)
+        weigh(0, k, gtop, second_r, third_r)
+        top_delta(1, k)
         return carry
 
     def layer_back(k, weight, source, act, acc, left, fresh=None):
         held = None
 
-        def put(c, cols, d):
+        def put(par, cols, d):
             for i in range(SUB // BJ):
                 here = slice(cols.start + i * BJ, cols.start + (i + 1) * BJ)
-                t = act[c, :, here].astype(f32)
-                act[c, :, here] = (d[:, i * BJ:(i + 1) * BJ] * (1.0 - t * t)).astype(bf16)
-
-        for half in range(2):
-            c = 2 * k + half
+                t = act[par][k, :, here].astype(f32)
+                act[par][k, :, here] = (d[:, i * BJ:(i + 1) * BJ] * (1.0 - t * t)).astype(bf16)
+
+        for par in range(2):
             for j in range(CW // SUB):
                 cols = slice(j * SUB, (j + 1) * SUB)
-                d = mm(weight[...], source[c, :, cols])
+                d = mm(weight[...], source[par][k, :, cols])
                 if held is not None:
                     put(*held)
-                held = (c, cols, d)
-            if half == 0:
-                weigh(before(k, 0), acc, left, act, fresh)
+                held = (par, cols, d)
+                if j == 0:
+                    if par == 0:
+                        weigh(1, before(k), acc, left, act, fresh)
+                    else:
+                        put(*held)
+                        held = None
+                        weigh(0, k, acc, left, act)
         put(*held)
-        weigh(before(k, 1), acc, left, act, fresh)
 
     def back_mid(k, carry):
         layer_back(k, top_w, third_r, second_r, gmid, first_r, k > 0)
@@ -552,19 +566,17 @@
 
     LAST = NCH // 2 - 1
     lax.fori_loop(0, LAST, back_top, 0)
-    weigh(EDGE - 3, gtop, second_r, third_r)
-    weigh(EDGE - 2, gtop, second_r, third_r)
+    weigh(1, LAST - 1, gtop, second_r, third_r)
     table()
+    top_delta(0, LAST)
+    weigh(0, LAST, gtop, second_r, third_r)
     lax.fori_loop(0, LAST, back_mid, 0)
-    top_delta(EDGE - 1)
-    weigh(EDGE - 1, gtop, second_r, third_r)
     returned()
-    top_delta(EDGE)
-    weigh(EDGE, gtop, second_r, third_r)
+    top_delta(1, LAST)
+    weigh(1, LAST, gtop, second_r, third_r)
     hand(0)
     layer_back(LAST, top_w, third_r, second_r, gmid, first_r)
-    weigh(EDGE - 1, gmid, first_r, second_r)
-    weigh(EDGE, gmid, first_r, second_r)
+    weigh(1, LAST, gmid, first_r, second_r)
     hand(1)
 
     @pl.when(core == 0)
@@ -585,8 +597,7 @@
         return carry
 
     lax.fori_loop(0, LAST + 1, back_first, 0)
-    weigh(EDGE - 1, gin, x_r, first_r)
-    weigh(EDGE, gin, x_r, first_r)
+    weigh(1, LAST, gin, x_r, first_r)
 
     small_0()
 
@@ -655,6 +666,7 @@
     loss_scale = 2.0 / math.sqrt(cells)
     vmem = pl.BlockSpec(memory_space=pltpu.VMEM)
     smem = pl.BlockSpec(memory_space=pltpu.SMEM)
+    anywhere = pl.BlockSpec(memory_space=pl.ANY)
     dma = pltpu.SemaphoreType.DMA
     field = pltpu.VMEM((NV, NS, BI, BJ), f32)
     outs = pl.pallas_call(
@@ -666,13 +678,18 @@
             jax.ShapeDtypeStruct((HID, HID), f32),
             jax.ShapeDtypeStruct((4, HID), f32),
         ),
-        in_specs=[vmem, vmem, vmem, smem, vmem, vmem, vmem, vmem, vmem, smem, smem, smem, smem],
+        in_specs=[anywhere, anywhere, anywhere, smem, vmem, vmem, vmem, vmem, vmem, smem, smem, smem, smem],
         out_specs=(vmem,) * 5,
         scratch_shapes=[
-            pltpu.VMEM((NCH, NF, CW), bf16),
-            pltpu.VMEM((NCH, HID, CW), bf16),
-            pltpu.VMEM((NCH, HID, CW), bf16),
-            pltpu.VMEM((NCH, HID, CW), bf16),
+            field, field, pltpu.VMEM((NF, NS, BI, BJ), bf16),
+            pltpu.VMEM((NCH // 2, NF, CW), bf16),
+            pltpu.VMEM((NCH // 2, NF, CW), bf16),
+            pltpu.VMEM((NCH // 2, HID, CW), bf16),
+            pltpu.VMEM((NCH // 2, HID, CW), bf16),
+            pltpu.VMEM((NCH // 2, HID, CW), bf16),
+            pltpu.VMEM((NCH // 2, HID, CW), bf16),
+            pltpu.VMEM((NCH // 2, HID, CW), bf16),
+            pltpu.VMEM((NCH // 2, HID, CW), bf16),
             pltpu.VMEM((NS, 2, NF * 16, BJ), f32),
             pltpu.VMEM((HID, NF), bf16),
             pltpu.VMEM((HID, HID), bf16),
@@ -714,7 +731,7 @@
             pltpu.VMEM((24, HID), f32),
             dma((2, PL)), dma((2, PL)), dma((ZN,)), dma((ZN,)), dma((2, ZN)), dma((2, ZN)),
             dma((ZN,)), dma((ZN,)), dma((PL,)), dma((PL,)),
-            dma, dma, dma, dma, dma, dma, dma, dma, dma, dma, dma, dma, dma, dma, dma, dma, dma, dma,
+            dma((3,)), dma, dma, dma, dma, dma, dma, dma, dma, dma, dma, dma, dma, dma, dma, dma, dma, dma, dma,
         ],
         compiler_params=pltpu.CompilerParams(
             collective_id=0, has_side_effects=True, vmem_limit_bytes=56 * 2**20

time: 74.9 us -> 71.5 us (0.955)
  Pallas kernels: 73.5 us -> 70.1 us
    pallas_call x1, Pallas kernels: 71.4 us -> 68 us  [per_device(): pl.pallas_call(functools.partial(kernel, loss_scale), out_shape=(jax.Shap...]
where the time goes in v4:
time: 71.5 us; the launch traced here: 71.4 us
  Pallas kernels  70.1 us (98%)
  between operations  1.29 us (2%)
    pallas_call x1, Pallas kernels, per_device(): pl.pallas_call(functools.partial(kernel, loss_scale), out_shape=(jax.Shap...  68 us
    pallas_call x1, Pallas kernels, per_device(): pl.pallas_call(copy_kernel, out_shape=tuple((jax.ShapeDtypeStruct(x.shape...  2.07 us

profile of v4, /device:TPU:1, one launch (start us, length us, event | category | flops | bytes accessed | tf_op | source)
XLA Modules:
  0.0 71.4 jit_solution(14343706044883729517)
XLA Ops:
  1.3 68.0 %shard_map.164 = (f32[6,3,32,128]{3,2,1,0:T(8,128)}, f32[16,256]{1,0:T(8,128)}, f32[256,256]{1,0:T(8,128)}, f32[256,256]{1,0:T(8,128)}, f32[4,256]{1,0:T(4,128)}) custom-call(f32[6,3,32,128]{3,2,1,0:T(8,128)} %bitcast.8, f32[6,3,32,128]{3,2,1,0:T(8,128)} %bitcast.9, bf16[16,3,32,128]{3,2,1,0:T(8,128)(2,1)} %bitcast.7, f32[6,6]{1,0:T(8,128)} %coup.1, ...), custom_call_target="tpu_custom_call" | custom-call | tf_op jit(solution)/shard_map/pallas_call | solution.py:672
  69.3 2.1 %shard_map.165 = (f32[6,3,32,128]{3,2,1,0:T(8,128)}, f32[16,256]{1,0:T(8,128)}, f32[256,256]{1,0:T(8,128)}, f32[256,256]{1,0:T(8,128)}, f32[4,256]{1,0:T(4,128)}) custom-call(f32[6,3,32,128]{3,2,1,0:T(8,128)} %get-tuple-element.15.refs_0_, f32[16,256]{1,0:T(8,128)} %get-tuple-element.16.refs_1_, f32[256,256]{1,0:T(8,128)} %get-tuple-element.17.refs_2_, ...), custom_call_target="tpu_custom_call" | custom-call | tf_op jit(solution)/shard_map/pallas_call | solution.py:743

commit v5 on v4

--- a/solution.py
+++ b/solution.py
@@ -13,7 +13,6 @@
 passage_angle = 2.0 * math.pi / 36.0
 cos_step = math.cos(passage_angle)
 sin_step = math.sin(passage_angle)
-highest = lax.Precision.HIGHEST
 f32 = jnp.float32
 bf16 = jnp.bfloat16
 
@@ -25,7 +24,8 @@
 EDGE = NCH - 1
 AN = 16
 BN = 8
-ROW = NV * BJ
+HV = NV // 2
+HALF = HV * BJ
 
 
 def row_of(s, i):
@@ -65,8 +65,8 @@
     state, target, feat, x0, x1, first0, first1, second0, second1, third0, third1,
     xs, win_t, wmid_t, wtop_t, bias_c, ow_c,
     mid_r, ts_r, tm_r, fc_r, beta_r, betan_r, bc_r, bcn_r,
-    plane, zout, zin, inner, tile_r, meta, sel_r, selt_r, ghost_r,
-    cz, tbl, ret,
+    edge, gath, picked, arr, inner, tile_r, meta, sel_r, selt_r, ghost_r,
+    cote, cz, tbl, ret,
     gtop, gmid, gin, gout,
     cg, gsum, ra, rb, full, other, sg, sc, sa, sb, sf, st,
     pl_s, pl_r, me_s, me_r, zz_s, zz_r, cz_s, cz_r, rt_s, rt_r,
@@ -79,18 +79,19 @@
     p = lax.rem(b, PL)
 
     plane_peers = [lax.rem(p + d, PL) for d in range(1, PL)]
-    z_peers = [lax.rem(z + d, ZN) for d in range(1, ZN)]
     x_at = lax.div(o, 2)
     z_lo = lax.rem(o, 2)
     core = lax.rem(b, 2)
+    mine = z * 2 + core
+    tower = [lax.rem(mine + d, 2 * ZN) for d in range(1, 2 * ZN)]
     a = x_at * ZN + lax.div(p, 2)
     zz = z * 2 + z_lo
 
     def at_plane(q):
         return {"blk": z * PL + q}
 
-    def at_z(w):
-        return {"blk": w * PL + p}
+    def at_tower(w):
+        return {"blk": lax.div(w, 2) * PL + p - core + lax.rem(w, 2)}
 
     def at_a(q):
         return {"blk": z * PL + lax.rem(q, 4) * 2 + core, "op": lax.div(q, 4) * 2 + z_lo}
@@ -127,6 +128,8 @@
         greet(at_a(lax.rem(x_at * 4 + d, AN)))
     for d in range(1, BN):
         greet(at_b(lax.rem(zz + d, BN)))
+    for d in range(1, ZN):
+        greet(at_tower(lax.rem(mine + 2 * d, 2 * ZN) + 1 - 2 * core))
 
     loads = [pltpu.make_async_copy(h, v, in_s.at[i]) for i, (h, v) in enumerate(((state_h, state), (feat_h, feat), (target_h, target)))]
     for load in loads:
@@ -152,76 +155,90 @@
             cos_t = jnp.where(here, jnp.where(turn == 0, 1.0, cos_step).astype(f32), cos_t)
             sin_t = jnp.where(here, turn.astype(f32) * sin_step, sin_t)
             live_t = jnp.where(here, live[s], live_t)
-    meta[z] = meta_t
+    meta[mine] = meta_t
     tile_r[0] = flip_t
     tile_r[1] = cos_t
     tile_r[2] = sin_t
     tile_r[3] = live_t
 
+    def part(ref, v):
+        return ref.at[v // HV, :, v % HV * BJ:(v % HV + 1) * BJ]
+
     def pack(dst, field, rows):
-        dst[...] = jnp.zeros((8, ROW), f32)
+        dst[...] = jnp.zeros((2, 8, HALF), f32)
         for v in range(NV):
             for s in range(NS):
                 for e in range(2):
-                    dst[2 * s + e:2 * s + e + 1, v * BJ:(v + 1) * BJ] = field[v, s, rows[e]:rows[e] + 1, :]
+                    part(dst, v)[2 * s + e:2 * s + e + 1, :] = field[v, s, rows[e]:rows[e] + 1, :]
 
     def cut(ref):
-        return [ref[:, v * BJ:(v + 1) * BJ] for v in range(NV)]
+        return [part(ref, v)[...] for v in range(NV)]
+
+    def thirds(u):
+        u1 = u.astype(bf16)
+        u2 = (u - u1.astype(f32)).astype(bf16)
+        u3 = (u - u1.astype(f32) - u2.astype(f32)).astype(bf16)
+        return u1, u2, u3
+
+    def by_rows(mask, u):
+        r = mm(mask, jnp.concatenate(thirds(u), axis=1))
+        return r[:, :HALF] + r[:, HALF:2 * HALF] + r[:, 2 * HALF:]
 
     loads[0].wait()
-    mine = plane.at[0, p]
-    pack(mine, state, (0, BI - 1))
-
-    pl.semaphore_wait(barrier, PL - 1 + AN - 4 + BN - 1)
+    pack(edge.at[0], state, (0, BI - 1))
+
+    pl.semaphore_wait(barrier, PL - 1 + AN - 4 + BN - 1 + ZN - 1)
 
     def send_plane(k):
         for q in plane_peers:
-            send(plane.at[k, p], plane.at[k, p], pl_s.at[k, q], pl_r.at[k, p], at_plane(q))
-
-    for w in z_peers:
-        send(meta.at[z], meta.at[z], me_s.at[w], me_r.at[z], at_z(w))
+            send(edge.at[k, lax.rem(q, 2)], gath.at[k, p], pl_s.at[k, q], pl_r.at[k, p], at_plane(q))
+        gath[k, p] = edge[k, core]
+
+    for w in tower:
+        send(meta.at[mine], meta.at[mine], me_s.at[w], me_r.at[mine], at_tower(w))
     send_plane(0)
 
     def pick(k):
         for q in plane_peers:
-            got(plane.at[k, q], pl_s.at[k, q], pl_r.at[k, q], at_plane(q))
-        every = plane[k].reshape(PL * 8, ROW)
-        chosen = jnp.dot(sel_r[:, :PL * 8], every, preferred_element_type=f32, precision=highest)
-        for w in range(ZN):
-            zout[k, w] = chosen[8 * w:8 * w + 8]
-        zin[k, z] = zout[k, z]
-        for w in z_peers:
-            send(zout.at[k, w], zin.at[k, z], zz_s.at[k, w], zz_r.at[k, z], at_z(w))
+            got(gath.at[k, q], pl_s.at[k, q], pl_r.at[k, q], at_plane(q))
+        chosen = by_rows(sel_r[...], gath[k].reshape(PL * 8, HALF))
+        picked[k] = chosen.reshape(2 * ZN, 8, HALF)
+        arr[k, mine] = picked[k, mine]
+        for w in tower:
+            send(picked.at[k, w], arr.at[k, mine], zz_s.at[k, w], zz_r.at[k, mine], at_tower(w))
 
     def make_sel():
-        for w in z_peers:
-            got(meta.at[w], me_s.at[w], me_r.at[w], at_z(w))
-        lane = lax.broadcasted_iota(jnp.int32, (ZN * 8, BJ), 1)
-        named = meta[...].reshape(ZN * 8, BJ)
+        for w in tower:
+            got(meta.at[w], me_s.at[w], me_r.at[w], at_tower(w))
+        n = 2 * ZN * 8
+        lane = lax.broadcasted_iota(jnp.int32, (n, BJ), 1)
+        named = meta[...].reshape(n, BJ)
         local = named - (z * (PL * 8)).astype(f32)
         sel = jnp.where((local == lane.astype(f32)) & (lane < PL * 8), 1.0, 0.0).astype(f32)
-        sel_r[...] = sel
-        selt_r[...] = jnp.concatenate([sel, jnp.zeros((BJ - ZN * 8, BJ), f32)], axis=0).T
+        sel_r[...] = sel[:, :PL * 8].astype(bf16)
+        wide = jnp.concatenate([sel, jnp.zeros((BJ - n, BJ), f32)], axis=0).T
+        selt_r[...] = wide[:PL * 8, :n].astype(bf16)
 
     def turned(parts, sign):
         flip, cos, sin = tile_r[0], tile_r[1], tile_r[2] * sign
-        whole = jnp.concatenate(parts, axis=0)
         r = lax.broadcasted_iota(jnp.int32, (BJ, BJ), 0)
         c = lax.broadcasted_iota(jnp.int32, (BJ, BJ), 1)
-        anti = jnp.where(r + c == BJ - 1, 1.0, 0.0).astype(f32)
-        back = jnp.dot(whole, anti, preferred_element_type=f32, precision=highest)
+        anti = jnp.where(r + c == BJ - 1, 1.0, 0.0).astype(bf16)
+        n = 8 * NV
+        back = mm(jnp.concatenate(thirds(jnp.concatenate(parts, axis=0)), axis=0), anti)
+        back = back[:n] + back[n:2 * n] + back[2 * n:]
         out = [jnp.where(flip > 0.5, back[8 * v:8 * v + 8], parts[v]) for v in range(NV)]
         c2 = cos * out[2] - sin * out[3]
         c3 = sin * out[2] + cos * out[3]
         return [out[0], out[1], c2, c3, out[4], out[5]]
 
     def ghosts(k):
-        for w in z_peers:
-            got(zin.at[k, w], zz_s.at[k, w], zz_r.at[k, w], at_z(w))
-        total = (zin[k, 0] + zin[k, 1]) + (zin[k, 2] + zin[k, 3])
-        parts = turned([total[:, v * BJ:(v + 1) * BJ] for v in range(NV)], 1.0)
+        for w in tower:
+            got(arr.at[k, w], zz_s.at[k, w], zz_r.at[k, w], at_tower(w))
+        total = [(arr[k, h] + arr[k, 2 + h]) + (arr[k, 4 + h] + arr[k, 6 + h]) for h in range(2)]
+        parts = turned([total[v // HV][:, v % HV * BJ:(v % HV + 1) * BJ] for v in range(NV)], 1.0)
         for v in range(NV):
-            ghost_r[k, :, v * BJ:(v + 1) * BJ] = parts[v]
+            ghost_r[k, v] = parts[v]
 
     def edge_sweep(e, n, gh):
         res = []
@@ -303,9 +320,9 @@
         def _():
             ghosts(0)
             pack(inner, state, (1, BI - 2))
-            res = edge_sweep(cut(plane.at[0, p]), cut(inner), cut(ghost_r.at[0]))
+            res = edge_sweep(cut(edge.at[0]), cut(inner), [ghost_r[0, v] for v in range(NV)])
             for v in range(NV):
-                plane[1, p, :, v * BJ:(v + 1) * BJ] = res[v]
+                part(edge.at[1], v)[...] = res[v]
             send_plane(1)
 
         @pl.when(k == 4)
@@ -333,8 +350,7 @@
         return up + down + lanes_sum(u, lane32) - 4.0 * u
 
     def low_high(k, s, v):
-        cols = slice(v * BJ, (v + 1) * BJ)
-        return ghost_r[k, 2 * s:2 * s + 1, cols], ghost_r[k, 2 * s + 1:2 * s + 2, cols]
+        return ghost_r[k, v, 2 * s:2 * s + 1, :], ghost_r[k, v, 2 * s + 1:2 * s + 2, :]
 
     for s in range(NS):
         us = [state[v, s] for v in range(NV)]
@@ -350,16 +366,17 @@
 
     ghosts(1)
     pack(inner, mid_r, (1, BI - 2))
-    final_e = edge_sweep(cut(plane.at[1, p]), cut(inner), cut(ghost_r.at[1]))
+    final_e = edge_sweep(cut(edge.at[1]), cut(inner), [ghost_r[1, v] for v in range(NV)])
     loads[2].wait()
     pack(inner, target, (0, BI - 1))
     goal_e = cut(inner)
     cot_e = [tau * (loss_scale * tile_r[3] * (final_e[v] - goal_e[v])) for v in range(NV)]
     cot_e = turned(cot_e, -1.0)
     for v in range(NV):
-        cz[z, :, v * BJ:(v + 1) * BJ] = cot_e[v]
-    for w in z_peers:
-        send(cz.at[z], cz.at[z], cz_s.at[w], cz_r.at[z], at_z(w))
+        part(cote, v)[...] = cot_e[v]
+    cz[mine] = cote[core]
+    for w in tower:
+        send(cote.at[lax.rem(w, 2)], cz.at[mine], cz_s.at[w], cz_r.at[mine], at_tower(w))
 
     for s in range(NS):
         us = [mid_r[v, s] for v in range(NV)]
@@ -391,12 +408,10 @@
             bc_r[place:place + length, :] = bcn_r[s * BI + first:s * BI + first + length, :]
 
     def table():
-        for w in z_peers:
-            got(cz.at[w], cz_s.at[w], cz_r.at[w], at_z(w))
-        cots = cz[...].reshape(ZN * 8, ROW)
-        sums = jnp.dot(selt_r[:PL * 8, :ZN * 8], cots, preferred_element_type=f32, precision=highest)
-        for q in range(PL):
-            tbl[q] = sums[8 * q:8 * q + 8]
+        for w in tower:
+            got(cz.at[w], cz_s.at[w], cz_r.at[w], at_tower(w))
+        sums = by_rows(selt_r[...], cz[...].reshape(2 * ZN * 8, HALF))
+        tbl[...] = sums.reshape(PL, 8, HALF)
         ret[p] = tbl[p]
         for q in plane_peers:
             send(tbl.at[q], ret.at[p], rt_s.at[q], rt_r.at[p], at_plane(q))
@@ -404,14 +419,12 @@
     def returned():
         for q in plane_peers:
             got(ret.at[q], rt_s.at[q], rt_r.at[q], at_plane(q))
-        total = ret[0]
-        for q in range(1, PL):
-            total = total + ret[q]
-        start = plane[0, p]
         extra = jnp.zeros((8, BJ), f32)
-        for v in range(NV):
-            cols = slice(v * BJ, (v + 1) * BJ)
-            extra = extra + total[:, cols] * jnp.tanh(start[:, cols])
+        for h in range(2):
+            total = (ret[h] + ret[2 + h]) + (ret[4 + h] + ret[6 + h])
+            for v in range(HV):
+                cols = slice(v * BJ, (v + 1) * BJ)
+                extra = extra + total[:, cols] * jnp.tanh(edge[0, h, :, cols])
         for s in range(NS):
             for e in range(2):
                 g = 2 * s + e
@@ -624,12 +637,12 @@
 
     for k in range(2):
         for q in plane_peers:
-            gone(plane.at[k, p], pl_s.at[k, q], pl_r.at[k, p], at_plane(q))
-        for w in z_peers:
-            gone(zout.at[k, w], zz_s.at[k, w], zz_r.at[k, z], at_z(w))
-    for w in z_peers:
-        gone(meta.at[z], me_s.at[w], me_r.at[z], at_z(w))
-        gone(cz.at[z], cz_s.at[w], cz_r.at[z], at_z(w))
+            gone(edge.at[k, core], pl_s.at[k, q], pl_r.at[k, p], at_plane(q))
+        for w in tower:
+            gone(picked.at[k, w], zz_s.at[k, w], zz_r.at[k, mine], at_tower(w))
+    for w in tower:
+        gone(meta.at[mine], me_s.at[w], me_r.at[mine], at_tower(w))
+        gone(cote.at[core], cz_s.at[w], cz_r.at[mine], at_tower(w))
     for q in plane_peers:
         gone(tbl.at[q], rt_s.at[q], rt_r.at[p], at_plane(q))
     gone(cg, c_s, c_r, partner())
@@ -701,18 +714,20 @@
             pltpu.VMEM((NS * BI, BJ), f32),
             pltpu.VMEM((NS * BI, BJ), f32),
             pltpu.VMEM((NS * BI, BJ), f32),
-            pltpu.VMEM((2, PL, 8, ROW), f32),
-            pltpu.VMEM((2, ZN, 8, ROW), f32),
-            pltpu.VMEM((2, ZN, 8, ROW), f32),
-            pltpu.VMEM((8, ROW), f32),
+            pltpu.VMEM((2, 2, 8, HALF), f32),
+            pltpu.VMEM((2, PL, 8, HALF), f32),
+            pltpu.VMEM((2, 2 * ZN, 8, HALF), f32),
+            pltpu.VMEM((2, 2 * ZN, 8, HALF), f32),
+            pltpu.VMEM((2, 8, HALF), f32),
             pltpu.VMEM((4, 8, BJ), f32),
-            pltpu.VMEM((ZN, 8, BJ), f32),
-            pltpu.VMEM((ZN * 8, BJ), f32),
-            pltpu.VMEM((BJ, BJ), f32),
-            pltpu.VMEM((2, 8, ROW), f32),
-            pltpu.VMEM((ZN, 8, ROW), f32),
-            pltpu.VMEM((PL, 8, ROW), f32),
-            pltpu.VMEM((PL, 8, ROW), f32),
+            pltpu.VMEM((2 * ZN, 8, BJ), f32),
+            pltpu.VMEM((2 * ZN * 8, PL * 8), bf16),
+            pltpu.VMEM((PL * 8, 2 * ZN * 8), bf16),
+            pltpu.VMEM((2, NV, 8, BJ), f32),
+            pltpu.VMEM((2, 8, HALF), f32),
+            pltpu.VMEM((2 * ZN, 8, HALF), f32),
+            pltpu.VMEM((PL, 8, HALF), f32),
+            pltpu.VMEM((PL, 8, HALF), f32),
             pltpu.VMEM((HID + 16, HID), f32),
             pltpu.VMEM((HID + 16, HID), f32),
             pltpu.VMEM((NF + 16, HID), f32),
@@ -729,8 +744,8 @@
             pltpu.VMEM((BN, 24, HID), f32),
             pltpu.VMEM((24, HID), f32),
             pltpu.VMEM((24, HID), f32),
-            dma((2, PL)), dma((2, PL)), dma((ZN,)), dma((ZN,)), dma((2, ZN)), dma((2, ZN)),
-            dma((ZN,)), dma((ZN,)), dma((PL,)), dma((PL,)),
+            dma((2, PL)), dma((2, PL)), dma((2 * ZN,)), dma((2 * ZN,)), dma((2, 2 * ZN)), dma((2, 2 * ZN)),
+            dma((2 * ZN,)), dma((2 * ZN,)), dma((PL,)), dma((PL,)),
             dma((3,)), dma, dma, dma, dma, dma, dma, dma, dma, dma, dma, dma, dma, dma, dma, dma, dma, dma, dma,
         ],
         compiler_params=pltpu.CompilerParams(

time: 71.5 us -> 71.1 us (level)
  no operation moved by 1% of the time
where the time goes in v5:
time: 71.1 us; the launch traced here: 71 us
  Pallas kernels  69.7 us (98%)
  between operations  1.29 us (2%)
    pallas_call x1, Pallas kernels, per_device(): pl.pallas_call(functools.partial(kernel, loss_scale), out_shape=(jax.Shap...  67.6 us
    pallas_call x1, Pallas kernels, per_device(): pl.pallas_call(copy_kernel, out_shape=tuple((jax.ShapeDtypeStruct(x.shape...  2.07 us

profile of v5, /device:TPU:1, one launch (start us, length us, event | category | flops | bytes accessed | tf_op | source)
XLA Modules:
  0.0 71.0 jit_solution(5666759384978352304)
XLA Ops:
  1.3 67.6 %shard_map.164 = (f32[6,3,32,128]{3,2,1,0:T(8,128)}, f32[16,256]{1,0:T(8,128)}, f32[256,256]{1,0:T(8,128)}, f32[256,256]{1,0:T(8,128)}, f32[4,256]{1,0:T(4,128)}) custom-call(f32[6,3,32,128]{3,2,1,0:T(8,128)} %bitcast.8, f32[6,3,32,128]{3,2,1,0:T(8,128)} %bitcast.9, bf16[16,3,32,128]{3,2,1,0:T(8,128)(2,1)} %bitcast.7, f32[6,6]{1,0:T(8,128)} %coup.1, ...), custom_call_target="tpu_custom_call" | custom-call | tf_op jit(solution)/shard_map/pallas_call | solution.py:685
  68.9 2.1 %shard_map.165 = (f32[6,3,32,128]{3,2,1,0:T(8,128)}, f32[16,256]{1,0:T(8,128)}, f32[256,256]{1,0:T(8,128)}, f32[256,256]{1,0:T(8,128)}, f32[4,256]{1,0:T(4,128)}) custom-call(f32[6,3,32,128]{3,2,1,0:T(8,128)} %get-tuple-element.15.refs_0_, f32[16,256]{1,0:T(8,128)} %get-tuple-element.16.refs_1_, f32[256,256]{1,0:T(8,128)} %get-tuple-element.17.refs_2_, ...), custom_call_target="tpu_custom_call" | custom-call | tf_op jit(solution)/shard_map/pallas_call | solution.py:758

commit v6 on v5

--- a/solution.py
+++ b/solution.py
@@ -68,9 +68,9 @@
     edge, gath, picked, arr, inner, tile_r, meta, sel_r, selt_r, ghost_r,
     cote, cz, tbl, ret,
     gtop, gmid, gin, gout,
-    cg, gsum, ra, rb, full, other, sg, sc, sa, sb, sf, st,
+    cg, gsum, ra, rb, full, sg, sa, sb, sf,
     pl_s, pl_r, me_s, me_r, zz_s, zz_r, cz_s, cz_r, rt_s, rt_r,
-    in_s, c_s, c_r, a1_s, a1_r, a2_s, a2_r, a3_s, a3_r, f_s, f_r, s0_s, s0_r, s1_s, s1_r, s2_s, s2_r, s3_s, s3_r,
+    in_s, c_s, c_r, a1_s, a1_r, a2_s, a2_r, a3_s, a3_r, f_s, f_r, s1_s, s1_r, s2_s, s2_r, s3_s, s3_r,
 ):
     x_r, first_r, second_r, third_r = (x0, x1), (first0, first1), (second0, second1), (third0, third1)
     b = lax.axis_index("blk")
@@ -96,6 +96,9 @@
     def at_a(q):
         return {"blk": z * PL + lax.rem(q, 4) * 2 + core, "op": lax.div(q, 4) * 2 + z_lo}
 
+    def at_zc(w, c):
+        return {"blk": lax.div(w, 2) * PL + p - core + c, "op": x_at * 2 + lax.rem(w, 2)}
+
     def partner():
         return {"blk": b + 1 - 2 * core}
 
@@ -127,9 +130,8 @@
     for d in range(4, AN):
         greet(at_a(lax.rem(x_at * 4 + d, AN)))
     for d in range(1, BN):
-        greet(at_b(lax.rem(zz + d, BN)))
-    for d in range(1, ZN):
-        greet(at_tower(lax.rem(mine + 2 * d, 2 * ZN) + 1 - 2 * core))
+        for c in range(2):
+            greet(at_zc(lax.rem(zz + d, BN), c))
 
     loads = [pltpu.make_async_copy(h, v, in_s.at[i]) for i, (h, v) in enumerate(((state_h, state), (feat_h, feat), (target_h, target)))]
     for load in loads:
@@ -187,7 +189,7 @@
     loads[0].wait()
     pack(edge.at[0], state, (0, BI - 1))
 
-    pl.semaphore_wait(barrier, PL - 1 + AN - 4 + BN - 1 + ZN - 1)
+    pl.semaphore_wait(barrier, PL - 1 + AN - 4 + 2 * (BN - 1))
 
     def send_plane(k):
         for q in plane_peers:
@@ -500,82 +502,88 @@
         return carry
 
     grads = (gtop, gmid)
-    R = HID // AN
+    HR = HID // 2
+    R = HR // AN
 
     def hand(i):
-        @pl.when(core != i)
-        def _():
-            send(grads[i].at[pl.ds(0, HID)], cg, c_s, c_r, partner())
+        other = pl.ds(pl.multiple_of((1 - core) * HR, HR), HR)
+        send(grads[i].at[other], cg.at[i], c_s.at[i], c_r.at[i], partner())
 
     def ar_1(i):
-        got(cg, c_s, c_r, partner())
-        gsum[...] = (grads[i][0:HID] + cg[...]).reshape(AN, R, HID)
+        got(cg.at[i], c_s.at[i], c_r.at[i], partner())
+        half = grads[i][pl.ds(pl.multiple_of(core * HR, HR), HR), :] + cg[i]
+        gsum[i] = half.reshape(AN, R, HID)
         for d in range(1, AN):
             q = lax.rem(a + d, AN)
-            send(gsum.at[q], ra.at[a], a1_s, a1_r, at_a(q))
-        ra[a] = gsum[a]
-
-    def ar_2():
-        got(ra.at[pl.ds(0, AN - 1)], a1_s, a1_r, at_a(a))
-        total = ra[0]
+            send(gsum.at[i, q], ra.at[i, a], a1_s.at[i], a1_r.at[i], at_a(q))
+        ra[i, a] = gsum[i, a]
+
+    def ar_2(i):
+        got(ra.at[i, pl.ds(0, AN - 1)], a1_s.at[i], a1_r.at[i], at_b(zz))
+        total = ra[i, 0]
         for q in range(1, AN):
-            total = total + ra[q]
-        rb[zz] = total
+            total = total + ra[i, q]
+        rb[i, zz] = total
         for d in range(1, BN):
-            send(rb.at[zz], rb.at[zz], a2_s, a2_r, at_b(lax.rem(zz + d, BN)))
-
-    def ar_3():
-        got(rb.at[pl.ds(0, BN - 1)], a2_s, a2_r, at_b(zz))
-        total = rb[0]
+            send(rb.at[i, zz], rb.at[i, zz], a2_s.at[i], a2_r.at[i], at_b(lax.rem(zz + d, BN)))
+
+    def ar_3(i):
+        got(rb.at[i, pl.ds(0, BN - 1)], a2_s.at[i], a2_r.at[i], at_b(zz))
+        total = rb[i, 0]
         for w in range(1, BN):
-            total = total + rb[w]
-        full[a] = total
+            total = total + rb[i, w]
+        full[i, core, a] = total
         for d in range(1, AN):
-            send(full.at[a], full.at[a], a3_s, a3_r, at_a(lax.rem(a + d, AN)))
-
-    def ar_4(out):
-        got(full.at[pl.ds(0, AN - 1)], a3_s, a3_r, at_a(a))
-        send(full, other, f_s, f_r, partner())
-        out[...] = full[...].reshape(HID, HID)
-
-    def ar_5(out):
-        got(other, f_s, f_r, partner())
-        out[...] = other[...].reshape(HID, HID)
-
-    def small_0():
-        sg[0:NF] = gin[0:NF]
-        sg[NF:NF + 1] = jnp.sum(gout[...].T, axis=0, keepdims=True)
-        sg[NF + 1:NF + 2] = gin[NF:NF + 1]
-        sg[NF + 2:NF + 3] = gmid[HID:HID + 1]
-        sg[NF + 3:NF + 4] = gtop[HID:HID + 1]
-        sg[NF + 4:NF + 8] = jnp.zeros((4, HID), f32)
-
-        @pl.when(core == 1)
-        def _():
-            send(sg, sc, s0_s, s0_r, partner())
+            send(full.at[i, core, a], full.at[i, core, a], a3_s.at[i], a3_r.at[i], at_a(lax.rem(a + d, AN)))
+
+    def ar_4(i):
+        got(full.at[i, core, pl.ds(0, AN - 1)], a3_s.at[i], a3_r.at[i], at_b(zz))
+        send(full.at[i, core], full.at[i, core], f_s.at[i], f_r.at[i], partner())
+
+    def ar_5(i, out):
+        got(full.at[i, 1 - core], f_s.at[i], f_r.at[i], partner())
+        out[...] = full[i].reshape(HID, HID)
 
     def small_1():
-        got(sc, s0_s, s0_r, partner())
-        sa[a] = sg[...] + sc[...]
+        for r in range(NF):
+            sg[r // 2, r % 2:r % 2 + 1] = gin[r:r + 1]
+        sg[NF // 2, 0:1] = jnp.sum(gout[...].T, axis=0, keepdims=True)
+        sg[NF // 2, 1:2] = gin[NF:NF + 1]
+        sg[NF // 2 + 1, 0:1] = gmid[HID:HID + 1]
+        sg[NF // 2 + 1, 1:2] = gtop[HID:HID + 1]
+        sg[NF // 2 + 2:] = jnp.zeros((AN - NF // 2 - 2, 2, HID), f32)
         for d in range(1, AN):
-            send(sa.at[a], sa.at[a], s1_s, s1_r, at_a(lax.rem(a + d, AN)))
+            q = lax.rem(a + d, AN)
+            send(sg.at[q], sa.at[a], s1_s, s1_r, at_a(q))
+        sa[a] = sg[a]
 
     def small_2():
         got(sa.at[pl.ds(0, AN - 1)], s1_s, s1_r, at_a(a))
         total = sa[0]
         for q in range(1, AN):
             total = total + sa[q]
-        sb[zz] = total
+        own = 2 * zz + core
+        sb[own] = total
+        send(sb.at[own], sb.at[own], s2_s, s2_r, partner())
         for d in range(1, BN):
-            send(sb.at[zz], sb.at[zz], s2_s, s2_r, at_b(lax.rem(zz + d, BN)))
+            for c in range(2):
+                send(sb.at[own], sb.at[own], s2_s, s2_r, at_zc(lax.rem(zz + d, BN), c))
 
     def small_3():
-        got(sb.at[pl.ds(0, BN - 1)], s2_s, s2_r, at_b(zz))
+        got(sb.at[pl.ds(0, 2 * BN - 1)], s2_s, s2_r, at_b(zz))
         total = sb[0]
-        for w in range(1, BN):
+        for w in range(1, 2 * BN):
             total = total + sb[w]
-        sf[...] = total
-        send(sf, st, s3_s, s3_r, partner())
+        sf[a] = total
+        for d in range(1, AN):
+            send(sf.at[a], sf.at[a], s3_s, s3_r, at_a(lax.rem(a + d, AN)))
+
+    def small_4():
+        got(sf.at[pl.ds(0, AN - 1)], s3_s, s3_r, at_a(a))
+        for r in range(NF):
+            out_in[r:r + 1] = sf[r // 2, r % 2:r % 2 + 1]
+        for r in range(4):
+            out_vec[r:r + 1] = sf[(NF + r) // 2, r % 2:r % 2 + 1]
 
     LAST = NCH // 2 - 1
     lax.fori_loop(0, LAST, back_top, 0)
@@ -591,49 +599,38 @@
     layer_back(LAST, top_w, third_r, second_r, gmid, first_r)
     weigh(1, LAST, gmid, first_r, second_r)
     hand(1)
-
-    @pl.when(core == 0)
-    def _():
-        ar_1(0)
+    ar_1(0)
 
     def back_first(k, carry):
         layer_back(k, mid_w, second_r, first_r, gin, x_r, k > 0)
 
-        @pl.when((k == 1) & (core == 1))
+        @pl.when(k == 1)
         def _():
             ar_1(1)
 
-        @pl.when((k == 4) & (core == 0))
+        @pl.when(k == 3)
         def _():
-            ar_2()
+            ar_2(0)
+
+        @pl.when(k == 5)
+        def _():
+            ar_2(1)
 
         return carry
 
     lax.fori_loop(0, LAST + 1, back_first, 0)
     weigh(1, LAST, gin, x_r, first_r)
 
-    small_0()
-
-    @pl.when(core == 0)
-    def _():
-        small_1()
-        ar_3()
-        small_2()
-        ar_4(out_top)
-        small_3()
-        out_in[...] = sf[0:NF]
-        out_vec[...] = sf[NF:NF + 4]
-        ar_5(out_mid)
-
-    @pl.when(core == 1)
-    def _():
-        ar_2()
-        ar_3()
-        ar_4(out_mid)
-        ar_5(out_top)
-        got(st, s3_s, s3_r, partner())
-        out_in[...] = st[0:NF]
-        out_vec[...] = st[NF:NF + 4]
+    small_1()
+    ar_3(0)
+    ar_3(1)
+    small_2()
+    ar_4(0)
+    ar_4(1)
+    small_3()
+    ar_5(0, out_top)
+    ar_5(1, out_mid)
+    small_4()
 
     for k in range(2):
         for q in plane_peers:
@@ -645,21 +642,15 @@
         gone(cote.at[core], cz_s.at[w], cz_r.at[mine], at_tower(w))
     for q in plane_peers:
         gone(tbl.at[q], rt_s.at[q], rt_r.at[p], at_plane(q))
-    gone(cg, c_s, c_r, partner())
-    gone(ra.at[pl.ds(0, AN - 1)], a1_s, a1_r, at_a(a))
-    gone(rb.at[pl.ds(0, BN - 1)], a2_s, a2_r, at_b(zz))
-    gone(full.at[pl.ds(0, AN - 1)], a3_s, a3_r, at_a(a))
-    gone(full, f_s, f_r, partner())
-
-    @pl.when(core == 0)
-    def _():
-        gone(sa.at[pl.ds(0, AN - 1)], s1_s, s1_r, at_a(a))
-        gone(sb.at[pl.ds(0, BN - 1)], s2_s, s2_r, at_b(zz))
-        gone(sf, s3_s, s3_r, partner())
-
-    @pl.when(core == 1)
-    def _():
-        gone(sg, s0_s, s0_r, partner())
+    for i in range(2):
+        gone(cg.at[i], c_s.at[i], c_r.at[i], partner())
+        gone(ra.at[i, pl.ds(0, AN - 1)], a1_s.at[i], a1_r.at[i], at_b(zz))
+        gone(rb.at[i, pl.ds(0, BN - 1)], a2_s.at[i], a2_r.at[i], at_b(zz))
+        gone(ra.at[i, pl.ds(0, AN - 1)], a3_s.at[i], a3_r.at[i], at_b(zz))
+        gone(cg.at[i], f_s.at[i], f_r.at[i], partner())
+    gone(sa.at[pl.ds(0, AN - 1)], s1_s, s1_r, at_a(a))
+    gone(sb.at[pl.ds(0, 2 * BN - 1)], s2_s, s2_r, at_b(zz))
+    gone(sf.at[pl.ds(0, AN - 1)], s3_s, s3_r, at_a(a))
 
 
 def copy_kernel(*refs):
@@ -732,21 +723,19 @@
             pltpu.VMEM((HID + 16, HID), f32),
             pltpu.VMEM((NF + 16, HID), f32),
             pltpu.VMEM((HID, BJ), f32),
-            pltpu.VMEM((HID, HID), f32),
-            pltpu.VMEM((AN, HID // AN, HID), f32),
-            pltpu.VMEM((AN, HID // AN, HID), f32),
-            pltpu.VMEM((BN, HID // AN, HID), f32),
-            pltpu.VMEM((AN, HID // AN, HID), f32),
-            pltpu.VMEM((AN, HID // AN, HID), f32),
-            pltpu.VMEM((24, HID), f32),
-            pltpu.VMEM((24, HID), f32),
-            pltpu.VMEM((AN, 24, HID), f32),
-            pltpu.VMEM((BN, 24, HID), f32),
-            pltpu.VMEM((24, HID), f32),
-            pltpu.VMEM((24, HID), f32),
+            pltpu.VMEM((2, HID // 2, HID), f32),
+            pltpu.VMEM((2, AN, HID // 2 // AN, HID), f32),
+            pltpu.VMEM((2, AN, HID // 2 // AN, HID), f32),
+            pltpu.VMEM((2, BN, HID // 2 // AN, HID), f32),
+            pltpu.VMEM((2, 2, AN, HID // 2 // AN, HID), f32),
+            pltpu.VMEM((AN, 2, HID), f32),
+            pltpu.VMEM((AN, 2, HID), f32),
+            pltpu.VMEM((2 * BN, 2, HID), f32),
+            pltpu.VMEM((AN, 2, HID), f32),
             dma((2, PL)), dma((2, PL)), dma((2 * ZN,)), dma((2 * ZN,)), dma((2, 2 * ZN)), dma((2, 2 * ZN)),
             dma((2 * ZN,)), dma((2 * ZN,)), dma((PL,)), dma((PL,)),
-            dma((3,)), dma, dma, dma, dma, dma, dma, dma, dma, dma, dma, dma, dma, dma, dma, dma, dma, dma, dma,
+            dma((3,)), dma((2,)), dma((2,)), dma((2,)), dma((2,)), dma((2,)), dma((2,)), dma((2,)), dma((2,)), dma((2,)), dma((2,)),
+            dma, dma, dma, dma, dma, dma,
         ],
         compiler_params=pltpu.CompilerParams(
             collective_id=0, has_side_effects=True, vmem_limit_bytes=56 * 2**20

time: 71.1 us -> 71 us (level)
  no operation moved by 1% of the time
where the time goes in v6:
time: 71 us; the launch traced here: 70.9 us
  Pallas kernels  69.6 us (98%)
  between operations  1.29 us (2%)
    pallas_call x1, Pallas kernels, per_device(): pl.pallas_call(functools.partial(kernel, loss_scale), out_shape=(jax.Shap...  67.5 us
    pallas_call x1, Pallas kernels, per_device(): pl.pallas_call(copy_kernel, out_shape=tuple((jax.ShapeDtypeStruct(x.shape...  2.07 us

profile of v6, /device:TPU:1, one launch (start us, length us, event | category | flops | bytes accessed | tf_op | source)
XLA Modules:
  0.0 70.9 jit_solution(6935438929675345344)
XLA Ops:
  1.3 67.5 %shard_map.164 = (f32[6,3,32,128]{3,2,1,0:T(8,128)}, f32[16,256]{1,0:T(8,128)}, f32[256,256]{1,0:T(8,128)}, f32[256,256]{1,0:T(8,128)}, f32[4,256]{1,0:T(4,128)}) custom-call(f32[6,3,32,128]{3,2,1,0:T(8,128)} %bitcast.8, f32[6,3,32,128]{3,2,1,0:T(8,128)} %bitcast.9, bf16[16,3,32,128]{3,2,1,0:T(8,128)(2,1)} %bitcast.7, f32[6,6]{1,0:T(8,128)} %coup.1, ...), custom_call_target="tpu_custom_call" | custom-call | tf_op jit(solution)/shard_map/pallas_call | solution.py:676
  68.8 2.1 %shard_map.165 = (f32[6,3,32,128]{3,2,1,0:T(8,128)}, f32[16,256]{1,0:T(8,128)}, f32[256,256]{1,0:T(8,128)}, f32[256,256]{1,0:T(8,128)}, f32[4,256]{1,0:T(4,128)}) custom-call(f32[6,3,32,128]{3,2,1,0:T(8,128)} %get-tuple-element.15.refs_0_, f32[16,256]{1,0:T(8,128)} %get-tuple-element.16.refs_1_, f32[256,256]{1,0:T(8,128)} %get-tuple-element.17.refs_2_, ...), custom_call_target="tpu_custom_call" | custom-call | tf_op jit(solution)/shard_map/pallas_call | solution.py:747

commit v7 on v6

--- a/solution.py
+++ b/solution.py
@@ -61,8 +61,8 @@
 def kernel(
     loss_scale,
     state_h, target_h, feat_h, coup, in_w, mid_w, top_w, out_w, biases, count, conn, orient, rot,
-    out_state, out_in, out_mid, out_top, out_vec,
-    state, target, feat, x0, x1, first0, first1, second0, second1, third0, third1,
+    out_h, out_in, out_mid, out_top, out_vec,
+    out_state, state, target, feat, x0, x1, first0, first1, second0, second1, third0, third1,
     xs, win_t, wmid_t, wtop_t, bias_c, ow_c,
     mid_r, ts_r, tm_r, fc_r, beta_r, betan_r, bc_r, bcn_r,
     edge, gath, picked, arr, inner, tile_r, meta, sel_r, selt_r, ghost_r,
@@ -271,7 +271,7 @@
                 row = row_of(s, 16 * h + r)
                 x_r[row // 8 % 2][row // 16, :, (row % 8) * BJ:(row % 8 + 1) * BJ] = xs[s, h, pl.ds(r, NF, stride=16), :].astype(bf16)
 
-    SUB = 256
+    SUB = 512
 
     weights = (win_t, wmid_t, wtop_t)
     acts = (x_r, first_r, second_r, third_r)
@@ -408,6 +408,9 @@
         bcn_r[s * BI:(s + 1) * BI, :] = tau * acc
         for first, place, length in runs(s):
             bc_r[place:place + length, :] = bcn_r[s * BI + first:s * BI + first + length, :]
+
+    leave = pltpu.make_async_copy(out_state, out_h, in_s.at[3])
+    leave.start()
 
     def table():
         for w in tower:
@@ -632,6 +635,7 @@
     ar_5(1, out_mid)
     small_4()
 
+    leave.wait()
     for k in range(2):
         for q in plane_peers:
             gone(edge.at[k, core], pl_s.at[k, q], pl_r.at[k, p], at_plane(q))
@@ -654,11 +658,16 @@
 
 
 def copy_kernel(*refs):
-    ins, outs, sem = refs[:5], refs[5:10], refs[10]
-    copies = [pltpu.make_async_copy(ins[i], outs[i], sem.at[i]) for i in range(5)]
-    for copy in copies:
+    ins, outs, held, sem = refs[:5], refs[5:10], refs[10:15], refs[15]
+    parts = [(0, slice(v, v + 1)) for v in range(NV)] + [(i, slice(None)) for i in range(1, 5)]
+    come = [pltpu.make_async_copy(ins[i].at[at], held[i].at[at], sem.at[0, n]) for n, (i, at) in enumerate(parts)]
+    go = [pltpu.make_async_copy(held[i].at[at], outs[i].at[at], sem.at[1, n]) for n, (i, at) in enumerate(parts)]
+    for copy in come:
         copy.start()
-    for copy in copies:
+    for first, then in zip(come, go):
+        first.wait()
+        then.start()
+    for copy in go:
         copy.wait()
 
 
@@ -683,9 +692,9 @@
             jax.ShapeDtypeStruct((4, HID), f32),
         ),
         in_specs=[anywhere, anywhere, anywhere, smem, vmem, vmem, vmem, vmem, vmem, smem, smem, smem, smem],
-        out_specs=(vmem,) * 5,
+        out_specs=(anywhere, vmem, vmem, vmem, vmem),
         scratch_shapes=[
-            field, field, pltpu.VMEM((NF, NS, BI, BJ), bf16),
+            field, field, field, pltpu.VMEM((NF, NS, BI, BJ), bf16),
             pltpu.VMEM((NCH // 2, NF, CW), bf16),
             pltpu.VMEM((NCH // 2, NF, CW), bf16),
             pltpu.VMEM((NCH // 2, HID, CW), bf16),
@@ -734,7 +743,7 @@
             pltpu.VMEM((AN, 2, HID), f32),
             dma((2, PL)), dma((2, PL)), dma((2 * ZN,)), dma((2 * ZN,)), dma((2, 2 * ZN)), dma((2, 2 * ZN)),
             dma((2 * ZN,)), dma((2 * ZN,)), dma((PL,)), dma((PL,)),
-            dma((3,)), dma((2,)), dma((2,)), dma((2,)), dma((2,)), dma((2,)), dma((2,)), dma((2,)), dma((2,)), dma((2,)), dma((2,)),
+            dma((4,)), dma((2,)), dma((2,)), dma((2,)), dma((2,)), dma((2,)), dma((2,)), dma((2,)), dma((2,)), dma((2,)), dma((2,)),
             dma, dma, dma, dma, dma, dma,
         ],
         compiler_params=pltpu.CompilerParams(
@@ -747,9 +756,9 @@
     outs = pl.pallas_call(
         copy_kernel,
         out_shape=tuple(jax.ShapeDtypeStruct(x.shape, x.dtype) for x in outs),
-        in_specs=[vmem] * 5,
-        out_specs=(pl.BlockSpec(memory_space=pl.ANY),) * 5,
-        scratch_shapes=[dma((5,))],
+        in_specs=[anywhere] * 5,
+        out_specs=(anywhere,) * 5,
+        scratch_shapes=[pltpu.VMEM(x.shape, x.dtype) for x in outs] + [dma((2, NV + 4))],
     )(*outs)
     return (outs[0][None],) + tuple(outs[1:])
 

time: 71 us -> 70.8 us (level)
  no operation moved by 1% of the time
where the time goes in v7:
time: 70.8 us; the launch traced here: 70.7 us
  Pallas kernels  69.4 us (98%)
  between operations  1.29 us (2%)
    pallas_call x1, Pallas kernels, per_device(): pl.pallas_call(functools.partial(kernel, loss_scale), out_shape=(jax.Shap...  67.3 us
    pallas_call x1, Pallas kernels, per_device(): pl.pallas_call(copy_kernel, out_shape=tuple((jax.ShapeDtypeStruct(x.shape...  2.1 us

profile of v7, /device:TPU:1, one launch (start us, length us, event | category | flops | bytes accessed | tf_op | source)
XLA Modules:
  0.0 70.7 jit_solution(16424464948341669585)
XLA Ops:
  1.3 67.3 %shard_map.164 = (f32[6,3,32,128]{3,2,1,0:T(8,128)}, f32[16,256]{1,0:T(8,128)}, f32[256,256]{1,0:T(8,128)}, f32[256,256]{1,0:T(8,128)}, f32[4,256]{1,0:T(4,128)}) custom-call(f32[6,3,32,128]{3,2,1,0:T(8,128)} %bitcast.8, f32[6,3,32,128]{3,2,1,0:T(8,128)} %bitcast.9, bf16[16,3,32,128]{3,2,1,0:T(8,128)(2,1)} %bitcast.7, f32[6,6]{1,0:T(8,128)} %coup.1, ...), custom_call_target="tpu_custom_call" | custom-call | tf_op jit(solution)/shard_map/pallas_call | solution.py:685
  68.6 2.1 %shard_map.165 = (f32[6,3,32,128]{3,2,1,0:T(8,128)}, f32[16,256]{1,0:T(8,128)}, f32[256,256]{1,0:T(8,128)}, f32[256,256]{1,0:T(8,128)}, f32[4,256]{1,0:T(4,128)}) custom-call(f32[6,3,32,128]{3,2,1,0:T(8,128)} %get-tuple-element.15.refs_0_, f32[16,256]{1,0:T(8,128)} %get-tuple-element.16.refs_1_, f32[256,256]{1,0:T(8,128)} %get-tuple-element.17.refs_2_, ...), custom_call_target="tpu_custom_call" | custom-call | tf_op jit(solution)/shard_map/pallas_call | solution.py:756

commit v8 on v7

--- a/solution.py
+++ b/solution.py
@@ -352,11 +352,14 @@
         return up + down + lanes_sum(u, lane32) - 4.0 * u
 
     def low_high(k, s, v):
-        return ghost_r[k, v, 2 * s:2 * s + 1, :], ghost_r[k, v, 2 * s + 1:2 * s + 2, :]
-
-    for s in range(NS):
+        return ghost_r[k, v, pl.ds(2 * s, 1), :], ghost_r[k, v, pl.ds(2 * s + 1, 1), :]
+
+    def rows_of(s):
+        return pl.ds(pl.multiple_of(s * BI, BI), BI)
+
+    def first_sweep(s, carry):
         us = [state[v, s] for v in range(NV)]
-        beta = betan_r[s * BI:(s + 1) * BI, :]
+        beta = betan_r[rows_of(s), :]
         for v in range(NV):
             t = jnp.tanh(us[v])
             ts_r[v, s] = t
@@ -365,6 +368,9 @@
             for w in range(1, NV):
                 coupled = coupled + coup[v, w] * us[w]
             mid_r[v, s] = us[v] + tau * (stencil(us[v], low, high) - coupled + beta * t)
+        return carry
+
+    lax.fori_loop(0, NS, first_sweep, 0)
 
     ghosts(1)
     pack(inner, mid_r, (1, BI - 2))
@@ -380,9 +386,10 @@
     for w in tower:
         send(cote.at[lax.rem(w, 2)], cz.at[mine], cz_s.at[w], cz_r.at[mine], at_tower(w))
 
-    for s in range(NS):
+    def second_sweep(s, carry):
+        alive = jnp.where(s < count[0], 1.0, 0.0).astype(f32)
         us = [mid_r[v, s] for v in range(NV)]
-        beta = betan_r[s * BI:(s + 1) * BI, :]
+        beta = betan_r[rows_of(s), :]
         for v in range(NV):
             t = jnp.tanh(us[v])
             tm_r[v, s] = t
@@ -391,12 +398,15 @@
             for w in range(1, NV):
                 coupled = coupled + coup[v, w] * us[w]
             final = us[v] + tau * (stencil(us[v], low, high) - coupled + beta * t)
-            out_state[v, s] = live[s] * final
-            fc_r[v, s] = loss_scale * live[s] * (final - target[v, s])
-
-    for s in range(NS):
+            out_state[v, s] = alive * final
+            fc_r[v, s] = loss_scale * alive * (final - target[v, s])
+        return carry
+
+    lax.fori_loop(0, NS, second_sweep, 0)
+
+    def back_sweep(s, carry):
         gs = [fc_r[v, s] for v in range(NV)]
-        beta = betan_r[s * BI:(s + 1) * BI, :]
+        beta = betan_r[rows_of(s), :]
         acc = jnp.zeros((BI, BJ), f32)
         for v in range(NV):
             t = tm_r[v, s]
@@ -405,7 +415,11 @@
                 coupled = coupled + coup[w, v] * gs[w]
             mc = gs[v] + tau * (stencil(gs[v], 0.0, 0.0) - coupled + beta * (1.0 - t * t) * gs[v])
             acc = acc + (gs[v] * t + mc * ts_r[v, s])
-        bcn_r[s * BI:(s + 1) * BI, :] = tau * acc
+        bcn_r[rows_of(s), :] = tau * acc
+        return carry
+
+    lax.fori_loop(0, NS, back_sweep, 0)
+    for s in range(NS):
         for first, place, length in runs(s):
             bc_r[place:place + length, :] = bcn_r[s * BI + first:s * BI + first + length, :]
 
@@ -469,6 +483,14 @@
             gout[rows] = acc
 
     def back_top(k, carry):
+        @pl.when(k == 2)
+        def _():
+            table()
+
+        @pl.when(k == NCH // 2 - 1)
+        def _():
+            returned()
+
         weigh(1, before(k), gtop, second_r, third_r, k > 0)
         top_delta(0, k)
         weigh(0, k, gtop, second_r, third_r)
@@ -500,10 +522,6 @@
                         weigh(0, k, acc, left, act)
         put(*held)
 
-    def back_mid(k, carry):
-        layer_back(k, top_w, third_r, second_r, gmid, first_r, k > 0)
-        return carry
-
     grads = (gtop, gmid)
     HR = HID // 2
     R = HR // AN
@@ -588,21 +606,27 @@
         for r in range(4):
             out_vec[r:r + 1] = sf[(NF + r) // 2, r % 2:r % 2 + 1]
 
-    LAST = NCH // 2 - 1
-    lax.fori_loop(0, LAST, back_top, 0)
-    weigh(1, LAST - 1, gtop, second_r, third_r)
-    table()
-    top_delta(0, LAST)
-    weigh(0, LAST, gtop, second_r, third_r)
-    lax.fori_loop(0, LAST, back_mid, 0)
-    returned()
-    top_delta(1, LAST)
-    weigh(1, LAST, gtop, second_r, third_r)
+    PAIRS = NCH // 2
+    lax.fori_loop(0, PAIRS, back_top, 0)
+    weigh(1, PAIRS - 1, gtop, second_r, third_r)
     hand(0)
-    layer_back(LAST, top_w, third_r, second_r, gmid, first_r)
-    weigh(1, LAST, gmid, first_r, second_r)
+
+    def back_mid(k, carry):
+        layer_back(k, top_w, third_r, second_r, gmid, first_r, k > 0)
+
+        @pl.when(k == 1)
+        def _():
+            ar_1(0)
+
+        @pl.when(k == 4)
+        def _():
+            ar_2(0)
+
+        return carry
+
+    lax.fori_loop(0, PAIRS, back_mid, 0)
+    weigh(1, PAIRS - 1, gmid, first_r, second_r)
     hand(1)
-    ar_1(0)
 
     def back_first(k, carry):
         layer_back(k, mid_w, second_r, first_r, gin, x_r, k > 0)
@@ -610,30 +634,26 @@
         @pl.when(k == 1)
         def _():
             ar_1(1)
-
-        @pl.when(k == 3)
-        def _():
-            ar_2(0)
-
-        @pl.when(k == 5)
+            ar_3(0)
+
+        @pl.when(k == 4)
         def _():
             ar_2(1)
+            ar_4(0)
 
         return carry
 
-    lax.fori_loop(0, LAST + 1, back_first, 0)
-    weigh(1, LAST, gin, x_r, first_r)
+    lax.fori_loop(0, PAIRS, back_first, 0)
+    weigh(1, PAIRS - 1, gin, x_r, first_r)
 
     small_1()
-    ar_3(0)
     ar_3(1)
     small_2()
-    ar_4(0)
+    ar_5(0, out_top)
+    small_3()
     ar_4(1)
-    small_3()
-    ar_5(0, out_top)
+    small_4()
     ar_5(1, out_mid)
-    small_4()
 
     leave.wait()
     for k in range(2):

time: 70.8 us -> 78.9 us (1.11)
  Pallas kernels: 69.4 us -> 77.5 us
    pallas_call x1, Pallas kernels: 67.3 us -> 75.4 us  [per_device(): pl.pallas_call(functools.partial(kernel, loss_scale), out_shape=(jax.Shap...]
where the time goes in v8:
time: 78.9 us; the launch traced here: 78.7 us
  Pallas kernels  77.5 us (98%)
  between operations  1.29 us (2%)
    pallas_call x1, Pallas kernels, per_device(): pl.pallas_call(functools.partial(kernel, loss_scale), out_shape=(jax.Shap...  75.4 us
    pallas_call x1, Pallas kernels, per_device(): pl.pallas_call(copy_kernel, out_shape=tuple((jax.ShapeDtypeStruct(x.shape...  2.1 us

profile of v8, /device:TPU:1, one launch (start us, length us, event | category | flops | bytes accessed | tf_op | source)
XLA Modules:
  0.0 78.7 jit_solution(8475179122160934348)
XLA Ops:
  1.3 75.4 %shard_map.164 = (f32[6,3,32,128]{3,2,1,0:T(8,128)}, f32[16,256]{1,0:T(8,128)}, f32[256,256]{1,0:T(8,128)}, f32[256,256]{1,0:T(8,128)}, f32[4,256]{1,0:T(4,128)}) custom-call(f32[6,3,32,128]{3,2,1,0:T(8,128)} %bitcast.8, f32[6,3,32,128]{3,2,1,0:T(8,128)} %bitcast.9, bf16[16,3,32,128]{3,2,1,0:T(8,128)(2,1)} %bitcast.7, f32[6,6]{1,0:T(8,128)} %coup.1, ...), custom_call_target="tpu_custom_call" | custom-call | tf_op jit(solution)/shard_map/pallas_call | solution.py:705
  76.6 2.1 %shard_map.165 = (f32[6,3,32,128]{3,2,1,0:T(8,128)}, f32[16,256]{1,0:T(8,128)}, f32[256,256]{1,0:T(8,128)}, f32[256,256]{1,0:T(8,128)}, f32[4,256]{1,0:T(4,128)}) custom-call(f32[6,3,32,128]{3,2,1,0:T(8,128)} %get-tuple-element.15.refs_0_, f32[16,256]{1,0:T(8,128)} %get-tuple-element.16.refs_1_, f32[256,256]{1,0:T(8,128)} %get-tuple-element.17.refs_2_, ...), custom_call_target="tpu_custom_call" | custom-call | tf_op jit(solution)/shard_map/pallas_call | solution.py:776

commit v9 on v7

--- a/solution.py
+++ b/solution.py
@@ -26,6 +26,9 @@
 BN = 8
 HV = NV // 2
 HALF = HV * BJ
+FH = NF // 2
+FROW = FH * BJ
+GHOST = NCH // 2
 
 
 def row_of(s, i):
@@ -65,11 +68,11 @@
     out_state, state, target, feat, x0, x1, first0, first1, second0, second1, third0, third1,
     xs, win_t, wmid_t, wtop_t, bias_c, ow_c,
     mid_r, ts_r, tm_r, fc_r, beta_r, betan_r, bc_r, bcn_r,
-    edge, gath, picked, arr, inner, tile_r, meta, sel_r, selt_r, ghost_r,
-    cote, cz, tbl, ret,
+    edge, gath, picked, arr, inner, tile_r, meta, sel_r, ghost_r, rawt,
+    fedge, fgath, fpicked, farr, xg,
     gtop, gmid, gin, gout,
     cg, gsum, ra, rb, full, sg, sa, sb, sf,
-    pl_s, pl_r, me_s, me_r, zz_s, zz_r, cz_s, cz_r, rt_s, rt_r,
+    pl_s, pl_r, me_s, me_r, zz_s, zz_r, fz_s, fz_r, fp_s, fp_r,
     in_s, c_s, c_r, a1_s, a1_r, a2_s, a2_r, a3_s, a3_r, f_s, f_r, s1_s, s1_r, s2_s, s2_r, s3_s, s3_r,
 ):
     x_r, first_r, second_r, third_r = (x0, x1), (first0, first1), (second0, second1), (third0, third1)
@@ -218,8 +221,25 @@
         local = named - (z * (PL * 8)).astype(f32)
         sel = jnp.where((local == lane.astype(f32)) & (lane < PL * 8), 1.0, 0.0).astype(f32)
         sel_r[...] = sel[:, :PL * 8].astype(bf16)
-        wide = jnp.concatenate([sel, jnp.zeros((BJ - n, BJ), f32)], axis=0).T
-        selt_r[...] = wide[:PL * 8, :n].astype(bf16)
+
+    def pick_features():
+        for q in plane_peers:
+            got(fgath.at[q], fp_s.at[q], fp_r.at[q], at_plane(q))
+        chosen = mm(sel_r[...], fgath[...].reshape(PL * 8, FROW).astype(bf16))
+        fpicked[...] = chosen.reshape(2 * ZN, 8, FROW)
+        farr[mine] = fpicked[mine]
+        for w in tower:
+            send(fpicked.at[w], farr.at[mine], fz_s.at[w], fz_r.at[mine], at_tower(w))
+
+    def ghost_features():
+        for w in tower:
+            got(farr.at[w], fz_s.at[w], fz_r.at[w], at_tower(w))
+        for h in range(2):
+            total = (farr[h] + farr[2 + h]) + (farr[4 + h] + farr[6 + h])
+            for f in range(FH):
+                for g in range(8):
+                    xg[h * FH + f:h * FH + f + 1, g * BJ:(g + 1) * BJ] = total[g:g + 1, f * BJ:(f + 1) * BJ]
+        x0[GHOST] = xg[...].astype(bf16)
 
     def turned(parts, sign):
         flip, cos, sin = tile_r[0], tile_r[1], tile_r[2] * sign
@@ -238,6 +258,9 @@
         for w in tower:
             got(arr.at[k, w], zz_s.at[k, w], zz_r.at[k, w], at_tower(w))
         total = [(arr[k, h] + arr[k, 2 + h]) + (arr[k, 4 + h] + arr[k, 6 + h]) for h in range(2)]
+        if k == 0:
+            for v in range(NV):
+                rawt[v] = jnp.tanh(total[v // HV][:, v % HV * BJ:(v % HV + 1) * BJ])
         parts = turned([total[v // HV][:, v % HV * BJ:(v % HV + 1) * BJ] for v in range(NV)], 1.0)
         for v in range(NV):
             ghost_r[k, v] = parts[v]
@@ -265,6 +288,16 @@
     for s in range(NS):
         for h in range(2):
             xs[s, h] = feat[:, s, 16 * h:16 * h + 16, :].astype(f32).reshape(NF * 16, BJ)
+    fedge[...] = jnp.zeros((2, 8, FROW), f32)
+    for s in range(NS):
+        for e in range(2):
+            for f in range(NF):
+                at = f * 16 + 15 * e
+                fedge[f // FH, 2 * s + e:2 * s + e + 1, f % FH * BJ:(f % FH + 1) * BJ] = xs[s, e, at:at + 1, :]
+    for q in plane_peers:
+        send(fedge.at[lax.rem(q, 2)], fgath.at[p], fp_s.at[q], fp_r.at[p], at_plane(q))
+    fgath[p] = fedge[core]
+
     for s in range(NS):
         for h in range(2):
             for r in range(16):
@@ -330,6 +363,7 @@
         @pl.when(k == 4)
         def _():
             pick(1)
+            pick_features()
 
         return carry
 
@@ -374,11 +408,10 @@
     goal_e = cut(inner)
     cot_e = [tau * (loss_scale * tile_r[3] * (final_e[v] - goal_e[v])) for v in range(NV)]
     cot_e = turned(cot_e, -1.0)
-    for v in range(NV):
-        part(cote, v)[...] = cot_e[v]
-    cz[mine] = cote[core]
-    for w in tower:
-        send(cote.at[lax.rem(w, 2)], cz.at[mine], cz_s.at[w], cz_r.at[mine], at_tower(w))
+    gained = cot_e[0] * rawt[0]
+    for v in range(1, NV):
+        gained = gained + cot_e[v] * rawt[v]
+    bc_r[8 * NCH:8 * NCH + 8, :] = tau * gained
 
     for s in range(NS):
         us = [mid_r[v, s] for v in range(NV)]
@@ -406,35 +439,25 @@
             mc = gs[v] + tau * (stencil(gs[v], 0.0, 0.0) - coupled + beta * (1.0 - t * t) * gs[v])
             acc = acc + (gs[v] * t + mc * ts_r[v, s])
         bcn_r[s * BI:(s + 1) * BI, :] = tau * acc
+        for e in range(2):
+            g = 8 * EDGE + 2 * s + e
+            row = s * BI + e * (BI - 1)
+            bc_r[g:g + 1, :] = bcn_r[row:row + 1, :]
         for first, place, length in runs(s):
             bc_r[place:place + length, :] = bcn_r[s * BI + first:s * BI + first + length, :]
 
     leave = pltpu.make_async_copy(out_state, out_h, in_s.at[3])
     leave.start()
 
-    def table():
-        for w in tower:
-            got(cz.at[w], cz_s.at[w], cz_r.at[w], at_tower(w))
-        sums = by_rows(selt_r[...], cz[...].reshape(2 * ZN * 8, HALF))
-        tbl[...] = sums.reshape(PL, 8, HALF)
-        ret[p] = tbl[p]
-        for q in plane_peers:
-            send(tbl.at[q], ret.at[p], rt_s.at[q], rt_r.at[p], at_plane(q))
-
-    def returned():
-        for q in plane_peers:
-            got(ret.at[q], rt_s.at[q], rt_r.at[q], at_plane(q))
-        extra = jnp.zeros((8, BJ), f32)
-        for h in range(2):
-            total = (ret[h] + ret[2 + h]) + (ret[4 + h] + ret[6 + h])
-            for v in range(HV):
-                cols = slice(v * BJ, (v + 1) * BJ)
-                extra = extra + total[:, cols] * jnp.tanh(edge[0, h, :, cols])
-        for s in range(NS):
-            for e in range(2):
-                g = 2 * s + e
-                row = s * BI + e * (BI - 1)
-                bc_r[8 * EDGE + g:8 * EDGE + g + 1, :] = bcn_r[row:row + 1, :] + tau * extra[g:g + 1]
+    def forward_ghost():
+        ghost_features()
+        for layer in range(3):
+            for j in range(CW // SUB):
+                cols = slice(j * SUB, (j + 1) * SUB)
+                d = mm(weights[layer][...], acts[layer][0][GHOST, :, cols])
+                for i in range(SUB // BJ):
+                    here = slice(cols.start + i * BJ, cols.start + (i + 1) * BJ)
+                    acts[layer + 1][0][GHOST, :, here] = jnp.tanh(d[:, i * BJ:(i + 1) * BJ] + bias_c[layer]).astype(bf16)
 
     ones = jnp.ones((16, CW), bf16)
     gout[...] = jnp.zeros((HID, BJ), f32)
@@ -504,6 +527,14 @@
         layer_back(k, top_w, third_r, second_r, gmid, first_r, k > 0)
         return carry
 
+    def layer_ghost(weight, source, act, acc, left):
+        for j in range(CW // SUB):
+            cols = slice(j * SUB, (j + 1) * SUB)
+            d = mm(weight[...], source[0][GHOST, :, cols])
+            t = act[0][GHOST, :, cols].astype(f32)
+            act[0][GHOST, :, cols] = (d * (1.0 - t * t)).astype(bf16)
+        weigh(0, GHOST, acc, left, act)
+
     grads = (gtop, gmid)
     HR = HID // 2
     R = HR // AN
@@ -591,16 +622,18 @@
     LAST = NCH // 2 - 1
     lax.fori_loop(0, LAST, back_top, 0)
     weigh(1, LAST - 1, gtop, second_r, third_r)
-    table()
     top_delta(0, LAST)
     weigh(0, LAST, gtop, second_r, third_r)
     lax.fori_loop(0, LAST, back_mid, 0)
-    returned()
+    forward_ghost()
     top_delta(1, LAST)
     weigh(1, LAST, gtop, second_r, third_r)
+    top_delta(0, GHOST)
+    weigh(0, GHOST, gtop, second_r, third_r)
     hand(0)
     layer_back(LAST, top_w, third_r, second_r, gmid, first_r)
     weigh(1, LAST, gmid, first_r, second_r)
+    layer_ghost(top_w, third_r, second_r, gmid, first_r)
     hand(1)
     ar_1(0)
 
@@ -623,6 +656,7 @@
 
     lax.fori_loop(0, LAST + 1, back_first, 0)
     weigh(1, LAST, gin, x_r, first_r)
+    layer_ghost(mid_w, second_r, first_r, gin, x_r)
 
     small_1()
     ar_3(0)
@@ -643,9 +677,9 @@
             gone(picked.at[k, w], zz_s.at[k, w], zz_r.at[k, mine], at_tower(w))
     for w in tower:
         gone(meta.at[mine], me_s.at[w], me_r.at[mine], at_tower(w))
-        gone(cote.at[core], cz_s.at[w], cz_r.at[mine], at_tower(w))
+        gone(fpicked.at[w], fz_s.at[w], fz_r.at[mine], at_tower(w))
     for q in plane_peers:
-        gone(tbl.at[q], rt_s.at[q], rt_r.at[p], at_plane(q))
+        gone(fedge.at[core], fp_s.at[q], fp_r.at[p], at_plane(q))
     for i in range(2):
         gone(cg.at[i], c_s.at[i], c_r.at[i], partner())
         gone(ra.at[i, pl.ds(0, AN - 1)], a1_s.at[i], a1_r.at[i], at_b(zz))
@@ -695,13 +729,13 @@
         out_specs=(anywhere, vmem, vmem, vmem, vmem),
         scratch_shapes=[
             field, field, field, pltpu.VMEM((NF, NS, BI, BJ), bf16),
+            pltpu.VMEM((NCH // 2 + 1, NF, CW), bf16),
             pltpu.VMEM((NCH // 2, NF, CW), bf16),
-            pltpu.VMEM((NCH // 2, NF, CW), bf16),
+            pltpu.VMEM((NCH // 2 + 1, HID, CW), bf16),
             pltpu.VMEM((NCH // 2, HID, CW), bf16),
+            pltpu.VMEM((NCH // 2 + 1, HID, CW), bf16),
             pltpu.VMEM((NCH // 2, HID, CW), bf16),
-            pltpu.VMEM((NCH // 2, HID, CW), bf16),
-            pltpu.VMEM((NCH // 2, HID, CW), bf16),
-            pltpu.VMEM((NCH // 2, HID, CW), bf16),
+            pltpu.VMEM((NCH // 2 + 1, HID, CW), bf16),
             pltpu.VMEM((NCH // 2, HID, CW), bf16),
             pltpu.VMEM((NS, 2, NF * 16, BJ), f32),
             pltpu.VMEM((HID, NF), bf16),
@@ -712,7 +746,7 @@
             field, field, field, field,
             pltpu.VMEM((NS * BI, BJ), f32),
             pltpu.VMEM((NS * BI, BJ), f32),
-            pltpu.VMEM((NS * BI, BJ), f32),
+            pltpu.VMEM((NS * BI + 8, BJ), f32),
             pltpu.VMEM((NS * BI, BJ), f32),
             pltpu.VMEM((2, 2, 8, HALF), f32),
             pltpu.VMEM((2, PL, 8, HALF), f32),
@@ -722,12 +756,13 @@
             pltpu.VMEM((4, 8, BJ), f32),
             pltpu.VMEM((2 * ZN, 8, BJ), f32),
             pltpu.VMEM((2 * ZN * 8, PL * 8), bf16),
-            pltpu.VMEM((PL * 8, 2 * ZN * 8), bf16),
             pltpu.VMEM((2, NV, 8, BJ), f32),
-            pltpu.VMEM((2, 8, HALF), f32),
-            pltpu.VMEM((2 * ZN, 8, HALF), f32),
-            pltpu.VMEM((PL, 8, HALF), f32),
-            pltpu.VMEM((PL, 8, HALF), f32),
+            pltpu.VMEM((NV, 8, BJ), f32),
+            pltpu.VMEM((2, 8, FROW), f32),
+            pltpu.VMEM((PL, 8, FROW), f32),
+            pltpu.VMEM((2 * ZN, 8, FROW), f32),
+            pltpu.VMEM((2 * ZN, 8, FROW), f32),
+            pltpu.VMEM((NF, CW), f32),
             pltpu.VMEM((HID + 16, HID), f32),
             pltpu.VMEM((HID + 16, HID), f32),
             pltpu.VMEM((NF + 16, HID), f32),

time: 70.8 us -> 74.2 us (1.048)
  Pallas kernels: 69.4 us -> 72.7 us
    pallas_call x1, Pallas kernels: 67.3 us -> 70.6 us  [per_device(): pl.pallas_call(functools.partial(kernel, loss_scale), out_shape=(jax.Shap...]
where the time goes in v9:
time: 74.2 us; the launch traced here: 74 us
  Pallas kernels  72.7 us (98%)
  between operations  1.29 us (2%)
    pallas_call x1, Pallas kernels, per_device(): pl.pallas_call(functools.partial(kernel, loss_scale), out_shape=(jax.Shap...  70.6 us
    pallas_call x1, Pallas kernels, per_device(): pl.pallas_call(copy_kernel, out_shape=tuple((jax.ShapeDtypeStruct(x.shape...  2.1 us

profile of v9, /device:TPU:1, one launch (start us, length us, event | category | flops | bytes accessed | tf_op | source)
XLA Modules:
  0.0 74.0 jit_solution(1764863048045456771)
XLA Ops:
  1.3 70.6 %shard_map.164 = (f32[6,3,32,128]{3,2,1,0:T(8,128)}, f32[16,256]{1,0:T(8,128)}, f32[256,256]{1,0:T(8,128)}, f32[256,256]{1,0:T(8,128)}, f32[4,256]{1,0:T(4,128)}) custom-call(f32[6,3,32,128]{3,2,1,0:T(8,128)} %bitcast.8, f32[6,3,32,128]{3,2,1,0:T(8,128)} %bitcast.9, bf16[16,3,32,128]{3,2,1,0:T(8,128)(2,1)} %bitcast.7, f32[6,6]{1,0:T(8,128)} %coup.1, ...), custom_call_target="tpu_custom_call" | custom-call | tf_op jit(solution)/shard_map/pallas_call | solution.py:719
  71.9 2.1 %shard_map.165 = (f32[6,3,32,128]{3,2,1,0:T(8,128)}, f32[16,256]{1,0:T(8,128)}, f32[256,256]{1,0:T(8,128)}, f32[256,256]{1,0:T(8,128)}, f32[4,256]{1,0:T(4,128)}) custom-call(f32[6,3,32,128]{3,2,1,0:T(8,128)} %get-tuple-element.15.refs_0_, f32[16,256]{1,0:T(8,128)} %get-tuple-element.16.refs_1_, f32[256,256]{1,0:T(8,128)} %get-tuple-element.17.refs_2_, ...), custom_call_target="tpu_custom_call" | custom-call | tf_op jit(solution)/shard_map/pallas_call | solution.py:791

commit v10 on v7

--- a/solution.py
+++ b/solution.py
@@ -594,11 +594,17 @@
     table()
     top_delta(0, LAST)
     weigh(0, LAST, gtop, second_r, third_r)
-    lax.fori_loop(0, LAST, back_mid, 0)
-    returned()
-    top_delta(1, LAST)
-    weigh(1, LAST, gtop, second_r, third_r)
-    hand(0)
+    def back_mid_first(k, carry):
+        @pl.when(k == 3)
+        def _():
+            returned()
+            top_delta(1, LAST)
+            weigh(1, LAST, gtop, second_r, third_r)
+            hand(0)
+
+        return back_mid(k, carry)
+
+    lax.fori_loop(0, LAST, back_mid_first, 0)
     layer_back(LAST, top_w, third_r, second_r, gmid, first_r)
     weigh(1, LAST, gmid, first_r, second_r)
     hand(1)

time: 70.8 us -> 72.4 us (1.023)
  Pallas kernels: 69.4 us -> 71 us
    pallas_call x1, Pallas kernels: 67.3 us -> 68.9 us  [per_device(): pl.pallas_call(functools.partial(kernel, loss_scale), out_shape=(jax.Shap...]
where the time goes in v10:
time: 72.4 us; the launch traced here: 72.3 us
  Pallas kernels  71 us (98%)
  between operations  1.29 us (2%)
    pallas_call x1, Pallas kernels, per_device(): pl.pallas_call(functools.partial(kernel, loss_scale), out_shape=(jax.Shap...  68.9 us
    pallas_call x1, Pallas kernels, per_device(): pl.pallas_call(copy_kernel, out_shape=tuple((jax.ShapeDtypeStruct(x.shape...  2.1 us

profile of v10, /device:TPU:1, one launch (start us, length us, event | category | flops | bytes accessed | tf_op | source)
XLA Modules:
  0.0 72.3 jit_solution(7567970702380910527)
XLA Ops:
  1.3 68.9 %shard_map.164 = (f32[6,3,32,128]{3,2,1,0:T(8,128)}, f32[16,256]{1,0:T(8,128)}, f32[256,256]{1,0:T(8,128)}, f32[256,256]{1,0:T(8,128)}, f32[4,256]{1,0:T(4,128)}) custom-call(f32[6,3,32,128]{3,2,1,0:T(8,128)} %bitcast.8, f32[6,3,32,128]{3,2,1,0:T(8,128)} %bitcast.9, bf16[16,3,32,128]{3,2,1,0:T(8,128)(2,1)} %bitcast.7, f32[6,6]{1,0:T(8,128)} %coup.1, ...), custom_call_target="tpu_custom_call" | custom-call | tf_op jit(solution)/shard_map/pallas_call | solution.py:691
  70.2 2.1 %shard_map.165 = (f32[6,3,32,128]{3,2,1,0:T(8,128)}, f32[16,256]{1,0:T(8,128)}, f32[256,256]{1,0:T(8,128)}, f32[256,256]{1,0:T(8,128)}, f32[4,256]{1,0:T(4,128)}) custom-call(f32[6,3,32,128]{3,2,1,0:T(8,128)} %get-tuple-element.15.refs_0_, f32[16,256]{1,0:T(8,128)} %get-tuple-element.16.refs_1_, f32[256,256]{1,0:T(8,128)} %get-tuple-element.17.refs_2_, ...), custom_call_target="tpu_custom_call" | custom-call | tf_op jit(solution)/shard_map/pallas_call | solution.py:762
